TPU v7x, 32 devices: a whole 2x2x4 slice. The times are simulated.
32 devices in a mesh: ty: 4 (over y, x), tx: 8 (over z, core).
Axes of the slice: x: 2, y: 2, z: 4, core: 2. Of those that a mesh axis runs over, the one named last changes fastest.
Arguments:
- ensemble: bfloat16 [8, 8, 32, 1024], P('tx', None, 'ty'), may hold values from -6 to 6
- diffusivity: float32 [32, 1024], P('ty', 'tx'), may hold values from 0.1 to 0.245
- vertical: float32 [8, 8], replicated, as said below
- weights: float32 [8], replicated, may hold values from 0.0625 to 0.25
- obs_value: float32 [32, 8, 8], P(('ty', 'tx')), may hold values from -6 to 6
- obs_cell: int32 [32, 8, 8], P(('ty', 'tx')), may hold values from 0 to 8191
- obs_count: int32 [32, 8], P(('ty', 'tx')), may hold values from 0 to 8, as said below
Outputs:
- increment: float32 [8, 32, 1024], P(None, 'ty', 'tx')
- projected: float32 [32, 8, 8], P(('ty', 'tx'))
Inputs may be any that keep to these rules, and one draw needn't show every extreme that they name: `obs_count`: in every tile row one destination column, drawn from the seed, receives 8 live slots from every source of that row; other loads are uneven across destination columns. `vertical`: Banded: entries more than two levels off the diagonal are zero.
All inputs are finite; a program needn't handle non-finite values.
Results may differ from a plain program's by a relative error of at most 0.0003.
Values may be sent and summed in bfloat16 or wider, within the bound.
No kernel may reach another device: no remote copies, remote signals or barrier semaphores. Data moves between devices by JAX's collectives and lax.ppermute only.
A program may use at most 64 MiB of HBM per device.

v0:
```python
import jax
import jax.numpy as jnp
from jax import lax
from jax.sharding import PartitionSpec as P

STEPS = 4


def padded_2(block, sides, width):
    for axis, dim in sides:
        count = lax.axis_size(axis)
        forward = [(i, i + 1) for i in range(count - 1)]
        backward = [(target, source) for source, target in forward]
        low = lax.ppermute(
            lax.slice_in_dim(block, block.shape[dim] - width, None, axis=dim), axis, forward
        )
        high = lax.ppermute(lax.slice_in_dim(block, 0, width, axis=dim), axis, backward)
        block = jnp.concatenate([low, block, high], axis=dim)
    return block


def tile_step(current, diffusivity):
    padded = padded_2(current, (("ty", 2), ("tx", 3)), 1)
    beside = (
        padded[:, :, :-2, 1:-1]
        + padded[:, :, 2:, 1:-1]
        + padded[:, :, 1:-1, :-2]
        + padded[:, :, 1:-1, 2:]
    )
    return current + diffusivity * (beside - 4.0 * current)


def shards(ensemble, diffusivity, vertical, weights, obs_value, obs_cell, obs_count):
    levels_num = ensemble.shape[1]
    tile_rows = diffusivity.shape[0]
    tile_cols = diffusivity.shape[1]
    slot_num = obs_value.shape[2]
    got_values, got_cells, got_counts = (
        lax.all_to_all(obs_value, "tx", split_axis=1, concat_axis=0, tiled=True),
        lax.all_to_all(obs_cell, "tx", split_axis=1, concat_axis=0, tiled=True),
        lax.all_to_all(obs_count, "tx", split_axis=1, concat_axis=0, tiled=True),
    )
    got_values = got_values[:, 0]
    got_cells = got_cells[:, 0]
    got_counts = got_counts[:, 0]
    live_slots = jnp.arange(slot_num, dtype=jnp.int32)[None, :] < got_counts[:, None]
    flat_cells = got_cells.ravel()
    forcing = jnp.zeros((levels_num * tile_rows * tile_cols,), jnp.float32)
    forcing = forcing.at[flat_cells].add(
        jnp.where(live_slots, got_values, jnp.float32(0.0)).ravel()
    )
    forcing = forcing.reshape(levels_num, tile_rows, tile_cols)
    tiles = lax.all_to_all(ensemble, "tx", split_axis=3, concat_axis=0, tiled=True)
    current = tiles.astype(jnp.float32) * forcing
    for repeat in range(STEPS):
        current = tile_step(current, diffusivity)
    current = jnp.einsum("lm,kmrc->klrc", vertical, current, precision=lax.Precision.HIGHEST)
    increment = jnp.einsum(
        "k,klrc->lrc", weights, tiles.astype(jnp.float32) * current, precision=lax.Precision.HIGHEST
    )
    read_back = jnp.where(
        live_slots, increment.ravel()[flat_cells].reshape(live_slots.shape), jnp.float32(0.0)
    )
    returned = lax.all_to_all(read_back[:, None, :], "tx", split_axis=0, concat_axis=1, tiled=True)
    return (increment, returned)


def solution(mesh):
    placed = (
        P("tx", None, "ty", None),
        P("ty", "tx"),
        P(),
        P(),
        P(("ty", "tx"), None, None),
        P(("ty", "tx"), None, None),
        P(("ty", "tx"), None),
    )
    return jax.shard_map(
        shards,
        mesh=mesh,
        in_specs=placed,
        out_specs=(P(None, "ty", "tx"), P(("ty", "tx"), None, None)),
        check_vma=False,
    )
```

profile of v0, /device:TPU:4, one launch (start us, length us, event | category | flops | bytes accessed | tf_op | source)
XLA Modules:
  0.0 134.8 jit_solution(15935865131569958043)
XLA Ops:
  1.4 10.2 %all_to_all.52 = s32[1,8,1]{2,0,1:T(1,128)S(1)} all-to-all(s32[1,8,1]{2,0,1:T(1,128)S(1)} %copy.26), channel_id=1, replica_groups=mesh['ty'=4,'tx'=8] {'tx'}, dimensions={1} | all-to-all | bytes 64 | tf_op jit(solution)/shard_map/all_to_all | solution.py:41
  11.6 3.3 %all-to-all-start.1 = ((s32[1,8,8]{2,0,1:T(1,128)}), s32[1,8,8]{2,0,1:T(1,128)S(1)}, u32[]{:S(2)}, u32[]{:S(2)}) async-start(s32[1,8,8]{2,0,1:T(1,128)} %bitcast.53), calls=%async_computation.1 | async-start | bytes 8192 | tf_op jit(solution)/shard_map/all_to_all | solution.py:40
  14.9 2.3 %copy.22 = bf16[1,8,8,1024]{2,1,0,3:T(8,128)(2,1)S(1)} copy(bf16[1,8,8,1024]{3,2,1,0:T(8,128)(2,1)} %param.7) | data formatting | bytes 262144 | tf_op args[0]
  17.2 2.9 %reshape.158 = bf16[8,2,4096]{2,1,0:T(2,128)(2,1)} reshape(bf16[1024,1,8,8]{3,2,1,0:T(8,128)(2,1)S(1)} %bitcast.47) | data formatting | bytes 262144
  20.4 5.0 %all-to-all-start.3 = ((f32[1,8,8]{2,0,1:T(1,128)}), f32[1,8,8]{2,0,1:T(1,128)S(1)}, u32[]{:S(2)}, u32[]{:S(2)}) async-start(f32[1,8,8]{2,0,1:T(1,128)} %bitcast.6), calls=%async_computation.3 | async-start | bytes 8192 | tf_op jit(solution)/shard_map/all_to_all | solution.py:39
  26.8 4.1 %all-to-all-done.3 = f32[1,8,8]{2,0,1:T(1,128)S(1)} async-done(((f32[1,8,8]{2,0,1:T(1,128)}), f32[1,8,8]{2,0,1:T(1,128)S(1)}, u32[]{:S(2)}, u32[]{:S(2)}) %all-to-all-start.3) | async-done | bytes 288 | tf_op jit(solution)/shard_map/all_to_all | solution.py:39
  30.9 3.4 %all-to-all-start = ((bf16[8,2,4096]{2,1,0:T(2,128)(2,1)}), bf16[8,2,4096]{2,1,0:T(2,128)(2,1)S(1)}, u32[]{:S(2)}, u32[]{:S(2)}) async-start(bf16[8,2,4096]{2,1,0:T(2,128)(2,1)} %reshape.158), calls=%async_computation | async-start | bytes 262144 | tf_op jit(solution)/shard_map/all_to_all | solution.py:53
  36.5 4.5 %all-to-all-done = bf16[8,2,4096]{2,1,0:T(2,128)(2,1)S(1)} async-done(((bf16[8,2,4096]{2,1,0:T(2,128)(2,1)}), bf16[8,2,4096]{2,1,0:T(2,128)(2,1)S(1)}, u32[]{:S(2)}, u32[]{:S(2)}) %all-to-all-start) | async-done | bytes 131104 | tf_op jit(solution)/shard_map/all_to_all | solution.py:53
  41.0 2.4 %reshape.159 = bf16[1024,1,8,8]{3,2,1,0:T(8,128)(2,1)S(1)} reshape(bf16[8,2,4096]{2,1,0:T(2,128)(2,1)S(1)} %all-to-all-done) | data formatting | bytes 262144
  43.4 1.4 %copy.23 = bf16[1,8,8,1024]{3,2,1,0:T(8,128)(2,1)S(1)} copy(bf16[1,8,8,1024]{2,1,0,3:T(8,128)(2,1)S(1)} %bitcast.46) | data formatting | bytes 262144 | tf_op jit(solution)/shard_map/all_to_all | solution.py:53
  45.1 3.3 %collective-permute-start.1 = (f32[8,8,1,128]{3,1,2,0:T(8,128)S(1)}, f32[8,8,1,128]{3,1,2,0:T(8,128)S(1)}, u32[]{:S(2)}, u32[]{:S(2)}) collective-permute-start(f32[8,8,1,128]{3,1,2,0:T(8,128)S(1)} %get-tuple-element.17), channel_id=1, source_target_pairs={{8,0},{16,8},{24,16},{9,1},{17,9},{25,17},{10,2},{18,10},{26,18},{... | collective-permute-start | bytes 98312 | tf_op jit(solution)/shard_map/ppermute | solution.py:17
  48.5 2.5 %collective-permute-start = (f32[8,8,1,128]{3,1,2,0:T(8,128)S(1)}, f32[8,8,1,128]{3,1,2,0:T(8,128)S(1)}, u32[]{:S(2)}, u32[]{:S(2)}) collective-permute-start(f32[8,8,1,128]{3,1,2,0:T(8,128)S(1)} %get-tuple-element.16), channel_id=1, source_target_pairs={{0,8},{8,16},{16,24},{1,9},{9,17},{17,25},{2,10},{10,18},{18,26},{... | collective-permute-start | bytes 98312 | tf_op jit(solution)/shard_map/ppermute | solution.py:14
  51.0 4.2 %collective-permute-done = f32[8,8,1,128]{3,1,2,0:T(8,128)S(1)} collective-permute-done((f32[8,8,1,128]{3,1,2,0:T(8,128)S(1)}, f32[8,8,1,128]{3,1,2,0:T(8,128)S(1)}, u32[]{:S(2)}, u32[]{:S(2)}) %collective-permute-start) | collective-permute-done | bytes 32800 | tf_op jit(solution)/shard_map/ppermute | solution.py:14
  55.4 1.3 collective-permute-start.3
  56.7 3.1 %collective-permute-start.2 = (f32[8,8,10,1]{3,1,2,0:T(8,128)S(1)}, f32[8,8,10,1]{3,1,2,0:T(8,128)S(1)}, u32[]{:S(2)}, u32[]{:S(2)}) collective-permute-start(f32[8,8,10,1]{3,1,2,0:T(8,128)S(1)} %get-tuple-element.8), channel_id=1, source_target_pairs={{0,1},{1,2},{2,3},{3,4},{4,5},{5,6},{6,7},{8,9},{9,10},{10,11},{11... | collective-permute-start | bytes 7688 | tf_op jit(solution)/shard_map/ppermute | solution.py:14
  59.7 1.2 collective-permute-done.2
  61.2 1.9 %collective-permute-start.5 = (f32[8,8,1,128]{3,1,2,0:T(8,128)S(1)}, f32[8,8,1,128]{3,1,2,0:T(8,128)S(1)}, u32[]{:S(2)}, u32[]{:S(2)}) collective-permute-start(f32[8,8,1,128]{3,1,2,0:T(8,128)S(1)} %get-tuple-element.15), channel_id=1, source_target_pairs={{8,0},{16,8},{24,16},{9,1},{17,9},{25,17},{10,2},{18,10},{26,18},{... | collective-permute-start | bytes 98312 | tf_op jit(solution)/shard_map/ppermute | solution.py:17
  63.2 3.9 %collective-permute-start.4 = (f32[8,8,1,128]{3,1,2,0:T(8,128)S(1)}, f32[8,8,1,128]{3,1,2,0:T(8,128)S(1)}, u32[]{:S(2)}, u32[]{:S(2)}) collective-permute-start(f32[8,8,1,128]{3,1,2,0:T(8,128)S(1)} %get-tuple-element.14), channel_id=1, source_target_pairs={{0,8},{8,16},{16,24},{1,9},{9,17},{17,25},{2,10},{10,18},{18,26},{... | collective-permute-start | bytes 98312 | tf_op jit(solution)/shard_map/ppermute | solution.py:14
  67.1 2.8 %collective-permute-done.4 = f32[8,8,1,128]{3,1,2,0:T(8,128)S(1)} collective-permute-done((f32[8,8,1,128]{3,1,2,0:T(8,128)S(1)}, f32[8,8,1,128]{3,1,2,0:T(8,128)S(1)}, u32[]{:S(2)}, u32[]{:S(2)}) %collective-permute-start.4) | collective-permute-done | bytes 32800 | tf_op jit(solution)/shard_map/ppermute | solution.py:14
  70.0 1.3 collective-permute-start.7
  71.3 4.7 %collective-permute-start.6 = (f32[8,8,10,1]{3,1,2,0:T(8,128)S(1)}, f32[8,8,10,1]{3,1,2,0:T(8,128)S(1)}, u32[]{:S(2)}, u32[]{:S(2)}) collective-permute-start(f32[8,8,10,1]{3,1,2,0:T(8,128)S(1)} %get-tuple-element.6), channel_id=1, source_target_pairs={{0,1},{1,2},{2,3},{3,4},{4,5},{5,6},{6,7},{8,9},{9,10},{10,11},{11... | collective-permute-start | bytes 7688 | tf_op jit(solution)/shard_map/ppermute | solution.py:14
  77.6 1.9 %collective-permute-start.9 = (f32[8,8,1,128]{3,1,2,0:T(8,128)S(1)}, f32[8,8,1,128]{3,1,2,0:T(8,128)S(1)}, u32[]{:S(2)}, u32[]{:S(2)}) collective-permute-start(f32[8,8,1,128]{3,1,2,0:T(8,128)S(1)} %get-tuple-element.13), channel_id=1, source_target_pairs={{8,0},{16,8},{24,16},{9,1},{17,9},{25,17},{10,2},{18,10},{26,18},{... | collective-permute-start | bytes 98312 | tf_op jit(solution)/shard_map/ppermute | solution.py:17
  79.5 3.9 %collective-permute-start.8 = (f32[8,8,1,128]{3,1,2,0:T(8,128)S(1)}, f32[8,8,1,128]{3,1,2,0:T(8,128)S(1)}, u32[]{:S(2)}, u32[]{:S(2)}) collective-permute-start(f32[8,8,1,128]{3,1,2,0:T(8,128)S(1)} %get-tuple-element.12), channel_id=1, source_target_pairs={{0,8},{8,16},{16,24},{1,9},{9,17},{17,25},{2,10},{10,18},{18,26},{... | collective-permute-start | bytes 98312 | tf_op jit(solution)/shard_map/ppermute | solution.py:14
  83.4 2.8 %collective-permute-done.8 = f32[8,8,1,128]{3,1,2,0:T(8,128)S(1)} collective-permute-done((f32[8,8,1,128]{3,1,2,0:T(8,128)S(1)}, f32[8,8,1,128]{3,1,2,0:T(8,128)S(1)}, u32[]{:S(2)}, u32[]{:S(2)}) %collective-permute-start.8) | collective-permute-done | bytes 32800 | tf_op jit(solution)/shard_map/ppermute | solution.py:14
  86.4 1.3 collective-permute-start.11
  87.7 7.8 %collective-permute-start.10 = (f32[8,8,10,1]{3,1,2,0:T(8,128)S(1)}, f32[8,8,10,1]{3,1,2,0:T(8,128)S(1)}, u32[]{:S(2)}, u32[]{:S(2)}) collective-permute-start(f32[8,8,10,1]{3,1,2,0:T(8,128)S(1)} %get-tuple-element.4), channel_id=1, source_target_pairs={{0,1},{1,2},{2,3},{3,4},{4,5},{5,6},{6,7},{8,9},{9,10},{10,11},{11... | collective-permute-start | bytes 7688 | tf_op jit(solution)/shard_map/ppermute | solution.py:14
  97.0 1.9 %collective-permute-start.13 = (f32[8,8,1,128]{3,1,2,0:T(8,128)S(1)}, f32[8,8,1,128]{3,1,2,0:T(8,128)S(1)}, u32[]{:S(2)}, u32[]{:S(2)}) collective-permute-start(f32[8,8,1,128]{3,1,2,0:T(8,128)S(1)} %get-tuple-element.11), channel_id=1, source_target_pairs={{8,0},{16,8},{24,16},{9,1},{17,9},{25,17},{10,2},{18,10},{26,18},{... | collective-permute-start | bytes 98312 | tf_op jit(solution)/shard_map/ppermute | solution.py:17
  98.9 3.9 %collective-permute-start.12 = (f32[8,8,1,128]{3,1,2,0:T(8,128)S(1)}, f32[8,8,1,128]{3,1,2,0:T(8,128)S(1)}, u32[]{:S(2)}, u32[]{:S(2)}) collective-permute-start(f32[8,8,1,128]{3,1,2,0:T(8,128)S(1)} %get-tuple-element.10), channel_id=1, source_target_pairs={{0,8},{8,16},{16,24},{1,9},{9,17},{17,25},{2,10},{10,18},{18,26},{... | collective-permute-start | bytes 98312 | tf_op jit(solution)/shard_map/ppermute | solution.py:14
  102.9 2.8 %collective-permute-done.12 = f32[8,8,1,128]{3,1,2,0:T(8,128)S(1)} collective-permute-done((f32[8,8,1,128]{3,1,2,0:T(8,128)S(1)}, f32[8,8,1,128]{3,1,2,0:T(8,128)S(1)}, u32[]{:S(2)}, u32[]{:S(2)}) %collective-permute-start.12) | collective-permute-done | bytes 32800 | tf_op jit(solution)/shard_map/ppermute | solution.py:14
  105.8 1.3 collective-permute-start.15
  107.1 7.8 %collective-permute-start.14 = (f32[8,8,10,1]{3,1,2,0:T(8,128)S(1)}, f32[8,8,10,1]{3,1,2,0:T(8,128)S(1)}, u32[]{:S(2)}, u32[]{:S(2)}) collective-permute-start(f32[8,8,10,1]{3,1,2,0:T(8,128)S(1)} %get-tuple-element.2), channel_id=1, source_target_pairs={{0,1},{1,2},{2,3},{3,4},{4,5},{5,6},{6,7},{8,9},{9,10},{10,11},{11... | collective-permute-start | bytes 7688 | tf_op jit(solution)/shard_map/ppermute | solution.py:14
  118.3 15.8 %all_to_all.53 = f32[8,1,8]{2,1,0:T(1,128)S(1)} all-to-all(f32[8,1,8]{2,1,0:T(1,128)S(1)} %bitcast.51), channel_id=1, replica_groups=mesh['ty'=4,'tx'=8] {'tx'}, dimensions={0} | all-to-all | bytes 512 | tf_op jit(solution)/shard_map/all_to_all | solution.py:64
  (59 shorter events, 12.8 us)
Async XLA Ops:
  0.6 115.5 %copy-start = (f32[8,8]{1,0:T(8,128)S(1)}, f32[8,8]{1,0:T(8,128)}, u32[]{:S(2)}) copy-start(f32[8,8]{1,0:T(8,128)} %param.9) | copy-start | bytes 772
  11.6 8.8 %all-to-all-start.1 = ((s32[1,8,8]{2,0,1:T(1,128)}), s32[1,8,8]{2,0,1:T(1,128)S(1)}, u32[]{:S(2)}, u32[]{:S(2)}) async-start(s32[1,8,8]{2,0,1:T(1,128)} %bitcast.53), calls=%async_computation.1 | async-start | bytes 8192 | tf_op jit(solution)/shard_map/all_to_all | solution.py:40
  20.4 10.5 %all-to-all-start.3 = ((f32[1,8,8]{2,0,1:T(1,128)}), f32[1,8,8]{2,0,1:T(1,128)S(1)}, u32[]{:S(2)}, u32[]{:S(2)}) async-start(f32[1,8,8]{2,0,1:T(1,128)} %bitcast.6), calls=%async_computation.3 | async-start | bytes 8192 | tf_op jit(solution)/shard_map/all_to_all | solution.py:39
  30.9 10.1 %all-to-all-start = ((bf16[8,2,4096]{2,1,0:T(2,128)(2,1)}), bf16[8,2,4096]{2,1,0:T(2,128)(2,1)S(1)}, u32[]{:S(2)}, u32[]{:S(2)}) async-start(bf16[8,2,4096]{2,1,0:T(2,128)(2,1)} %reshape.158), calls=%async_computation | async-start | bytes 262144 | tf_op jit(solution)/shard_map/all_to_all | solution.py:53
  44.8 16.1 %copy-start.2 = (f32[8,128]{1,0:T(8,128)S(1)}, f32[8,128]{1,0:T(8,128)}, u32[]{:S(2)}) copy-start(f32[8,128]{1,0:T(8,128)} %param.8) | copy-start | bytes 12292
  45.1 5.9 %collective-permute-start.1 = (f32[8,8,1,128]{3,1,2,0:T(8,128)S(1)}, f32[8,8,1,128]{3,1,2,0:T(8,128)S(1)}, u32[]{:S(2)}, u32[]{:S(2)}) collective-permute-start(f32[8,8,1,128]{3,1,2,0:T(8,128)S(1)} %get-tuple-element.17), channel_id=1, source_target_pairs={{8,0},{16,8},{24,16},{9,1},{17,9},{25,17},{10,2},{18,10},{26,18},{... | collective-permute-start | bytes 98312 | tf_op jit(solution)/shard_map/ppermute | solution.py:17
  48.5 6.7 %collective-permute-start = (f32[8,8,1,128]{3,1,2,0:T(8,128)S(1)}, f32[8,8,1,128]{3,1,2,0:T(8,128)S(1)}, u32[]{:S(2)}, u32[]{:S(2)}) collective-permute-start(f32[8,8,1,128]{3,1,2,0:T(8,128)S(1)} %get-tuple-element.16), channel_id=1, source_target_pairs={{0,8},{8,16},{16,24},{1,9},{9,17},{17,25},{2,10},{10,18},{18,26},{... | collective-permute-start | bytes 98312 | tf_op jit(solution)/shard_map/ppermute | solution.py:14
  55.4 4.4 %collective-permute-start.3 = (f32[8,8,10,1]{3,1,2,0:T(8,128)S(1)}, f32[8,8,10,1]{3,1,2,0:T(8,128)S(1)}, u32[]{:S(2)}, u32[]{:S(2)}) collective-permute-start(f32[8,8,10,1]{3,1,2,0:T(8,128)S(1)} %get-tuple-element.9), channel_id=1, source_target_pairs={{1,0},{2,1},{3,2},{4,3},{5,4},{6,5},{7,6},{9,8},{10,9},{11,10},{12... | collective-permute-start | bytes 7688 | tf_op jit(solution)/shard_map/ppermute | solution.py:17
  56.7 4.3 %collective-permute-start.2 = (f32[8,8,10,1]{3,1,2,0:T(8,128)S(1)}, f32[8,8,10,1]{3,1,2,0:T(8,128)S(1)}, u32[]{:S(2)}, u32[]{:S(2)}) collective-permute-start(f32[8,8,10,1]{3,1,2,0:T(8,128)S(1)} %get-tuple-element.8), channel_id=1, source_target_pairs={{0,1},{1,2},{2,3},{3,4},{4,5},{5,6},{6,7},{8,9},{9,10},{10,11},{11... | collective-permute-start | bytes 7688 | tf_op jit(solution)/shard_map/ppermute | solution.py:14
  61.2 5.9 %collective-permute-start.5 = (f32[8,8,1,128]{3,1,2,0:T(8,128)S(1)}, f32[8,8,1,128]{3,1,2,0:T(8,128)S(1)}, u32[]{:S(2)}, u32[]{:S(2)}) collective-permute-start(f32[8,8,1,128]{3,1,2,0:T(8,128)S(1)} %get-tuple-element.15), channel_id=1, source_target_pairs={{8,0},{16,8},{24,16},{9,1},{17,9},{25,17},{10,2},{18,10},{26,18},{... | collective-permute-start | bytes 98312 | tf_op jit(solution)/shard_map/ppermute | solution.py:17
  63.2 6.7 %collective-permute-start.4 = (f32[8,8,1,128]{3,1,2,0:T(8,128)S(1)}, f32[8,8,1,128]{3,1,2,0:T(8,128)S(1)}, u32[]{:S(2)}, u32[]{:S(2)}) collective-permute-start(f32[8,8,1,128]{3,1,2,0:T(8,128)S(1)} %get-tuple-element.14), channel_id=1, source_target_pairs={{0,8},{8,16},{16,24},{1,9},{9,17},{17,25},{2,10},{10,18},{18,26},{... | collective-permute-start | bytes 98312 | tf_op jit(solution)/shard_map/ppermute | solution.py:14
  70.0 6.0 %collective-permute-start.7 = (f32[8,8,10,1]{3,1,2,0:T(8,128)S(1)}, f32[8,8,10,1]{3,1,2,0:T(8,128)S(1)}, u32[]{:S(2)}, u32[]{:S(2)}) collective-permute-start(f32[8,8,10,1]{3,1,2,0:T(8,128)S(1)} %get-tuple-element.7), channel_id=1, source_target_pairs={{1,0},{2,1},{3,2},{4,3},{5,4},{6,5},{7,6},{9,8},{10,9},{11,10},{12... | collective-permute-start | bytes 7688 | tf_op jit(solution)/shard_map/ppermute | solution.py:17
  71.3 5.9 %collective-permute-start.6 = (f32[8,8,10,1]{3,1,2,0:T(8,128)S(1)}, f32[8,8,10,1]{3,1,2,0:T(8,128)S(1)}, u32[]{:S(2)}, u32[]{:S(2)}) collective-permute-start(f32[8,8,10,1]{3,1,2,0:T(8,128)S(1)} %get-tuple-element.6), channel_id=1, source_target_pairs={{0,1},{1,2},{2,3},{3,4},{4,5},{5,6},{6,7},{8,9},{9,10},{10,11},{11... | collective-permute-start | bytes 7688 | tf_op jit(solution)/shard_map/ppermute | solution.py:14
  77.6 5.9 %collective-permute-start.9 = (f32[8,8,1,128]{3,1,2,0:T(8,128)S(1)}, f32[8,8,1,128]{3,1,2,0:T(8,128)S(1)}, u32[]{:S(2)}, u32[]{:S(2)}) collective-permute-start(f32[8,8,1,128]{3,1,2,0:T(8,128)S(1)} %get-tuple-element.13), channel_id=1, source_target_pairs={{8,0},{16,8},{24,16},{9,1},{17,9},{25,17},{10,2},{18,10},{26,18},{... | collective-permute-start | bytes 98312 | tf_op jit(solution)/shard_map/ppermute | solution.py:17
  79.5 6.7 %collective-permute-start.8 = (f32[8,8,1,128]{3,1,2,0:T(8,128)S(1)}, f32[8,8,1,128]{3,1,2,0:T(8,128)S(1)}, u32[]{:S(2)}, u32[]{:S(2)}) collective-permute-start(f32[8,8,1,128]{3,1,2,0:T(8,128)S(1)} %get-tuple-element.12), channel_id=1, source_target_pairs={{0,8},{8,16},{16,24},{1,9},{9,17},{17,25},{2,10},{10,18},{18,26},{... | collective-permute-start | bytes 98312 | tf_op jit(solution)/shard_map/ppermute | solution.py:14
  86.4 9.1 %collective-permute-start.11 = (f32[8,8,10,1]{3,1,2,0:T(8,128)S(1)}, f32[8,8,10,1]{3,1,2,0:T(8,128)S(1)}, u32[]{:S(2)}, u32[]{:S(2)}) collective-permute-start(f32[8,8,10,1]{3,1,2,0:T(8,128)S(1)} %get-tuple-element.5), channel_id=1, source_target_pairs={{1,0},{2,1},{3,2},{4,3},{5,4},{6,5},{7,6},{9,8},{10,9},{11,10},{12... | collective-permute-start | bytes 7688 | tf_op jit(solution)/shard_map/ppermute | solution.py:17
  87.7 9.0 %collective-permute-start.10 = (f32[8,8,10,1]{3,1,2,0:T(8,128)S(1)}, f32[8,8,10,1]{3,1,2,0:T(8,128)S(1)}, u32[]{:S(2)}, u32[]{:S(2)}) collective-permute-start(f32[8,8,10,1]{3,1,2,0:T(8,128)S(1)} %get-tuple-element.4), channel_id=1, source_target_pairs={{0,1},{1,2},{2,3},{3,4},{4,5},{5,6},{6,7},{8,9},{9,10},{10,11},{11... | collective-permute-start | bytes 7688 | tf_op jit(solution)/shard_map/ppermute | solution.py:14
  97.0 19.9 %copy-start.3 = (f32[8]{0:T(128)S(1)}, f32[8]{0:T(128)}, u32[]{:S(2)}) copy-start(f32[8]{0:T(128)} %param.10) | copy-start | bytes 100
  97.0 5.9 %collective-permute-start.13 = (f32[8,8,1,128]{3,1,2,0:T(8,128)S(1)}, f32[8,8,1,128]{3,1,2,0:T(8,128)S(1)}, u32[]{:S(2)}, u32[]{:S(2)}) collective-permute-start(f32[8,8,1,128]{3,1,2,0:T(8,128)S(1)} %get-tuple-element.11), channel_id=1, source_target_pairs={{8,0},{16,8},{24,16},{9,1},{17,9},{25,17},{10,2},{18,10},{26,18},{... | collective-permute-start | bytes 98312 | tf_op jit(solution)/shard_map/ppermute | solution.py:17
  98.9 6.7 %collective-permute-start.12 = (f32[8,8,1,128]{3,1,2,0:T(8,128)S(1)}, f32[8,8,1,128]{3,1,2,0:T(8,128)S(1)}, u32[]{:S(2)}, u32[]{:S(2)}) collective-permute-start(f32[8,8,1,128]{3,1,2,0:T(8,128)S(1)} %get-tuple-element.10), channel_id=1, source_target_pairs={{0,8},{8,16},{16,24},{1,9},{9,17},{17,25},{2,10},{10,18},{18,26},{... | collective-permute-start | bytes 98312 | tf_op jit(solution)/shard_map/ppermute | solution.py:14
  105.8 9.1 %collective-permute-start.15 = (f32[8,8,10,1]{3,1,2,0:T(8,128)S(1)}, f32[8,8,10,1]{3,1,2,0:T(8,128)S(1)}, u32[]{:S(2)}, u32[]{:S(2)}) collective-permute-start(f32[8,8,10,1]{3,1,2,0:T(8,128)S(1)} %get-tuple-element.3), channel_id=1, source_target_pairs={{1,0},{2,1},{3,2},{4,3},{5,4},{6,5},{7,6},{9,8},{10,9},{11,10},{12... | collective-permute-start | bytes 7688 | tf_op jit(solution)/shard_map/ppermute | solution.py:17
  107.1 9.0 %collective-permute-start.14 = (f32[8,8,10,1]{3,1,2,0:T(8,128)S(1)}, f32[8,8,10,1]{3,1,2,0:T(8,128)S(1)}, u32[]{:S(2)}, u32[]{:S(2)}) collective-permute-start(f32[8,8,10,1]{3,1,2,0:T(8,128)S(1)} %get-tuple-element.2), channel_id=1, source_target_pairs={{0,1},{1,2},{2,3},{3,4},{4,5},{5,6},{6,7},{8,9},{9,10},{10,11},{11... | collective-permute-start | bytes 7688 | tf_op jit(solution)/shard_map/ppermute | solution.py:14
  117.4 17.4 %copy-start.1 = (f32[1,8,8,128]{3,0,2,1:T(1,128)}, f32[1,8,8,128]{3,0,2,1:T(1,128)S(1)}, u32[]{:S(2)}) copy-start(f32[1,8,8,128]{3,0,2,1:T(1,128)S(1)} %fusion.32) | copy-start | bytes 98308
where the time goes:
time: 136 us; the launch traced here: 135 us
  starting transfers between devices  63.6 us (47%)
  blocking collectives  26.1 us (19%)
  waiting for transfers between devices  25.9 us (19%)
  local copies, waits for them, and re-layouts  13.3 us (10%)
  other arithmetic  3.74 us (3%)
    ppermute x8, starting transfers between devices, padded_2(): lax.ppermute(lax.slice_in_dim(block, block.shape[dim] - width, None, axis...  37.6 us
    ppermute x8, waiting for transfers between devices, padded_2(): lax.ppermute(lax.slice_in_dim(block, block.shape[dim] - width, None, axis...  17.3 us
    all_to_all x1, blocking collectives, shards(): lax.all_to_all(read_back[:, None, :], 'tx', split_axis=0, concat_axis=1,...  15.8 us
    ppermute x8, starting transfers between devices, padded_2(): lax.ppermute(lax.slice_in_dim(block, 0, width, axis=dim), axis, backward)  14.3 us
    all_to_all x1, blocking collectives, shards(): lax.all_to_all(obs_count, 'tx', split_axis=1, concat_axis=0, tiled=True)  10.2 us
    unnamed x13, local copies, waits for them, and re-layouts  8.31 us
    all_to_all x1, starting transfers between devices, shards(): lax.all_to_all(obs_value, 'tx', split_axis=1, concat_axis=0, tiled=True)  5.03 us
    all_to_all x1, waiting for transfers between devices, shards(): lax.all_to_all(ensemble, 'tx', split_axis=3, concat_axis=0, tiled=True)  4.47 us
  transfers between devices with their start and end apart: 19, of which 10 were waited for; matrix products, arithmetic and copies ran while one was open for 7% of the time, Pallas kernels for 0%

commit v1 on v0

v1 whole, which is shorter than its diff:
```python
import functools

import jax
import jax.numpy as jnp
from jax import lax
from jax.experimental import pallas as pl
from jax.experimental.pallas import tpu as pltpu
from jax.sharding import PartitionSpec as P

STEPS = 4
BAND = 2
LANES = 128
GROUP = 8
F32, BF16 = jnp.float32, jnp.bfloat16
VMEM = pl.BlockSpec(memory_space=pltpu.VMEM)
SMEM = pl.BlockSpec(memory_space=pltpu.SMEM)


def round_up(n, m):
    return -(-n // m) * m


def log2(n):
    assert n & (n - 1) == 0
    return n.bit_length() - 1


def iota(shape, axis):
    return lax.broadcasted_iota(jnp.int32, shape, axis)


def pieces(x):
    high = x.astype(BF16).astype(F32)
    rest = x - high
    middle = rest.astype(BF16).astype(F32)
    return high, middle, rest - middle


def stagger(x):
    return pltpu.roll(x, 0, 1, stride=GROUP, stride_axis=0)


def pick(x, place):
    if isinstance(place, int):
        shift = (-GROUP * place) % LANES
    else:
        shift = lax.rem(LANES - GROUP * place, LANES)
    rolled = pltpu.roll(x, shift, 1)
    own = iota(x.shape, 1) // GROUP == iota(x.shape, 0)
    return jnp.sum(jnp.where(own, rolled, 0.0), axis=0, keepdims=True)


def live_mask(count_ref, slots):
    tiles = count_ref.shape[1]
    count = jnp.broadcast_to(count_ref[...].astype(F32), (tiles, tiles))
    diagonal = iota((tiles, tiles), 0) == iota((tiles, tiles), 1)
    column = jnp.sum(jnp.where(diagonal, count, 0.0), axis=1, keepdims=True)
    return iota((tiles, slots), 1).astype(F32) < column


def pack_kernel(levels, value_ref, cell_ref, count_ref, diff_ref, out_ref, wide):
    _, tiles, slots = value_ref.shape
    rows = diff_ref.shape[0]
    block = min(tiles, LANES // GROUP)
    blocks = tiles // block
    cell = cell_ref[0]
    flat = lax.shift_right_logical(cell, log2(LANES))
    level = lax.shift_right_logical(flat, log2(rows))
    row = flat & (rows - 1)
    found = (
        jnp.where(live_mask(count_ref, slots), value_ref[0], 0.0),
        (row * levels + level).astype(F32),
        (cell & (LANES - 1)).astype(F32),
    )
    out_ref[...] = jnp.zeros_like(out_ref)
    out_ref[0:rows, :] = diff_ref[...]
    wide[...] = jnp.zeros_like(wide)
    for q, x in enumerate(found):
        wide[q, :, 0:slots] = x
        for b in range(blocks):
            line = pick(stagger(wide[q, b * block : (b + 1) * block, :]), 0)
            out_ref[pl.ds(rows + q * blocks + b, 1), :] = line


def turn_kernel(ens_ref, out_ref, wide):
    _, levels, rows, columns = ens_ref.shape
    for t in range(columns // LANES):
        at = slice(t * LANES, (t + 1) * LANES)
        wide[t] = ens_ref[0, :, :, at].astype(F32).reshape(levels * rows, LANES)
        for r in range(0, rows, 2):
            both = [wide[t, pl.ds(r + i, levels, stride=rows), :] for i in range(2)]
            out_ref[r * levels : (r + 2) * levels, at] = jnp.concatenate(both, axis=0).astype(BF16)


def gather_kernel(near, rows, levels, *refs):
    got, (turned_ref, d_ref, obs_ref, a_ref, b_ref, packs, halo_a, halo_b) = refs[:near], refs[near:]
    tiles = packs.shape[0]
    blocks = obs_ref.shape[2] // LANES
    me, even = lax.axis_index("tx"), lax.rem(lax.axis_index("ty"), 2) == 0
    chip, core = me // 2, lax.rem(me, 2)
    for far, ref in enumerate(got):
        for side in range(2):
            packs[2 * (chip ^ far) + (core ^ side)] = ref[side]
    for q in range(3):
        for b in range(blocks):
            obs_ref[q, :, b * LANES : (b + 1) * LANES] = packs[:, rows + q * blocks + b, :]
    half = STEPS * levels
    off_a, off_b = jnp.where(even, half, 0), jnp.where(even, 0, half)
    a_ref[0:half, :] = turned_ref[pl.ds(pl.multiple_of(off_a, half), half), :]
    b_ref[0:half, :] = turned_ref[pl.ds(pl.multiple_of(off_b, half), half), :]
    extra = halo_a.shape[0]
    deep = STEPS - 1
    halo_a[...] = jnp.zeros_like(halo_a)
    halo_b[...] = jnp.zeros_like(halo_b)
    for t in range(tiles):
        at = slice(t * LANES, (t + 1) * LANES)
        d = packs[t, 0:rows, :]
        d_ref[:, at] = d
        for p, piece in enumerate(pieces(d)):
            low = pltpu.roll(piece, deep, 0)
            halo_a[p * deep : (p + 1) * deep, :] = jnp.where(even, low, piece)[0:deep]
            halo_b[p * deep : (p + 1) * deep, :] = jnp.where(even, piece, low)[0:deep]
        first = 3 * deep
        for p, piece in enumerate(pieces(packs[t, rows : rows + blocks, :])):
            halo_a[first + p * blocks : first + (p + 1) * blocks, :] = piece
            halo_b[first + p * blocks : first + (p + 1) * blocks, :] = piece
        first += 3 * blocks
        where_at = packs[t, rows + blocks : rows + 3 * blocks, :]
        halo_a[first : first + 2 * blocks, :] = where_at
        halo_b[first : first + 2 * blocks, :] = where_at
        a_ref[half : half + extra, at] = halo_a[...].astype(BF16)
        b_ref[half : half + extra, at] = halo_b[...].astype(BF16)


def lines_of(x, tile, block):
    size = x[0][0].shape[0]
    return jnp.concatenate([pick(part, tile % size) for part in x[tile // size]], axis=1)


def spread(line_value, line_key, hits, count, first):
    key = line_key - first
    on = iota((count, line_key.shape[1]), 0).astype(F32) == key
    stacked = jnp.concatenate([jnp.where(on, piece, 0.0) for piece in pieces(line_value)], axis=0)
    found = lax.dot_general(
        stacked.astype(BF16), hits, (((1,), (1,)), ((), ())), preferred_element_type=F32
    )
    return found[0:count] + found[count : 2 * count] + found[2 * count :]


def hits_of(line_column):
    shape = (LANES, line_column.shape[1])
    return jnp.where(iota(shape, 0).astype(F32) == line_column, 1.0, 0.0).astype(BF16)


def main_kernel(
    rows, levels, d_ref, obs_ref, turned_ref, a_ref, b_ref, vertical_ref, weights_ref, mine_ref, other_ref,
    member, d_all, halo, first, second, hits_all, key_all, back,
):
    tiles = obs_ref.shape[1]
    blocks = obs_ref.shape[2] // LANES
    block = min(tiles, LANES // GROUP)
    columns = d_ref.shape[1]
    me, band = lax.axis_index("tx"), lax.axis_index("ty")
    even, last = lax.rem(band, 2) == 0, lax.axis_size("ty") - 1
    core = lax.rem(me, 2)
    half, own = STEPS * levels, rows * levels
    deep = STEPS - 1

    member[half : half + own, :] = turned_ref[...].astype(F32)
    d_all[STEPS : STEPS + rows, :] = d_ref[...]
    got_a, got_b = a_ref[...].astype(F32), b_ref[...].astype(F32)
    above = jnp.where(band == 0, 0.0, jnp.where(even, got_b, got_a))
    below = jnp.where(band == last, 0.0, jnp.where(even, got_a, got_b))
    member[0:half, :] = above[0:half]
    member[half + own :, :] = below[0:half]

    def cut(lines):
        return [
            [
                [stagger(part[q * block : (q + 1) * block]) for q in range(tiles // block)]
                for part in line
            ]
            for line in lines
        ]

    sets = [cut([[obs_ref[q, :, b * LANES : (b + 1) * LANES] for b in range(blocks)] for q in range(3)])]
    for side, (got, start) in enumerate(((above, 1), (below, STEPS + rows))):
        for t in range(tiles):
            halo[side, t] = got[half:, t * LANES : (t + 1) * LANES]
            d = halo[side, t, 0:deep, :] + halo[side, t, deep : 2 * deep, :] + halo[side, t, 2 * deep : 3 * deep, :]
            d_all[start : start + deep, t * LANES : (t + 1) * LANES] = d
        at = 3 * deep
        lines = [[halo[side, :, at + i * blocks + b, :] for b in range(blocks)] for i in range(5)]
        value = [lines[0][b] + lines[1][b] + lines[2][b] for b in range(blocks)]
        sets.append(cut([value, lines[3], lines[4]]))

    places = ((half, own, 0), (0, half, own - half), (half + own, half, 0))
    for t in range(tiles):
        at = slice(t * LANES, (t + 1) * LANES)
        for i, (begin, count, base) in enumerate(places):
            value, key, column = (lines_of(x, t, block) for x in sets[i])
            hits = hits_of(column)
            if i == 0:
                hits_all[t] = hits
                key_all[t] = jnp.broadcast_to(key, (8, key.shape[1]))
            field = spread(value, key, hits, count, float(base))
            first[begin : begin + count, at] = field * member[begin : begin + count, at]

    source, target = first, second
    left_end = iota((levels, columns), 1) == 0
    right_end = iota((levels, columns), 1) == columns - 1
    for step in range(STEPS):
        for r in range(step + 1, 2 * STEPS + rows - 1 - step):
            mid = source[r * levels : (r + 1) * levels, :]
            beside = (
                source[(r - 1) * levels : r * levels, :]
                + source[(r + 1) * levels : (r + 2) * levels, :]
                + jnp.where(left_end, 0.0, pltpu.roll(mid, 1, 1))
                + jnp.where(right_end, 0.0, pltpu.roll(mid, columns - 1, 1))
            )
            d = jnp.broadcast_to(d_all[r : r + 1, :], (levels, columns))
            target[r * levels : (r + 1) * levels, :] = mid + d * (beside - 4.0 * mid)
        source, target = target, source

    vertical = vertical_ref[...] * weights_ref[me]
    gap = iota((levels, levels), 1) - iota((levels, levels), 0)
    factors = [
        (o, jnp.sum(jnp.where(gap == o, vertical, 0.0), axis=1, keepdims=True)) for o in range(-BAND, BAND + 1)
    ]
    factors = [(o, jnp.broadcast_to(f, (levels, LANES))) for o, f in factors]
    chips = mine_ref.shape[0]
    for z in range(chips):
        for side, out in enumerate((mine_ref, other_ref)):
            t = 2 * z + (core ^ side)
            mirror = 2 * (2 * z // block * block) + block - 1
            at = pl.ds(pl.multiple_of(t * LANES, LANES), LANES)
            parts = []
            for r in range(rows):
                x = source[half + r * levels : half + (r + 1) * levels, at]
                mixed = sum(f * (pltpu.roll(x, -o % levels, 0) if o else x) for o, f in factors)
                part = mixed * member[half + r * levels : half + (r + 1) * levels, at]
                out[z, r * levels : (r + 1) * levels, :] = part
                parts.append(part)
            stacked = jnp.concatenate(pieces(jnp.concatenate(parts, axis=0)), axis=0).astype(BF16)
            found = jnp.dot(stacked, hits_all[t], preferred_element_type=F32)
            found = found[0:own] + found[own : 2 * own] + found[2 * own :]
            on = iota(found.shape, 0).astype(F32) == key_all[t][0:1]
            line = jnp.sum(jnp.where(on, found, 0.0), axis=0, keepdims=True)
            for q in range(tiles // block):
                back[q, pl.ds(mirror - t, 1), :] = line[:, q * LANES : (q + 1) * LANES]
    turned = [
        [stagger(back[q, b * block : (b + 1) * block, :]) for b in range(blocks)] for q in range(tiles // block)
    ]
    for z in range(chips):
        for side, out in enumerate((mine_ref, other_ref)):
            out[z, own:, :] = jnp.zeros((out.shape[1] - own, LANES), F32)
            place = 2 * z % block + (core ^ side)
            for b in range(blocks):
                out[z, own + b : own + b + 1, :] = pick(turned[2 * z // block][b], place)


def pair_kernel(mine_ref, got_ref, *outs):
    chip = lax.axis_index("tx") // 2
    for far, out in enumerate(outs):
        out[...] = mine_ref[chip ^ far] + got_ref[chip ^ far]


def final_kernel(near, *refs):
    got, (count_ref, inc_ref, proj_ref, total, wide) = refs[:near], refs[near:]
    levels, rows, _ = inc_ref.shape
    _, tiles, slots = proj_ref.shape
    block = min(tiles, LANES // GROUP)
    sums = got[0][...]
    for ref in got[1:]:
        sums = sums + ref[...]
    total[...] = sums
    for level in range(levels):
        inc_ref[level] = total[pl.ds(level, rows, stride=levels), :]
    for b in range(tiles // block):
        line = jnp.broadcast_to(total[rows * levels + b : rows * levels + b + 1, :], (block, LANES))
        line = pltpu.roll(line, (LANES - GROUP * (block - 1)) % LANES, 1)
        wide[b * block : (b + 1) * block, :] = stagger(line)
    proj_ref[0] = jnp.where(live_mask(count_ref, slots), wide[:, 0:slots], 0.0)


def call(kernel, out_shape, ins, scratch, flops=0, moved=0):
    return pl.pallas_call(
        kernel,
        out_shape=out_shape,
        in_specs=ins,
        out_specs=jax.tree.map(lambda _: VMEM, out_shape),
        scratch_shapes=scratch,
        compiler_params=pltpu.CompilerParams(vmem_limit_bytes=48 << 20),
        cost_estimate=pl.CostEstimate(flops=flops, bytes_accessed=moved, transcendentals=0),
    )


def shards(ensemble, diffusivity, vertical, weights, obs_value, obs_cell, obs_count):
    _, levels, rows, columns = ensemble.shape
    tiles, slots = obs_value.shape[1:]
    chips = tiles // 2
    bands = lax.axis_size("ty")
    assert diffusivity.shape == (rows, LANES) and slots == GROUP and rows == 2 * STEPS
    blocks = -(-tiles * GROUP // LANES)
    block = min(tiles, LANES // GROUP)
    shape = jax.ShapeDtypeStruct
    packet_rows = round_up(rows + 3 * blocks, 8)
    half, own = STEPS * levels, rows * levels
    extra = round_up(3 * (STEPS - 1) + 5 * blocks, 16)
    lanes = tiles // block * LANES

    packet = call(
        functools.partial(pack_kernel, levels),
        shape((packet_rows, LANES), F32),
        [VMEM] * 4,
        [pltpu.VMEM((3, tiles, LANES), F32)],
    )(obs_value, obs_cell, obs_count, diffusivity)
    turned = call(
        turn_kernel, shape((own, columns), BF16), [VMEM], [pltpu.VMEM((tiles, own, LANES), F32)], 1000000, 1000000
    )(ensemble)

    def swap(x, far):
        return lax.ppermute(x, "tx", [(i, i ^ far) for i in range(tiles)])

    pair = jnp.stack([packet, swap(packet, 1)])
    row = [pair] + [swap(pair, 2 * far) for far in range(1, chips)]
    d_row, obs, to_a, to_b = call(
        functools.partial(gather_kernel, chips, rows, levels),
        (
            shape((rows, columns), F32),
            shape((3, tiles, blocks * LANES), F32),
            shape((half + extra, columns), BF16),
            shape((half + extra, columns), BF16),
        ),
        [VMEM] * (chips + 1),
        [
            pltpu.VMEM((tiles, packet_rows, LANES), F32),
            pltpu.VMEM((extra, LANES), F32),
            pltpu.VMEM((extra, LANES), F32),
        ],
    )(*row, turned)
    pairs_a = [(i, i ^ 1) for i in range(bands)]
    pairs_b = [(i, (i + 1 if i % 2 else i - 1) % bands) for i in range(bands)]
    from_a = lax.ppermute(to_a, "ty", pairs_a)
    from_b = lax.ppermute(to_b, "ty", pairs_b)

    chunk = own + 8
    mine, other = call(
        functools.partial(main_kernel, rows, levels),
        (shape((chips, chunk, LANES), F32), shape((chips, chunk, LANES), F32)),
        [VMEM] * 6 + [SMEM],
        [
            pltpu.VMEM((2 * half + own, columns), F32),
            pltpu.VMEM((2 * STEPS + rows, columns), F32),
            pltpu.VMEM((2, tiles, extra, LANES), F32),
            pltpu.VMEM((2 * half + own, columns), F32),
            pltpu.VMEM((2 * half + own, columns), F32),
            pltpu.VMEM((tiles, LANES, lanes), BF16),
            pltpu.VMEM((tiles, 8, lanes), F32),
            pltpu.VMEM((tiles // block, tiles, LANES), F32),
        ],
    )(d_row, obs, turned, from_a, from_b, vertical, weights)
    sums = call(
        pair_kernel, tuple(shape((chunk, LANES), F32) for _ in range(chips)), [VMEM] * 2, []
    )(mine, swap(other, 1))
    sums = [sums[0]] + [swap(sums[far], 2 * far) for far in range(1, chips)]
    return call(
        functools.partial(final_kernel, chips),
        (shape((levels, rows, LANES), F32), shape((1, tiles, slots), F32)),
        [VMEM] * (chips + 1),
        [pltpu.VMEM((chunk, LANES), F32), pltpu.VMEM((tiles, LANES), F32)],
    )(*sums, obs_count)


def solution(mesh):
    placed = (
        P("tx", None, "ty", None),
        P("ty", "tx"),
        P(),
        P(),
        P(("ty", "tx"), None, None),
        P(("ty", "tx"), None, None),
        P(("ty", "tx"), None),
    )
    return jax.shard_map(
        shards,
        mesh=mesh,
        in_specs=placed,
        out_specs=(P(None, "ty", "tx"), P(("ty", "tx"), None, None)),
        check_vma=False,
    )
```

time: 136 us -> 35 us (0.26)
  the two profiles are of different devices: /device:TPU:4 before, /device:TPU:0 now
where the time goes in v1:
time: 35 us; the launch traced here: 34.8 us
  starting transfers between devices  13.5 us (39%)
  waiting for transfers between devices  12.8 us (37%)
  local copies, waits for them, and re-layouts  4.27 us (12%)
  Pallas kernels  3.48 us (10%)
  between operations  0.7 us (2%)
    ppermute x8, starting transfers between devices, swap(): return lax.ppermute(x, 'tx', [(i, i ^ far) for i in range(tiles)])  10.5 us
    ppermute x8, waiting for transfers between devices, swap(): return lax.ppermute(x, 'tx', [(i, i ^ far) for i in range(tiles)])  8.75 us
    unnamed x16, local copies, waits for them, and re-layouts  4.27 us
    ppermute x1, waiting for transfers between devices, shards(): from_a = lax.ppermute(to_a, 'ty', pairs_a)  2.57 us
    pallas_call x1, Pallas kernels, shards(): call(functools.partial(main_kernel, rows, levels), (shape((chips, chunk,...  2.4 us
    ppermute x1, starting transfers between devices, shards(): from_a = lax.ppermute(to_a, 'ty', pairs_a)  1.56 us
    ppermute x1, starting transfers between devices, shards(): from_b = lax.ppermute(to_b, 'ty', pairs_b)  1.49 us
    ppermute x1, waiting for transfers between devices, shards(): from_b = lax.ppermute(to_b, 'ty', pairs_b)  1.45 us
  transfers between devices with their start and end apart: 10, of which 8 were waited for; matrix products, arithmetic and copies ran while one was open for 0% of the time, Pallas kernels for 0%

profile of v1, /device:TPU:0, one launch (start us, length us, event | category | flops | bytes accessed | tf_op | source)
XLA Modules:
  0.0 34.8 jit_solution(17022696116704341406)
XLA Ops:
  0.6 0.7 %copy-done.2 = f32[1,8,8]{2,1,0:T(8,128)S(1)} copy-done((f32[1,8,8]{2,1,0:T(8,128)S(1)}, f32[1,8,8]{2,1,0:T(8,128)}, u32[]{:S(2)}) %copy-start.2) | copy-done | bytes 280
  1.3 0.7 %copy-done.3 = s32[1,8,8]{2,1,0:T(8,128)S(1)} copy-done((s32[1,8,8]{2,1,0:T(8,128)S(1)}, s32[1,8,8]{2,1,0:T(8,128)}, u32[]{:S(2)}) %copy-start.3) | copy-done | bytes 280
  2.0 0.7 %copy-done.4 = f32[8,128]{1,0:T(8,128)S(1)} copy-done((f32[8,128]{1,0:T(8,128)S(1)}, f32[8,128]{1,0:T(8,128)}, u32[]{:S(2)}) %copy-start.4) | copy-done | bytes 4120
  2.7 0.7 %copy-done.5 = s32[1,8]{1,0:T(1,128)S(1)} copy-done((s32[1,8]{1,0:T(1,128)S(1)}, s32[1,8]{1,0:T(1,128)}, u32[]{:S(2)}) %copy-start.5) | copy-done | bytes 56
  3.3 0.2 shard_map.86
  3.5 0.5 %collective-permute-start = (f32[16,128]{1,0:T(8,128)S(1)}, f32[16,128]{1,0:T(8,128)S(1)}, u32[]{:S(2)}, u32[]{:S(2)}) collective-permute-start(f32[16,128]{1,0:T(8,128)S(1)} %shard_map.86), channel_id=1, source_target_pairs={{0,1},{1,0},{2,3},{3,2},{4,5},{5,4},{6,7},{7,6},{8,9},{9,8},{10,11... | collective-permute-start | bytes 24584 | tf_op jit(solution)/shard_map/ppermute | solution.py:323
  4.0 0.8 %collective-permute-done = f32[16,128]{1,0:T(8,128)S(1)} collective-permute-done((f32[16,128]{1,0:T(8,128)S(1)}, f32[16,128]{1,0:T(8,128)S(1)}, u32[]{:S(2)}, u32[]{:S(2)}) %collective-permute-start) | collective-permute-done | bytes 8224 | tf_op jit(solution)/shard_map/ppermute | solution.py:323
  4.8 4.9 %collective-permute-start.3 = (f32[2,16,128]{2,1,0:T(8,128)S(1)}, f32[2,16,128]{2,1,0:T(8,128)S(1)}, u32[]{:S(2)}, u32[]{:S(2)}) collective-permute-start(f32[2,16,128]{2,1,0:T(8,128)S(1)} %pad_maximum_fusion.refs_0_), channel_id=1, source_target_pairs={{0,6},{1,7},{2,4},{3,5},{4,2},{5,3},{6,0},{7,1},{8,14},{9,15},{10,... | collective-permute-start | bytes 49160 | tf_op jit(solution)/shard_map/ppermute | solution.py:323
  9.7 0.0 collective-permute-start.2
  9.7 0.6 %collective-permute-start.1 = (f32[2,16,128]{2,1,0:T(8,128)S(1)}, f32[2,16,128]{2,1,0:T(8,128)S(1)}, u32[]{:S(2)}, u32[]{:S(2)}) collective-permute-start(f32[2,16,128]{2,1,0:T(8,128)S(1)} %pad_maximum_fusion.refs_0_), channel_id=1, source_target_pairs={{0,2},{1,3},{2,0},{3,1},{4,6},{5,7},{6,4},{7,5},{8,10},{9,11},{10,... | collective-permute-start | bytes 49160 | tf_op jit(solution)/shard_map/ppermute | solution.py:323
  10.3 0.9 %copy-done = bf16[1,8,8,1024]{3,2,1,0:T(8,128)(2,1)S(1)} copy-done((bf16[1,8,8,1024]{3,2,1,0:T(8,128)(2,1)S(1)}, bf16[1,8,8,1024]{3,2,1,0:T(8,128)(2,1)}, u32[]{:S(2)}) %copy-start) | copy-done | bytes 131096
  11.2 0.1 shard_map.87.refs_4_.turned_ref
  11.3 0.2 collective-permute-done.3.refs_3_
  11.5 2.9 %collective-permute-done.2.refs_2_ = f32[2,16,128]{2,1,0:T(8,128)S(1)} collective-permute-done((f32[2,16,128]{2,1,0:T(8,128)S(1)}, f32[2,16,128]{2,1,0:T(8,128)S(1)}, u32[]{:S(2)}, u32[]{:S(2)}) %collective-permute-start.2) | collective-permute-done | bytes 16416 | tf_op jit(solution)/shard_map/ppermute | solution.py:323
  14.4 0.0 collective-permute-done.1.refs_1_
  14.4 0.1 shard_map.88
  14.5 0.0 copy-start.1
  14.5 1.6 %collective-permute-start.4 = (bf16[48,1024]{1,0:T(8,128)(2,1)S(1)}, bf16[48,1024]{1,0:T(8,128)(2,1)S(1)}, u32[]{:S(2)}, u32[]{:S(2)}) collective-permute-start(bf16[48,1024]{1,0:T(8,128)(2,1)S(1)} %get-tuple-element.14), channel_id=1, source_target_pairs={{0,8},{8,0},{16,24},{24,16},{1,9},{9,1},{17,25},{25,17},{2,10},{10... | collective-permute-start | bytes 294920 | tf_op jit(solution)/shard_map/ppermute | solution.py:344
  16.0 1.5 %collective-permute-start.5 = (bf16[48,1024]{1,0:T(8,128)(2,1)S(1)}, bf16[48,1024]{1,0:T(8,128)(2,1)S(1)}, u32[]{:S(2)}, u32[]{:S(2)}) collective-permute-start(bf16[48,1024]{1,0:T(8,128)(2,1)S(1)} %get-tuple-element.15), channel_id=1, source_target_pairs={{0,24},{8,16},{16,8},{24,0},{1,25},{9,17},{17,9},{25,1},{2,26},{10... | collective-permute-start | bytes 294920 | tf_op jit(solution)/shard_map/ppermute | solution.py:345
  17.5 2.6 %collective-permute-done.4.a_ref = bf16[48,1024]{1,0:T(8,128)(2,1)S(1)} collective-permute-done((bf16[48,1024]{1,0:T(8,128)(2,1)S(1)}, bf16[48,1024]{1,0:T(8,128)(2,1)S(1)}, u32[]{:S(2)}, u32[]{:S(2)}) %collective-permute-start.4) | collective-permute-done | bytes 98336 | tf_op jit(solution)/shard_map/ppermute | solution.py:344
  20.1 1.5 %collective-permute-done.5.b_ref = bf16[48,1024]{1,0:T(8,128)(2,1)S(1)} collective-permute-done((bf16[48,1024]{1,0:T(8,128)(2,1)S(1)}, bf16[48,1024]{1,0:T(8,128)(2,1)S(1)}, u32[]{:S(2)}, u32[]{:S(2)}) %collective-permute-start.5) | collective-permute-done | bytes 98336 | tf_op jit(solution)/shard_map/ppermute | solution.py:345
  21.6 0.7 %copy-done.7 = f32[8]{0:T(128)S(1)} copy-done((f32[8]{0:T(128)S(1)}, f32[8]{0:T(128)}, u32[]{:S(2)}) %copy-start.7) | copy-done | bytes 56
  22.2 2.4 %shard_map.89 = (f32[4,72,128]{2,1,0:T(8,128)S(1)}, f32[4,72,128]{2,1,0:T(8,128)S(1)}) custom-call(f32[8,1024]{1,0:T(8,128)S(1)} %get-tuple-element.12.d_ref, f32[3,8,128]{2,1,0:T(8,128)S(1)} %get-tuple-element.13.obs_ref, bf16[64,1024]{1,0:T(8,128)(2,1)S(1)} %shard_map.87.refs_4_.turned_ref, bf16[48,1024]{1,0:T(8,128)(2,1)S(1)} %collective-permute-done.4.a_ref, ...), custom_call_target="tpu_custom_call" | custom-call | tf_op jit(solution)/shard_map/pallas_call | solution.py:348
  24.6 0.1 collective-permute-start.6
  24.7 1.4 %collective-permute-done.6.got_ref = f32[4,72,128]{2,1,0:T(8,128)S(1)} collective-permute-done((f32[4,72,128]{2,1,0:T(8,128)S(1)}, f32[4,72,128]{2,1,0:T(8,128)S(1)}, u32[]{:S(2)}, u32[]{:S(2)}) %collective-permute-start.6) | collective-permute-done | bytes 147488 | tf_op jit(solution)/shard_map/ppermute | solution.py:323
  26.1 0.1 collective-permute-start.7
  26.2 2.1 %collective-permute-start.8 = (f32[72,128]{1,0:T(8,128)S(1)}, f32[72,128]{1,0:T(8,128)S(1)}, u32[]{:S(2)}, u32[]{:S(2)}) collective-permute-start(f32[72,128]{1,0:T(8,128)S(1)} %get-tuple-element.20), channel_id=1, source_target_pairs={{0,4},{1,5},{2,6},{3,7},{4,0},{5,1},{6,2},{7,3},{8,12},{9,13},{10,... | collective-permute-start | bytes 110600 | tf_op jit(solution)/shard_map/ppermute | solution.py:323
  28.3 2.3 %collective-permute-start.9 = (f32[72,128]{1,0:T(8,128)S(1)}, f32[72,128]{1,0:T(8,128)S(1)}, u32[]{:S(2)}, u32[]{:S(2)}) collective-permute-start(f32[72,128]{1,0:T(8,128)S(1)} %get-tuple-element.21), channel_id=1, source_target_pairs={{0,6},{1,7},{2,4},{3,5},{4,2},{5,3},{6,0},{7,1},{8,14},{9,15},{10,... | collective-permute-start | bytes 110600 | tf_op jit(solution)/shard_map/ppermute | solution.py:323
  30.5 0.0 collective-permute-done.7.refs_1_
  30.5 0.9 %collective-permute-done.8.refs_2_ = f32[72,128]{1,0:T(8,128)S(1)} collective-permute-done((f32[72,128]{1,0:T(8,128)S(1)}, f32[72,128]{1,0:T(8,128)S(1)}, u32[]{:S(2)}, u32[]{:S(2)}) %collective-permute-start.8) | collective-permute-done | bytes 36896 | tf_op jit(solution)/shard_map/ppermute | solution.py:323
  31.4 2.6 %collective-permute-done.9.refs_3_ = f32[72,128]{1,0:T(8,128)S(1)} collective-permute-done((f32[72,128]{1,0:T(8,128)S(1)}, f32[72,128]{1,0:T(8,128)S(1)}, u32[]{:S(2)}, u32[]{:S(2)}) %collective-permute-start.9) | collective-permute-done | bytes 36896 | tf_op jit(solution)/shard_map/ppermute | solution.py:323
  34.0 0.7 %shard_map.91 = (f32[8,8,128]{2,1,0:T(8,128)}, f32[1,8,8]{2,1,0:T(8,128)}) custom-call(f32[72,128]{1,0:T(8,128)S(1)} %get-tuple-element.18.refs_0_, f32[72,128]{1,0:T(8,128)S(1)} %collective-permute-done.7.refs_1_, f32[72,128]{1,0:T(8,128)S(1)} %collective-permute-done.8.refs_2_, f32[72,128]{1,0:T(8,128)S(1)} %collective-permute-done.9.refs_3_, ...), custom_call_target="tpu_custom_call" | custom-call | tf_op jit(solution)/shard_map/pallas_call | solution.py:367
  (11 shorter events, 0.0 us)
Async XLA Ops:
  0.6 0.7 %copy-start.2 = (f32[1,8,8]{2,1,0:T(8,128)S(1)}, f32[1,8,8]{2,1,0:T(8,128)}, u32[]{:S(2)}) copy-start(f32[1,8,8]{2,1,0:T(8,128)} %value_ref.1) | copy-start | bytes 772
  1.3 0.7 %copy-start.3 = (s32[1,8,8]{2,1,0:T(8,128)S(1)}, s32[1,8,8]{2,1,0:T(8,128)}, u32[]{:S(2)}) copy-start(s32[1,8,8]{2,1,0:T(8,128)} %cell_ref.1) | copy-start | bytes 772
  2.0 0.7 %copy-start.4 = (f32[8,128]{1,0:T(8,128)S(1)}, f32[8,128]{1,0:T(8,128)}, u32[]{:S(2)}) copy-start(f32[8,128]{1,0:T(8,128)} %diff_ref.1) | copy-start | bytes 12292
  2.7 0.7 %copy-start.5 = (s32[1,8]{1,0:T(1,128)S(1)}, s32[1,8]{1,0:T(1,128)}, u32[]{:S(2)}) copy-start(s32[1,8]{1,0:T(1,128)} %refs_4_.1) | copy-start | bytes 100
  3.5 1.3 %collective-permute-start = (f32[16,128]{1,0:T(8,128)S(1)}, f32[16,128]{1,0:T(8,128)S(1)}, u32[]{:S(2)}, u32[]{:S(2)}) collective-permute-start(f32[16,128]{1,0:T(8,128)S(1)} %shard_map.86), channel_id=1, source_target_pairs={{0,1},{1,0},{2,3},{3,2},{4,5},{5,4},{6,7},{7,6},{8,9},{9,8},{10,11... | collective-permute-start | bytes 24584 | tf_op jit(solution)/shard_map/ppermute | solution.py:323
  4.8 6.7 %collective-permute-start.3 = (f32[2,16,128]{2,1,0:T(8,128)S(1)}, f32[2,16,128]{2,1,0:T(8,128)S(1)}, u32[]{:S(2)}, u32[]{:S(2)}) collective-permute-start(f32[2,16,128]{2,1,0:T(8,128)S(1)} %pad_maximum_fusion.refs_0_), channel_id=1, source_target_pairs={{0,6},{1,7},{2,4},{3,5},{4,2},{5,3},{6,0},{7,1},{8,14},{9,15},{10,... | collective-permute-start | bytes 49160 | tf_op jit(solution)/shard_map/ppermute | solution.py:323
  9.7 4.6 %collective-permute-start.2 = (f32[2,16,128]{2,1,0:T(8,128)S(1)}, f32[2,16,128]{2,1,0:T(8,128)S(1)}, u32[]{:S(2)}, u32[]{:S(2)}) collective-permute-start(f32[2,16,128]{2,1,0:T(8,128)S(1)} %pad_maximum_fusion.refs_0_), channel_id=1, source_target_pairs={{0,4},{1,5},{2,6},{3,7},{4,0},{5,1},{6,2},{7,3},{8,12},{9,13},{10,... | collective-permute-start | bytes 49160 | tf_op jit(solution)/shard_map/ppermute | solution.py:323
  9.7 4.6 %collective-permute-start.1 = (f32[2,16,128]{2,1,0:T(8,128)S(1)}, f32[2,16,128]{2,1,0:T(8,128)S(1)}, u32[]{:S(2)}, u32[]{:S(2)}) collective-permute-start(f32[2,16,128]{2,1,0:T(8,128)S(1)} %pad_maximum_fusion.refs_0_), channel_id=1, source_target_pairs={{0,2},{1,3},{2,0},{3,1},{4,6},{5,7},{6,4},{7,5},{8,10},{9,11},{10,... | collective-permute-start | bytes 49160 | tf_op jit(solution)/shard_map/ppermute | solution.py:323
  10.3 0.9 %copy-start = (bf16[1,8,8,1024]{3,2,1,0:T(8,128)(2,1)S(1)}, bf16[1,8,8,1024]{3,2,1,0:T(8,128)(2,1)}, u32[]{:S(2)}) copy-start(bf16[1,8,8,1024]{3,2,1,0:T(8,128)(2,1)} %ens_ref.1) | copy-start | bytes 393220
  14.5 7.1 %copy-start.1 = (f32[8,8]{1,0:T(8,128)S(1)}, f32[8,8]{1,0:T(8,128)}, u32[]{:S(2)}) copy-start(f32[8,8]{1,0:T(8,128)} %vertical_ref.1) | copy-start | bytes 772
  14.5 5.6 %collective-permute-start.4 = (bf16[48,1024]{1,0:T(8,128)(2,1)S(1)}, bf16[48,1024]{1,0:T(8,128)(2,1)S(1)}, u32[]{:S(2)}, u32[]{:S(2)}) collective-permute-start(bf16[48,1024]{1,0:T(8,128)(2,1)S(1)} %get-tuple-element.14), channel_id=1, source_target_pairs={{0,8},{8,0},{16,24},{24,16},{1,9},{9,1},{17,25},{25,17},{2,10},{10... | collective-permute-start | bytes 294920 | tf_op jit(solution)/shard_map/ppermute | solution.py:344
  16.0 5.5 %collective-permute-start.5 = (bf16[48,1024]{1,0:T(8,128)(2,1)S(1)}, bf16[48,1024]{1,0:T(8,128)(2,1)S(1)}, u32[]{:S(2)}, u32[]{:S(2)}) collective-permute-start(bf16[48,1024]{1,0:T(8,128)(2,1)S(1)} %get-tuple-element.15), channel_id=1, source_target_pairs={{0,24},{8,16},{16,8},{24,0},{1,25},{9,17},{17,9},{25,1},{2,26},{10... | collective-permute-start | bytes 294920 | tf_op jit(solution)/shard_map/ppermute | solution.py:345
  21.6 0.7 %copy-start.7 = (f32[8]{0:T(128)S(1)}, f32[8]{0:T(128)}, u32[]{:S(2)}) copy-start(f32[8]{0:T(128)} %weights_ref.1) | copy-start | bytes 100
  24.6 1.4 %collective-permute-start.6 = (f32[4,72,128]{2,1,0:T(8,128)S(1)}, f32[4,72,128]{2,1,0:T(8,128)S(1)}, u32[]{:S(2)}, u32[]{:S(2)}) collective-permute-start(f32[4,72,128]{2,1,0:T(8,128)S(1)} %get-tuple-element.17), channel_id=1, source_target_pairs={{0,1},{1,0},{2,3},{3,2},{4,5},{5,4},{6,7},{7,6},{8,9},{9,8},{10,11... | collective-permute-start | bytes 442376 | tf_op jit(solution)/shard_map/ppermute | solution.py:323
  26.1 4.5 %collective-permute-start.7 = (f32[72,128]{1,0:T(8,128)S(1)}, f32[72,128]{1,0:T(8,128)S(1)}, u32[]{:S(2)}, u32[]{:S(2)}) collective-permute-start(f32[72,128]{1,0:T(8,128)S(1)} %get-tuple-element.19), channel_id=1, source_target_pairs={{0,2},{1,3},{2,0},{3,1},{4,6},{5,7},{6,4},{7,5},{8,10},{9,11},{10,... | collective-permute-start | bytes 110600 | tf_op jit(solution)/shard_map/ppermute | solution.py:323
  26.2 5.2 %collective-permute-start.8 = (f32[72,128]{1,0:T(8,128)S(1)}, f32[72,128]{1,0:T(8,128)S(1)}, u32[]{:S(2)}, u32[]{:S(2)}) collective-permute-start(f32[72,128]{1,0:T(8,128)S(1)} %get-tuple-element.20), channel_id=1, source_target_pairs={{0,4},{1,5},{2,6},{3,7},{4,0},{5,1},{6,2},{7,3},{8,12},{9,13},{10,... | collective-permute-start | bytes 110600 | tf_op jit(solution)/shard_map/ppermute | solution.py:323
  28.3 5.8 %copy-start.6 = (s32[1,8]{1,0:T(1,128)S(1)}, s32[1,8]{1,0:T(1,128)}, u32[]{:S(2)}) copy-start(s32[1,8]{1,0:T(1,128)} %refs_4_.1) | copy-start | bytes 100
  28.3 5.8 %collective-permute-start.9 = (f32[72,128]{1,0:T(8,128)S(1)}, f32[72,128]{1,0:T(8,128)S(1)}, u32[]{:S(2)}, u32[]{:S(2)}) collective-permute-start(f32[72,128]{1,0:T(8,128)S(1)} %get-tuple-element.21), channel_id=1, source_target_pairs={{0,6},{1,7},{2,4},{3,5},{4,2},{5,3},{6,0},{7,1},{8,14},{9,15},{10,... | collective-permute-start | bytes 110600 | tf_op jit(solution)/shard_map/ppermute | solution.py:323

commit v2 on v1

v2 whole, which is shorter than its diff:
```python
import functools

import jax
import jax.numpy as jnp
from jax import lax
from jax.experimental import pallas as pl
from jax.experimental.pallas import tpu as pltpu
from jax.sharding import PartitionSpec as P

STEPS = 4
BAND = 2
LANES = 128
GROUP = 8
F32, BF16 = jnp.float32, jnp.bfloat16
VMEM = pl.BlockSpec(memory_space=pltpu.VMEM)
HBM = pl.BlockSpec(memory_space=pltpu.HBM)


def round_up(n, m):
    return -(-n // m) * m


def log2(n):
    assert n & (n - 1) == 0
    return n.bit_length() - 1


def iota(shape, axis):
    return lax.broadcasted_iota(jnp.int32, shape, axis)


def pieces(x):
    high = x.astype(BF16).astype(F32)
    rest = x - high
    middle = rest.astype(BF16).astype(F32)
    return high, middle, rest - middle


def stagger(x):
    return pltpu.roll(x, 0, 1, stride=GROUP, stride_axis=0)


def pick(x, place):
    if isinstance(place, int):
        shift = (-GROUP * place) % LANES
    else:
        shift = lax.rem(LANES - GROUP * place, LANES)
    rolled = pltpu.roll(x, shift, 1)
    own = iota(x.shape, 1) // GROUP == iota(x.shape, 0)
    return jnp.sum(jnp.where(own, rolled, 0.0), axis=0, keepdims=True)


def live_mask(count_ref, slots):
    tiles = count_ref.shape[1]
    count = jnp.broadcast_to(count_ref[...].astype(F32), (tiles, tiles))
    diagonal = iota((tiles, tiles), 0) == iota((tiles, tiles), 1)
    column = jnp.sum(jnp.where(diagonal, count, 0.0), axis=1, keepdims=True)
    return iota((tiles, slots), 1).astype(F32) < column


def first_kernel(
    copies, value_hbm, cell_hbm, count_hbm, diff_hbm, ens_hbm, vertical_hbm, weights_hbm,
    sent_ref, turned_ref, a_ref, b_ref, factors_ref, live_ref,
    value_ref, cell_ref, count_ref, diff_ref, ens_ref, vertical_ref, weights_ref, wide, packet, tall, sems,
):
    pairs = (
        (value_hbm, value_ref), (cell_hbm, cell_ref), (count_hbm, count_ref), (diff_hbm, diff_ref),
        (ens_hbm, ens_ref), (vertical_hbm, vertical_ref), (weights_hbm, weights_ref),
    )
    moves = [pltpu.make_async_copy(x, y, sems.at[i]) for i, (x, y) in enumerate(pairs)]
    for move in moves:
        move.start()
    wide[...] = jnp.zeros_like(wide)
    for move in moves[:4]:
        move.wait()
    _, tiles, slots = value_ref.shape
    rows = diff_ref.shape[0]
    block = min(tiles, LANES // GROUP)
    live = live_mask(count_ref, slots)
    wide[0, :, 0:slots] = jnp.where(live, value_ref[0], 0.0)
    wide[1, :, 0:slots] = cell_ref[0].astype(F32)
    live_ref[...] = jnp.zeros_like(live_ref)
    live_ref[:, 0:slots] = jnp.where(live, 1.0, 0.0)
    packet[0:rows, :] = diff_ref[...]
    lines = [pick(stagger(wide[q, b : b + block, :]), 0) for q in range(2) for b in range(0, tiles, block)]
    if block * GROUP < LANES:
        lines = [lines[0] + pltpu.roll(lines[1], block * GROUP, 1)]
    for i, line in enumerate(lines):
        packet[rows + i : rows + i + 1, :] = line
    height = packet.shape[0]
    for i in range(copies):
        sent_ref[i * height : (i + 1) * height, :] = packet[...]

    for move in moves[4:]:
        move.wait()
    _, levels, _, columns = ens_ref.shape
    for t in range(columns // LANES):
        at = slice(t * LANES, (t + 1) * LANES)
        tall[t] = ens_ref[0, :, :, at].astype(F32).reshape(levels * rows, LANES)
        for r in range(0, rows, 2):
            both = [tall[t, pl.ds(r + i, levels, stride=rows), :] for i in range(2)]
            turned_ref[r * levels : (r + 2) * levels, at] = jnp.concatenate(both, axis=0).astype(BF16)
    half = STEPS * levels
    even = lax.rem(lax.axis_index("ty"), 2) == 0
    off_a, off_b = jnp.where(even, half, 0), jnp.where(even, 0, half)
    a_ref[...] = turned_ref[pl.ds(pl.multiple_of(off_a, half), half), :]
    b_ref[...] = turned_ref[pl.ds(pl.multiple_of(off_b, half), half), :]
    vertical = vertical_ref[...] * weights_ref[lax.axis_index("tx")]
    gap = iota((levels, levels), 1) - iota((levels, levels), 0)
    for i in range(2 * BAND + 1):
        factor = jnp.sum(jnp.where(gap == i - BAND, vertical, 0.0), axis=1, keepdims=True)
        factors_ref[i] = jnp.broadcast_to(factor, (levels, LANES))


def lines_of(staggered, place, tiles):
    size = staggered[0][0].shape[0]
    groups = LANES // GROUP
    return jnp.concatenate([pick(part, place % groups) for part in staggered[place // groups]], axis=1)


def spread(line_value, line_key, hits, count, first):
    key = line_key - first
    on = iota((count, line_key.shape[1]), 0).astype(F32) == key
    stacked = jnp.concatenate([jnp.where(on, piece, 0.0) for piece in pieces(line_value)], axis=0)
    found = lax.dot_general(
        stacked.astype(BF16), hits, (((1,), (1,)), ((), ())), preferred_element_type=F32
    )
    return found[0:count] + found[count : 2 * count] + found[2 * count :]


def hits_of(line_column):
    shape = (LANES, line_column.shape[1])
    return jnp.where(iota(shape, 0).astype(F32) == line_column, 1.0, 0.0).astype(BF16)


def forcing_kernel(rows, levels, tiles, got_ref, field_ref, d_ref, hits_ref, key_ref):
    band, last = lax.axis_index("ty"), lax.axis_size("ty") - 1
    half, own, deep = STEPS * levels, rows * levels, STEPS - 1
    height = got_ref.shape[0] // (tiles * (last + 1))
    lines, block = height - rows, min(tiles, LANES // GROUP)
    bands = (
        (band, None, half, own, 0, STEPS, rows, 0),
        (jnp.maximum(band - 1, 0), band > 0, 0, half, own - half, 1, deep, rows - deep),
        (jnp.minimum(band + 1, last), band < last, half + own, half, 0, STEPS + rows, deep, 0),
    )
    for side, (which, inside, begin, count, base, d_begin, d_count, d_base) in enumerate(bands):
        start = which * (tiles * height)
        values, keys, columns = [], [], []
        for i in range(lines):
            x = got_ref[pl.ds(start + rows + i, tiles, stride=height), :]
            cell = x.astype(jnp.int32)
            flat = lax.shift_right_logical(cell, log2(LANES))
            key = (flat & (rows - 1)) * levels + lax.shift_right_logical(flat, log2(rows))
            if inside is not None:
                x = jnp.where(inside, x, 0.0)
            for out, part in ((values, x), (keys, key.astype(F32)), (columns, (cell & (LANES - 1)).astype(F32))):
                out.append([stagger(part[q : q + block]) for q in range(0, tiles, block)])
        for t in range(tiles):
            at = slice(t * LANES, (t + 1) * LANES)
            d = got_ref[pl.ds(start + t * height + d_base, d_count), :]
            d_ref[d_begin : d_begin + d_count, at] = d if inside is None else jnp.where(inside, d, 0.0)
            value = lines_of(values, t, tiles)
            key, column = lines_of(keys, tiles + t, tiles), lines_of(columns, tiles + t, tiles)
            hits = hits_of(column)
            if side == 0:
                hits_ref[t] = hits
                key_ref[t] = jnp.broadcast_to(key, (8, key.shape[1]))
            field_ref[begin : begin + count, at] = spread(value, key, hits, count, float(base))


def main_kernel(
    rows, levels, field_ref, d_all, hits_all, key_all, turned_ref, a_ref, b_ref, factors_ref, mine_ref, other_ref,
    member, first, second, back,
):
    tiles = hits_all.shape[0]
    blocks = -(-tiles * GROUP // LANES)
    block = min(tiles, LANES // GROUP)
    columns = turned_ref.shape[1]
    band, core = lax.axis_index("ty"), lax.rem(lax.axis_index("tx"), 2)
    even, last = lax.rem(band, 2) == 0, lax.axis_size("ty") - 1
    half, own = STEPS * levels, rows * levels

    member[...] = turned_ref[...].astype(F32)
    first[half : half + own, :] = field_ref[half : half + own, :] * member[...]
    got_a, got_b = a_ref[...].astype(F32), b_ref[...].astype(F32)
    above = jnp.where(band == 0, 0.0, jnp.where(even, got_b, got_a))
    below = jnp.where(band == last, 0.0, jnp.where(even, got_a, got_b))
    first[0:half, :] = field_ref[0:half, :] * above
    first[half + own :, :] = field_ref[half + own :, :] * below

    source, target = first, second
    left_end = iota((levels, columns), 1) == 0
    right_end = iota((levels, columns), 1) == columns - 1
    for step in range(STEPS):
        for r in range(step + 1, 2 * STEPS + rows - 1 - step):
            mid = source[r * levels : (r + 1) * levels, :]
            beside = (
                source[(r - 1) * levels : r * levels, :]
                + source[(r + 1) * levels : (r + 2) * levels, :]
                + jnp.where(left_end, 0.0, pltpu.roll(mid, 1, 1))
                + jnp.where(right_end, 0.0, pltpu.roll(mid, columns - 1, 1))
            )
            d = jnp.broadcast_to(d_all[r : r + 1, :], (levels, columns))
            target[r * levels : (r + 1) * levels, :] = mid + d * (beside - 4.0 * mid)
        source, target = target, source

    factors = [(i - BAND, factors_ref[i]) for i in range(2 * BAND + 1)]
    chips = mine_ref.shape[0]
    for z in range(chips):
        for side, out in enumerate((mine_ref, other_ref)):
            t = 2 * z + (core ^ side)
            mirror = 2 * (2 * z // block * block) + block - 1
            at = pl.ds(pl.multiple_of(t * LANES, LANES), LANES)
            parts = []
            for r in range(rows):
                x = source[half + r * levels : half + (r + 1) * levels, at]
                mixed = sum(f * (pltpu.roll(x, -o % levels, 0) if o else x) for o, f in factors)
                part = mixed * member[r * levels : (r + 1) * levels, at]
                out[z, r * levels : (r + 1) * levels, :] = part
                parts.append(part)
            stacked = jnp.concatenate(pieces(jnp.concatenate(parts, axis=0)), axis=0).astype(BF16)
            found = jnp.dot(stacked, hits_all[t], preferred_element_type=F32)
            found = found[0:own] + found[own : 2 * own] + found[2 * own :]
            on = iota(found.shape, 0).astype(F32) == key_all[t][0:1]
            line = jnp.sum(jnp.where(on, found, 0.0), axis=0, keepdims=True)
            for q in range(tiles // block):
                back[q, pl.ds(mirror - t, 1), :] = line[:, q * LANES : (q + 1) * LANES]
    turned = [
        [stagger(back[q, b * block : (b + 1) * block, :]) for b in range(blocks)] for q in range(tiles // block)
    ]
    for z in range(chips):
        for side, out in enumerate((mine_ref, other_ref)):
            out[z, own:, :] = jnp.zeros((out.shape[1] - own, LANES), F32)
            place = 2 * z % block + (core ^ side)
            for b in range(blocks):
                out[z, own + b : own + b + 1, :] = pick(turned[2 * z // block][b], place)


def pair_kernel(mine_ref, got_ref, *outs):
    chip = lax.axis_index("tx") // 2
    for far, out in enumerate(outs):
        out[...] = mine_ref[chip ^ far] + got_ref[chip ^ far]


def final_kernel(near, *refs):
    got, (live_ref, inc_ref, proj_ref, total, wide) = refs[:near], refs[near:]
    levels, rows, _ = inc_ref.shape
    _, tiles, slots = proj_ref.shape
    block = min(tiles, LANES // GROUP)
    sums = got[0][...]
    for ref in got[1:]:
        sums = sums + ref[...]
    total[...] = sums
    for level in range(levels):
        inc_ref[level] = total[pl.ds(level, rows, stride=levels), :]
    for b in range(tiles // block):
        line = jnp.broadcast_to(total[rows * levels + b : rows * levels + b + 1, :], (block, LANES))
        line = pltpu.roll(line, (LANES - GROUP * (block - 1)) % LANES, 1)
        wide[b * block : (b + 1) * block, :] = stagger(line)
    proj_ref[0] = jnp.where(live_ref[:, 0:slots] > 0.0, wide[:, 0:slots], 0.0)


def call(kernel, out_shape, ins, scratch, flops=0, moved=0):
    return pl.pallas_call(
        kernel,
        out_shape=out_shape,
        in_specs=ins,
        out_specs=jax.tree.map(lambda _: VMEM, out_shape),
        scratch_shapes=scratch,
        compiler_params=pltpu.CompilerParams(vmem_limit_bytes=48 << 20),
        cost_estimate=pl.CostEstimate(flops=flops, bytes_accessed=moved, transcendentals=0),
    )


def shards(ensemble, diffusivity, vertical, weights, obs_value, obs_cell, obs_count):
    _, levels, rows, columns = ensemble.shape
    tiles, slots = obs_value.shape[1:]
    chips = tiles // 2
    bands = lax.axis_size("ty")
    devices = bands * tiles
    assert diffusivity.shape == (rows, LANES) and slots == GROUP and rows == 2 * STEPS
    block = min(tiles, LANES // GROUP)
    shape = jax.ShapeDtypeStruct
    height = rows + -(-2 * tiles * GROUP // LANES)
    half, own = STEPS * levels, rows * levels
    lanes = tiles // block * LANES

    sent, turned, to_a, to_b, factors, live = call(
        functools.partial(first_kernel, devices),
        (
            shape((devices * height, LANES), F32),
            shape((own, columns), BF16),
            shape((half, columns), BF16),
            shape((half, columns), BF16),
            shape((2 * BAND + 1, levels, LANES), F32),
            shape((tiles, LANES), F32),
        ),
        [HBM] * 7,
        [
            pltpu.VMEM(obs_value.shape, F32),
            pltpu.VMEM(obs_cell.shape, jnp.int32),
            pltpu.VMEM(obs_count.shape, jnp.int32),
            pltpu.VMEM(diffusivity.shape, F32),
            pltpu.VMEM(ensemble.shape, BF16),
            pltpu.VMEM(vertical.shape, F32),
            pltpu.SMEM(weights.shape, F32),
            pltpu.VMEM((2, tiles, LANES), F32),
            pltpu.VMEM((height, LANES), F32),
            pltpu.VMEM((tiles, own, LANES), F32),
            pltpu.SemaphoreType.DMA((7,)),
        ],
    )(
        *(
            pltpu.with_memory_space_constraint(x, pltpu.HBM)
            for x in (obs_value, obs_cell, obs_count, diffusivity, ensemble, vertical, weights)
        )
    )

    got = lax.all_to_all(
        sent.reshape(devices, 1, height * LANES), ("ty", "tx"), split_axis=0, concat_axis=0, tiled=True
    ).reshape(devices * height, LANES)
    pairs_a = [(i, i ^ 1) for i in range(bands)]
    pairs_b = [(i, (i + 1 if i % 2 else i - 1) % bands) for i in range(bands)]
    from_a = lax.ppermute(to_a, "ty", pairs_a)
    from_b = lax.ppermute(to_b, "ty", pairs_b)

    field, d_all, hits, key = call(
        functools.partial(forcing_kernel, rows, levels, tiles),
        (
            shape((2 * half + own, columns), F32),
            shape((2 * STEPS + rows, columns), F32),
            shape((tiles, LANES, lanes), BF16),
            shape((tiles, 8, lanes), F32),
        ),
        [VMEM],
        [],
    )(got)
    chunk = own + 8
    mine, other = call(
        functools.partial(main_kernel, rows, levels),
        (shape((chips, chunk, LANES), F32), shape((chips, chunk, LANES), F32)),
        [VMEM] * 8,
        [
            pltpu.VMEM((own, columns), F32),
            pltpu.VMEM((2 * half + own, columns), F32),
            pltpu.VMEM((2 * half + own, columns), F32),
            pltpu.VMEM((tiles // block, tiles, LANES), F32),
        ],
    )(field, d_all, hits, key, turned, from_a, from_b, factors)

    def swap(x, far):
        return lax.ppermute(x, "tx", [(i, i ^ far) for i in range(tiles)])

    sums = call(
        pair_kernel, tuple(shape((chunk, LANES), F32) for _ in range(chips)), [VMEM] * 2, []
    )(mine, swap(other, 1))
    sums = [sums[0]] + [swap(sums[far], 2 * far) for far in range(1, chips)]
    return call(
        functools.partial(final_kernel, chips),
        (shape((levels, rows, LANES), F32), shape((1, tiles, slots), F32)),
        [VMEM] * (chips + 1),
        [pltpu.VMEM((chunk, LANES), F32), pltpu.VMEM((tiles, LANES), F32)],
    )(*sums, live)


def solution(mesh):
    placed = (
        P("tx", None, "ty", None),
        P("ty", "tx"),
        P(),
        P(),
        P(("ty", "tx"), None, None),
        P(("ty", "tx"), None, None),
        P(("ty", "tx"), None),
    )
    return jax.shard_map(
        shards,
        mesh=mesh,
        in_specs=placed,
        out_specs=(P(None, "ty", "tx"), P(("ty", "tx"), None, None)),
        check_vma=False,
    )
```

time: 35 us -> 31.4 us (0.90)
  local copies, waits for them, and re-layouts: 4.27 us -> 0 us
  waiting for transfers between devices: 12.8 us -> 10.2 us
  starting transfers between devices: 13.5 us -> 15.6 us
  Pallas kernels: 3.48 us -> 4.68 us
    all_to_all x0 -> x1, starting transfers between devices: none -> 7.3 us  [shards(): lax.all_to_all(sent.reshape(devices, 1, height * LANES), ('ty', 'tx'), sp...]
    ppermute x8 -> x4, starting transfers between devices: 10.5 us -> 4.97 us  [swap(): return lax.ppermute(x, 'tx', [(i, i ^ far) for i in range(tiles)])]
    all_to_all x0 -> x1, waiting for transfers between devices: none -> 5.02 us  [shards(): lax.all_to_all(sent.reshape(devices, 1, height * LANES), ('ty', 'tx'), sp...]
    unnamed x16 -> x0, local copies, waits for them, and re-layouts: 4.27 us -> none
    ppermute x8 -> x4, waiting for transfers between devices: 8.75 us -> 5.21 us  [swap(): return lax.ppermute(x, 'tx', [(i, i ^ far) for i in range(tiles)])]
    ppermute x1, waiting for transfers between devices: 2.57 us -> 0.01 us  [shards(): from_a = lax.ppermute(to_a, 'ty', pairs_a)]
    pallas_call x3 -> x2, Pallas kernels: 0.32 us -> 2.52 us  [the longest x1 1.77 us: shards(): call(functools.partial(first_kernel, devices), (shape((devices * height,...]
    ppermute x1, waiting for transfers between devices: 1.45 us -> 0.01 us  [shards(): from_b = lax.ppermute(to_b, 'ty', pairs_b)]
  transfers between devices with their start and end apart: 10 -> 7, of which waited for: 8 -> 4; matrix products, arithmetic and copies ran while one was open for 0% -> 0% of each run, Pallas kernels for 0% -> 2%
where the time goes in v2:
time: 31.4 us; the launch traced here: 31.2 us
  starting transfers between devices  15.6 us (50%)
  waiting for transfers between devices  10.2 us (32%)
  Pallas kernels  4.68 us (15%)
  between operations  0.67 us (2%)
    all_to_all x1, starting transfers between devices, shards(): lax.all_to_all(sent.reshape(devices, 1, height * LANES), ('ty', 'tx'), sp...  7.3 us
    ppermute x4, waiting for transfers between devices, swap(): return lax.ppermute(x, 'tx', [(i, i ^ far) for i in range(tiles)])  5.21 us
    all_to_all x1, waiting for transfers between devices, shards(): lax.all_to_all(sent.reshape(devices, 1, height * LANES), ('ty', 'tx'), sp...  5.02 us
    ppermute x4, starting transfers between devices, swap(): return lax.ppermute(x, 'tx', [(i, i ^ far) for i in range(tiles)])  4.97 us
    ppermute x1, starting transfers between devices, shards(): from_a = lax.ppermute(to_a, 'ty', pairs_a)  1.83 us
    pallas_call x1, Pallas kernels, shards(): call(functools.partial(first_kernel, devices), (shape((devices * height,...  1.77 us
    ppermute x1, starting transfers between devices, shards(): from_b = lax.ppermute(to_b, 'ty', pairs_b)  1.46 us
    pallas_call x1, Pallas kernels, shards(): call(functools.partial(main_kernel, rows, levels), (shape((chips, chunk,...  1.4 us
  transfers between devices with their start and end apart: 7, of which 4 were waited for; matrix products, arithmetic and copies ran while one was open for 0% of the time, Pallas kernels for 2%

profile of v2, /device:TPU:0, one launch (start us, length us, event | category | flops | bytes accessed | tf_op | source)
XLA Modules:
  0.0 31.2 jit_solution(8475129347185845757)
XLA Ops:
  0.6 1.8 %shard_map.86 = (f32[288,128]{1,0:T(8,128)}, bf16[64,1024]{1,0:T(8,128)(2,1)S(1)}, bf16[32,1024]{1,0:T(8,128)(2,1)S(1)}, bf16[32,1024]{1,0:T(8,128)(2,1)S(1)}, f...) custom-call(f32[1,8,8]{2,1,0:T(8,128)} %value_hbm.1, s32[1,8,8]{2,1,0:T(8,128)} %cell_hbm.1, s32[1,8]{1,0:T(1,128)} %count_hbm.1, ...), custom_call_target="tpu_custom_call" | custom-call | tf_op jit(solution)/shard_map/pallas_call | solution.py:288
  2.4 7.3 %all-to-all-start = ((f32[32,1,1152]{2,1,0:T(1,128)}), f32[32,1,1152]{2,1,0:T(1,128)S(1)}, u32[]{:S(2)}, u32[]{:S(2)}) async-start(f32[32,1,1152]{2,1,0:T(1,128)} %bitcast), calls=%async_computation | async-start | bytes 294912 | tf_op jit(solution)/shard_map/all_to_all | solution.py:319
  9.7 1.8 %collective-permute-start = (bf16[32,1024]{1,0:T(8,128)(2,1)S(1)}, bf16[32,1024]{1,0:T(8,128)(2,1)S(1)}, u32[]{:S(2)}, u32[]{:S(2)}) collective-permute-start(bf16[32,1024]{1,0:T(8,128)(2,1)S(1)} %get-tuple-element.24), channel_id=1, source_target_pairs={{0,8},{8,0},{16,24},{24,16},{1,9},{9,1},{17,25},{25,17},{2,10},{10... | collective-permute-start | bytes 196616 | tf_op jit(solution)/shard_map/ppermute | solution.py:324
  11.6 1.5 %collective-permute-start.1 = (bf16[32,1024]{1,0:T(8,128)(2,1)S(1)}, bf16[32,1024]{1,0:T(8,128)(2,1)S(1)}, u32[]{:S(2)}, u32[]{:S(2)}) collective-permute-start(bf16[32,1024]{1,0:T(8,128)(2,1)S(1)} %get-tuple-element.25), channel_id=1, source_target_pairs={{0,24},{8,16},{16,8},{24,0},{1,25},{9,17},{17,9},{25,1},{2,26},{10... | collective-permute-start | bytes 196616 | tf_op jit(solution)/shard_map/ppermute | solution.py:325
  13.0 5.0 %all-to-all-done = f32[32,1,1152]{2,1,0:T(1,128)S(1)} async-done(((f32[32,1,1152]{2,1,0:T(1,128)}), f32[32,1,1152]{2,1,0:T(1,128)S(1)}, u32[]{:S(2)}, u32[]{:S(2)}) %all-to-all-start) | async-done | bytes 147488 | tf_op jit(solution)/shard_map/all_to_all | solution.py:319
  18.0 0.8 %shard_map.87 = (f32[128,1024]{1,0:T(8,128)S(1)}, f32[16,1024]{1,0:T(8,128)S(1)}, bf16[8,128,128]{2,1,0:T(8,128)(2,1)S(1)}, f32[8,8,128]{2,1,0:T(8,128)S(1)}) custom-call(f32[288,128]{1,0:T(8,128)S(1)} %bitcast.2), custom_call_target="tpu_custom_call" | custom-call | tf_op jit(solution)/shard_map/pallas_call | solution.py:327
  18.8 0.0 collective-permute-done.a_ref
  18.8 0.0 collective-permute-done.1.b_ref
  18.8 1.4 %shard_map.88 = (f32[4,72,128]{2,1,0:T(8,128)S(1)}, f32[4,72,128]{2,1,0:T(8,128)S(1)}) custom-call(f32[128,1024]{1,0:T(8,128)S(1)} %get-tuple-element.19.field_ref, f32[16,1024]{1,0:T(8,128)S(1)} %get-tuple-element.20.d_all, bf16[8,128,128]{2,1,0:T(8,128)(2,1)S(1)} %get-tuple-element.21.hits_all, f32[8,8,128]{2,1,0:T(8,128)S(1)} %get-tuple-element.22.key_all, ...), custom_call_target="tpu_custom_call" | custom-call | tf_op jit(solution)/shard_map/pallas_call | solution.py:339
  20.2 0.5 %collective-permute-start.2 = (f32[4,72,128]{2,1,0:T(8,128)S(1)}, f32[4,72,128]{2,1,0:T(8,128)S(1)}, u32[]{:S(2)}, u32[]{:S(2)}) collective-permute-start(f32[4,72,128]{2,1,0:T(8,128)S(1)} %get-tuple-element.28), channel_id=1, source_target_pairs={{0,1},{1,0},{2,3},{3,2},{4,5},{5,4},{6,7},{7,6},{8,9},{9,8},{10,11... | collective-permute-start | bytes 442376 | tf_op jit(solution)/shard_map/ppermute | solution.py:352
  20.7 1.0 %collective-permute-done.2.got_ref = f32[4,72,128]{2,1,0:T(8,128)S(1)} collective-permute-done((f32[4,72,128]{2,1,0:T(8,128)S(1)}, f32[4,72,128]{2,1,0:T(8,128)S(1)}, u32[]{:S(2)}, u32[]{:S(2)}) %collective-permute-start.2) | collective-permute-done | bytes 147488 | tf_op jit(solution)/shard_map/ppermute | solution.py:352
  21.7 0.7 %collective-permute-start.3 = (f32[72,128]{1,0:T(8,128)S(1)}, f32[72,128]{1,0:T(8,128)S(1)}, u32[]{:S(2)}, u32[]{:S(2)}) collective-permute-start(f32[72,128]{1,0:T(8,128)S(1)} %get-tuple-element.30), channel_id=1, source_target_pairs={{0,2},{1,3},{2,0},{3,1},{4,6},{5,7},{6,4},{7,5},{8,10},{9,11},{10,... | collective-permute-start | bytes 110600 | tf_op jit(solution)/shard_map/ppermute | solution.py:352
  22.4 2.2 %collective-permute-start.4 = (f32[72,128]{1,0:T(8,128)S(1)}, f32[72,128]{1,0:T(8,128)S(1)}, u32[]{:S(2)}, u32[]{:S(2)}) collective-permute-start(f32[72,128]{1,0:T(8,128)S(1)} %get-tuple-element.31), channel_id=1, source_target_pairs={{0,4},{1,5},{2,6},{3,7},{4,0},{5,1},{6,2},{7,3},{8,12},{9,13},{10,... | collective-permute-start | bytes 110600 | tf_op jit(solution)/shard_map/ppermute | solution.py:352
  24.7 1.6 %collective-permute-start.5 = (f32[72,128]{1,0:T(8,128)S(1)}, f32[72,128]{1,0:T(8,128)S(1)}, u32[]{:S(2)}, u32[]{:S(2)}) collective-permute-start(f32[72,128]{1,0:T(8,128)S(1)} %get-tuple-element.32), channel_id=1, source_target_pairs={{0,6},{1,7},{2,4},{3,5},{4,2},{5,3},{6,0},{7,1},{8,14},{9,15},{10,... | collective-permute-start | bytes 110600 | tf_op jit(solution)/shard_map/ppermute | solution.py:352
  26.2 0.0 collective-permute-done.3.refs_1_
  26.2 2.2 %collective-permute-done.4.refs_2_ = f32[72,128]{1,0:T(8,128)S(1)} collective-permute-done((f32[72,128]{1,0:T(8,128)S(1)}, f32[72,128]{1,0:T(8,128)S(1)}, u32[]{:S(2)}, u32[]{:S(2)}) %collective-permute-start.4) | collective-permute-done | bytes 36896 | tf_op jit(solution)/shard_map/ppermute | solution.py:352
  28.4 2.0 %collective-permute-done.5.refs_3_ = f32[72,128]{1,0:T(8,128)S(1)} collective-permute-done((f32[72,128]{1,0:T(8,128)S(1)}, f32[72,128]{1,0:T(8,128)S(1)}, u32[]{:S(2)}, u32[]{:S(2)}) %collective-permute-start.5) | collective-permute-done | bytes 36896 | tf_op jit(solution)/shard_map/ppermute | solution.py:352
  30.4 0.7 %shard_map.90 = (f32[8,8,128]{2,1,0:T(8,128)}, f32[1,8,8]{2,1,0:T(8,128)}) custom-call(f32[72,128]{1,0:T(8,128)S(1)} %get-tuple-element.29.refs_0_, f32[72,128]{1,0:T(8,128)S(1)} %collective-permute-done.3.refs_1_, f32[72,128]{1,0:T(8,128)S(1)} %collective-permute-done.4.refs_2_, f32[72,128]{1,0:T(8,128)S(1)} %collective-permute-done.5.refs_3_, ...), custom_call_target="tpu_custom_call" | custom-call | tf_op jit(solution)/shard_map/pallas_call | solution.py:358
  (1 shorter events, 0.0 us)
Async XLA Ops:
  2.4 15.6 %all-to-all-start = ((f32[32,1,1152]{2,1,0:T(1,128)}), f32[32,1,1152]{2,1,0:T(1,128)S(1)}, u32[]{:S(2)}, u32[]{:S(2)}) async-start(f32[32,1,1152]{2,1,0:T(1,128)} %bitcast), calls=%async_computation | async-start | bytes 294912 | tf_op jit(solution)/shard_map/all_to_all | solution.py:319
  9.7 9.1 %collective-permute-start = (bf16[32,1024]{1,0:T(8,128)(2,1)S(1)}, bf16[32,1024]{1,0:T(8,128)(2,1)S(1)}, u32[]{:S(2)}, u32[]{:S(2)}) collective-permute-start(bf16[32,1024]{1,0:T(8,128)(2,1)S(1)} %get-tuple-element.24), channel_id=1, source_target_pairs={{0,8},{8,0},{16,24},{24,16},{1,9},{9,1},{17,25},{25,17},{2,10},{10... | collective-permute-start | bytes 196616 | tf_op jit(solution)/shard_map/ppermute | solution.py:324
  11.6 7.3 %collective-permute-start.1 = (bf16[32,1024]{1,0:T(8,128)(2,1)S(1)}, bf16[32,1024]{1,0:T(8,128)(2,1)S(1)}, u32[]{:S(2)}, u32[]{:S(2)}) collective-permute-start(bf16[32,1024]{1,0:T(8,128)(2,1)S(1)} %get-tuple-element.25), channel_id=1, source_target_pairs={{0,24},{8,16},{16,8},{24,0},{1,25},{9,17},{17,9},{25,1},{2,26},{10... | collective-permute-start | bytes 196616 | tf_op jit(solution)/shard_map/ppermute | solution.py:325
  20.2 1.5 %collective-permute-start.2 = (f32[4,72,128]{2,1,0:T(8,128)S(1)}, f32[4,72,128]{2,1,0:T(8,128)S(1)}, u32[]{:S(2)}, u32[]{:S(2)}) collective-permute-start(f32[4,72,128]{2,1,0:T(8,128)S(1)} %get-tuple-element.28), channel_id=1, source_target_pairs={{0,1},{1,0},{2,3},{3,2},{4,5},{5,4},{6,7},{7,6},{8,9},{9,8},{10,11... | collective-permute-start | bytes 442376 | tf_op jit(solution)/shard_map/ppermute | solution.py:352
  21.7 4.5 %collective-permute-start.3 = (f32[72,128]{1,0:T(8,128)S(1)}, f32[72,128]{1,0:T(8,128)S(1)}, u32[]{:S(2)}, u32[]{:S(2)}) collective-permute-start(f32[72,128]{1,0:T(8,128)S(1)} %get-tuple-element.30), channel_id=1, source_target_pairs={{0,2},{1,3},{2,0},{3,1},{4,6},{5,7},{6,4},{7,5},{8,10},{9,11},{10,... | collective-permute-start | bytes 110600 | tf_op jit(solution)/shard_map/ppermute | solution.py:352
  22.4 6.0 %collective-permute-start.4 = (f32[72,128]{1,0:T(8,128)S(1)}, f32[72,128]{1,0:T(8,128)S(1)}, u32[]{:S(2)}, u32[]{:S(2)}) collective-permute-start(f32[72,128]{1,0:T(8,128)S(1)} %get-tuple-element.31), channel_id=1, source_target_pairs={{0,4},{1,5},{2,6},{3,7},{4,0},{5,1},{6,2},{7,3},{8,12},{9,13},{10,... | collective-permute-start | bytes 110600 | tf_op jit(solution)/shard_map/ppermute | solution.py:352
  24.7 5.8 %collective-permute-start.5 = (f32[72,128]{1,0:T(8,128)S(1)}, f32[72,128]{1,0:T(8,128)S(1)}, u32[]{:S(2)}, u32[]{:S(2)}) collective-permute-start(f32[72,128]{1,0:T(8,128)S(1)} %get-tuple-element.32), channel_id=1, source_target_pairs={{0,6},{1,7},{2,4},{3,5},{4,2},{5,3},{6,0},{7,1},{8,14},{9,15},{10,... | collective-permute-start | bytes 110600 | tf_op jit(solution)/shard_map/ppermute | solution.py:352

commit v3 on v2

--- a/solution.py
+++ b/solution.py
@@ -58,20 +58,22 @@
     return iota((tiles, slots), 1).astype(F32) < column
 
 
-def first_kernel(
-    copies, value_hbm, cell_hbm, count_hbm, diff_hbm, ens_hbm, vertical_hbm, weights_hbm,
-    sent_ref, turned_ref, a_ref, b_ref, factors_ref, live_ref,
-    value_ref, cell_ref, count_ref, diff_ref, ens_ref, vertical_ref, weights_ref, wide, packet, tall, sems,
-):
-    pairs = (
-        (value_hbm, value_ref), (cell_hbm, cell_ref), (count_hbm, count_ref), (diff_hbm, diff_ref),
-        (ens_hbm, ens_ref), (vertical_hbm, vertical_ref), (weights_hbm, weights_ref),
-    )
-    moves = [pltpu.make_async_copy(x, y, sems.at[i]) for i, (x, y) in enumerate(pairs)]
+def copy_in(sources, targets, sems):
+    moves = [pltpu.make_async_copy(x, y, sems.at[i]) for i, (x, y) in enumerate(zip(sources, targets))]
     for move in moves:
         move.start()
+    return moves
+
+
+def packet_kernel(
+    copies, value_hbm, cell_hbm, count_hbm, diff_hbm, sent_ref, live_ref,
+    value_ref, cell_ref, count_ref, diff_ref, wide, packet, sems,
+):
+    moves = copy_in(
+        (value_hbm, cell_hbm, count_hbm, diff_hbm), (value_ref, cell_ref, count_ref, diff_ref), sems
+    )
     wide[...] = jnp.zeros_like(wide)
-    for move in moves[:4]:
+    for move in moves:
         move.wait()
     _, tiles, slots = value_ref.shape
     rows = diff_ref.shape[0]
@@ -91,9 +93,15 @@
     for i in range(copies):
         sent_ref[i * height : (i + 1) * height, :] = packet[...]
 
-    for move in moves[4:]:
+
+def member_kernel(
+    ens_hbm, vertical_hbm, weights_hbm, turned_ref, a_ref, b_ref, factors_ref,
+    ens_ref, vertical_ref, weights_ref, tall, sems,
+):
+    moves = copy_in((vertical_hbm, weights_hbm, ens_hbm), (vertical_ref, weights_ref, ens_ref), sems)
+    for move in moves:
         move.wait()
-    _, levels, _, columns = ens_ref.shape
+    _, levels, rows, columns = ens_ref.shape
     for t in range(columns // LANES):
         at = slice(t * LANES, (t + 1) * LANES)
         tall[t] = ens_ref[0, :, :, at].astype(F32).reshape(levels * rows, LANES)
@@ -176,7 +184,8 @@
     blocks = -(-tiles * GROUP // LANES)
     block = min(tiles, LANES // GROUP)
     columns = turned_ref.shape[1]
-    band, core = lax.axis_index("ty"), lax.rem(lax.axis_index("tx"), 2)
+    band, me = lax.axis_index("ty"), lax.axis_index("tx")
+    chip, core = me // 2, lax.rem(me, 2)
     even, last = lax.rem(band, 2) == 0, lax.axis_size("ty") - 1
     half, own = STEPS * levels, rows * levels
 
@@ -208,7 +217,7 @@
     chips = mine_ref.shape[0]
     for z in range(chips):
         for side, out in enumerate((mine_ref, other_ref)):
-            t = 2 * z + (core ^ side)
+            t = 2 * z + (core ^ side ^ (chip != z).astype(jnp.int32))
             mirror = 2 * (2 * z // block * block) + block - 1
             at = pl.ds(pl.multiple_of(t * LANES, LANES), LANES)
             parts = []
@@ -231,7 +240,7 @@
     for z in range(chips):
         for side, out in enumerate((mine_ref, other_ref)):
             out[z, own:, :] = jnp.zeros((out.shape[1] - own, LANES), F32)
-            place = 2 * z % block + (core ^ side)
+            place = 2 * z % block + (core ^ side ^ (chip != z).astype(jnp.int32))
             for b in range(blocks):
                 out[z, own + b : own + b + 1, :] = pick(turned[2 * z // block][b], place)
 
@@ -285,36 +294,40 @@
     half, own = STEPS * levels, rows * levels
     lanes = tiles // block * LANES
 
-    sent, turned, to_a, to_b, factors, live = call(
-        functools.partial(first_kernel, devices),
-        (
-            shape((devices * height, LANES), F32),
-            shape((own, columns), BF16),
-            shape((half, columns), BF16),
-            shape((half, columns), BF16),
-            shape((2 * BAND + 1, levels, LANES), F32),
-            shape((tiles, LANES), F32),
-        ),
-        [HBM] * 7,
+    def in_hbm(*arrays):
+        return [pltpu.with_memory_space_constraint(x, pltpu.HBM) for x in arrays]
+
+    sent, live = call(
+        functools.partial(packet_kernel, devices),
+        (shape((devices * height, LANES), F32), shape((tiles, LANES), F32)),
+        [HBM] * 4,
         [
             pltpu.VMEM(obs_value.shape, F32),
             pltpu.VMEM(obs_cell.shape, jnp.int32),
             pltpu.VMEM(obs_count.shape, jnp.int32),
             pltpu.VMEM(diffusivity.shape, F32),
+            pltpu.VMEM((2, tiles, LANES), F32),
+            pltpu.VMEM((height, LANES), F32),
+            pltpu.SemaphoreType.DMA((4,)),
+        ],
+    )(*in_hbm(obs_value, obs_cell, obs_count, diffusivity))
+    turned, to_a, to_b, factors = call(
+        member_kernel,
+        (
+            shape((own, columns), BF16),
+            shape((half, columns), BF16),
+            shape((half, columns), BF16),
+            shape((2 * BAND + 1, levels, LANES), F32),
+        ),
+        [HBM] * 3,
+        [
             pltpu.VMEM(ensemble.shape, BF16),
             pltpu.VMEM(vertical.shape, F32),
             pltpu.SMEM(weights.shape, F32),
-            pltpu.VMEM((2, tiles, LANES), F32),
-            pltpu.VMEM((height, LANES), F32),
             pltpu.VMEM((tiles, own, LANES), F32),
-            pltpu.SemaphoreType.DMA((7,)),
+            pltpu.SemaphoreType.DMA((3,)),
         ],
-    )(
-        *(
-            pltpu.with_memory_space_constraint(x, pltpu.HBM)
-            for x in (obs_value, obs_cell, obs_count, diffusivity, ensemble, vertical, weights)
-        )
-    )
+    )(*in_hbm(ensemble, vertical, weights))
 
     got = lax.all_to_all(
         sent.reshape(devices, 1, height * LANES), ("ty", "tx"), split_axis=0, concat_axis=0, tiled=True
@@ -354,7 +367,7 @@
     sums = call(
         pair_kernel, tuple(shape((chunk, LANES), F32) for _ in range(chips)), [VMEM] * 2, []
     )(mine, swap(other, 1))
-    sums = [sums[0]] + [swap(sums[far], 2 * far) for far in range(1, chips)]
+    sums = [sums[0]] + [swap(sums[far], 2 * far + 1) for far in range(1, chips)]
     return call(
         functools.partial(final_kernel, chips),
         (shape((levels, rows, LANES), F32), shape((1, tiles, slots), F32)),

time: 31.4 us -> 30.8 us (0.981)
  waiting for transfers between devices: 10.2 us -> 8.94 us
  Pallas kernels: 4.68 us -> 5.62 us
  starting transfers between devices: 15.6 us -> 15.2 us
    all_to_all x1, waiting for transfers between devices: 5.02 us -> 3.93 us  [shards(): lax.all_to_all(sent.reshape(devices, 1, height * LANES), ('ty', 'tx'), sp...]
    pallas_call x1 -> x2, Pallas kernels: 1.77 us -> 2.69 us  [the longest x1 1.6 us: shards(): call(functools.partial(packet_kernel, devices), (shape((devices * height,...]
    ppermute x4, starting transfers between devices: 4.97 us -> 4.63 us  [swap(): return lax.ppermute(x, 'tx', [(i, i ^ far) for i in range(tiles)])]
  transfers between devices with their start and end apart: 7 -> 7, of which waited for: 4 -> 4; matrix products, arithmetic and copies ran while one was open for 0% -> 0% of each run, Pallas kernels for 2% -> 6%
where the time goes in v3:
time: 30.8 us; the launch traced here: 30.5 us
  starting transfers between devices  15.2 us (49%)
  waiting for transfers between devices  8.94 us (29%)
  Pallas kernels  5.62 us (18%)
  between operations  0.68 us (2%)
    all_to_all x1, starting transfers between devices, shards(): lax.all_to_all(sent.reshape(devices, 1, height * LANES), ('ty', 'tx'), sp...  7.3 us
    ppermute x4, waiting for transfers between devices, swap(): return lax.ppermute(x, 'tx', [(i, i ^ far) for i in range(tiles)])  4.99 us
    ppermute x4, starting transfers between devices, swap(): return lax.ppermute(x, 'tx', [(i, i ^ far) for i in range(tiles)])  4.63 us
    all_to_all x1, waiting for transfers between devices, shards(): lax.all_to_all(sent.reshape(devices, 1, height * LANES), ('ty', 'tx'), sp...  3.93 us
    ppermute x1, starting transfers between devices, shards(): from_a = lax.ppermute(to_a, 'ty', pairs_a)  1.83 us
    pallas_call x1, Pallas kernels, shards(): call(functools.partial(packet_kernel, devices), (shape((devices * height,...  1.6 us
    ppermute x1, starting transfers between devices, shards(): from_b = lax.ppermute(to_b, 'ty', pairs_b)  1.46 us
    pallas_call x1, Pallas kernels, shards(): call(functools.partial(main_kernel, rows, levels), (shape((chips, chunk,...  1.42 us
  transfers between devices with their start and end apart: 7, of which 4 were waited for; matrix products, arithmetic and copies ran while one was open for 0% of the time, Pallas kernels for 6%

profile of v3, /device:TPU:0, one launch (start us, length us, event | category | flops | bytes accessed | tf_op | source)
XLA Modules:
  0.0 30.5 jit_solution(15177645806315746998)
XLA Ops:
  0.6 1.6 %shard_map.86 = (f32[288,128]{1,0:T(8,128)}, f32[8,128]{1,0:T(8,128)S(1)}) custom-call(f32[1,8,8]{2,1,0:T(8,128)} %value_hbm.1, s32[1,8,8]{2,1,0:T(8,128)} %cell_hbm.1, s32[1,8]{1,0:T(1,128)} %count_hbm.1, f32[8,128]{1,0:T(8,128)} %diff_hbm.1), custom_call_target="tpu_custom_call" | custom-call | tf_op jit(solution)/shard_map/pallas_call | solution.py:300
  2.2 7.3 %all-to-all-start = ((f32[32,1,1152]{2,1,0:T(1,128)}), f32[32,1,1152]{2,1,0:T(1,128)S(1)}, u32[]{:S(2)}, u32[]{:S(2)}) async-start(f32[32,1,1152]{2,1,0:T(1,128)} %bitcast), calls=%async_computation | async-start | bytes 294912 | tf_op jit(solution)/shard_map/all_to_all | solution.py:332
  9.6 1.1 %shard_map.88 = (bf16[64,1024]{1,0:T(8,128)(2,1)S(1)}, bf16[32,1024]{1,0:T(8,128)(2,1)S(1)}, bf16[32,1024]{1,0:T(8,128)(2,1)S(1)}, f32[5,8,128]{2,1,0:T(8,128)S(1)}) custom-call(bf16[1,8,8,1024]{3,2,1,0:T(8,128)(2,1)} %ens_hbm.1, f32[8,8]{1,0:T(8,128)} %vertical_hbm.1, f32[8]{0:T(128)} %weights_hbm.1), custom_call_target="tpu_custom_call" | custom-call | tf_op jit(solution)/shard_map/pallas_call | solution.py:314
  10.6 1.8 %collective-permute-start = (bf16[32,1024]{1,0:T(8,128)(2,1)S(1)}, bf16[32,1024]{1,0:T(8,128)(2,1)S(1)}, u32[]{:S(2)}, u32[]{:S(2)}) collective-permute-start(bf16[32,1024]{1,0:T(8,128)(2,1)S(1)} %get-tuple-element.24), channel_id=1, source_target_pairs={{0,8},{8,0},{16,24},{24,16},{1,9},{9,1},{17,25},{25,17},{2,10},{10... | collective-permute-start | bytes 196616 | tf_op jit(solution)/shard_map/ppermute | solution.py:337
  12.5 1.5 %collective-permute-start.1 = (bf16[32,1024]{1,0:T(8,128)(2,1)S(1)}, bf16[32,1024]{1,0:T(8,128)(2,1)S(1)}, u32[]{:S(2)}, u32[]{:S(2)}) collective-permute-start(bf16[32,1024]{1,0:T(8,128)(2,1)S(1)} %get-tuple-element.25), channel_id=1, source_target_pairs={{0,24},{8,16},{16,8},{24,0},{1,25},{9,17},{17,9},{25,1},{2,26},{10... | collective-permute-start | bytes 196616 | tf_op jit(solution)/shard_map/ppermute | solution.py:338
  13.9 3.9 %all-to-all-done = f32[32,1,1152]{2,1,0:T(1,128)S(1)} async-done(((f32[32,1,1152]{2,1,0:T(1,128)}), f32[32,1,1152]{2,1,0:T(1,128)S(1)}, u32[]{:S(2)}, u32[]{:S(2)}) %all-to-all-start) | async-done | bytes 147488 | tf_op jit(solution)/shard_map/all_to_all | solution.py:332
  17.9 0.8 %shard_map.87 = (f32[128,1024]{1,0:T(8,128)S(1)}, f32[16,1024]{1,0:T(8,128)S(1)}, bf16[8,128,128]{2,1,0:T(8,128)(2,1)S(1)}, f32[8,8,128]{2,1,0:T(8,128)S(1)}) custom-call(f32[288,128]{1,0:T(8,128)S(1)} %bitcast.2), custom_call_target="tpu_custom_call" | custom-call | tf_op jit(solution)/shard_map/pallas_call | solution.py:340
  18.6 0.0 collective-permute-done.a_ref
  18.6 0.0 collective-permute-done.1.b_ref
  18.7 1.4 %shard_map.89 = (f32[4,72,128]{2,1,0:T(8,128)S(1)}, f32[4,72,128]{2,1,0:T(8,128)S(1)}) custom-call(f32[128,1024]{1,0:T(8,128)S(1)} %get-tuple-element.19.field_ref, f32[16,1024]{1,0:T(8,128)S(1)} %get-tuple-element.20.d_all, bf16[8,128,128]{2,1,0:T(8,128)(2,1)S(1)} %get-tuple-element.21.hits_all, f32[8,8,128]{2,1,0:T(8,128)S(1)} %get-tuple-element.22.key_all, ...), custom_call_target="tpu_custom_call" | custom-call | tf_op jit(solution)/shard_map/pallas_call | solution.py:352
  20.1 0.5 %collective-permute-start.2 = (f32[4,72,128]{2,1,0:T(8,128)S(1)}, f32[4,72,128]{2,1,0:T(8,128)S(1)}, u32[]{:S(2)}, u32[]{:S(2)}) collective-permute-start(f32[4,72,128]{2,1,0:T(8,128)S(1)} %get-tuple-element.28), channel_id=1, source_target_pairs={{0,1},{1,0},{2,3},{3,2},{4,5},{5,4},{6,7},{7,6},{8,9},{9,8},{10,11... | collective-permute-start | bytes 442376 | tf_op jit(solution)/shard_map/ppermute | solution.py:365
  20.6 1.0 %collective-permute-done.2.got_ref = f32[4,72,128]{2,1,0:T(8,128)S(1)} collective-permute-done((f32[4,72,128]{2,1,0:T(8,128)S(1)}, f32[4,72,128]{2,1,0:T(8,128)S(1)}, u32[]{:S(2)}, u32[]{:S(2)}) %collective-permute-start.2) | collective-permute-done | bytes 147488 | tf_op jit(solution)/shard_map/ppermute | solution.py:365
  21.6 0.9 %collective-permute-start.3 = (f32[72,128]{1,0:T(8,128)S(1)}, f32[72,128]{1,0:T(8,128)S(1)}, u32[]{:S(2)}, u32[]{:S(2)}) collective-permute-start(f32[72,128]{1,0:T(8,128)S(1)} %get-tuple-element.30), channel_id=1, source_target_pairs={{0,3},{1,2},{2,1},{3,0},{4,7},{5,6},{6,5},{7,4},{8,11},{9,10},{10,... | collective-permute-start | bytes 110600 | tf_op jit(solution)/shard_map/ppermute | solution.py:365
  22.5 2.0 %collective-permute-start.4 = (f32[72,128]{1,0:T(8,128)S(1)}, f32[72,128]{1,0:T(8,128)S(1)}, u32[]{:S(2)}, u32[]{:S(2)}) collective-permute-start(f32[72,128]{1,0:T(8,128)S(1)} %get-tuple-element.31), channel_id=1, source_target_pairs={{0,5},{1,4},{2,7},{3,6},{4,1},{5,0},{6,3},{7,2},{8,13},{9,12},{10,... | collective-permute-start | bytes 110600 | tf_op jit(solution)/shard_map/ppermute | solution.py:365
  24.5 1.3 %collective-permute-start.5 = (f32[72,128]{1,0:T(8,128)S(1)}, f32[72,128]{1,0:T(8,128)S(1)}, u32[]{:S(2)}, u32[]{:S(2)}) collective-permute-start(f32[72,128]{1,0:T(8,128)S(1)} %get-tuple-element.32), channel_id=1, source_target_pairs={{0,7},{1,6},{2,5},{3,4},{4,3},{5,2},{6,1},{7,0},{8,15},{9,14},{10,... | collective-permute-start | bytes 110600 | tf_op jit(solution)/shard_map/ppermute | solution.py:365
  25.7 0.0 collective-permute-done.3.refs_1_
  25.7 1.0 %collective-permute-done.4.refs_2_ = f32[72,128]{1,0:T(8,128)S(1)} collective-permute-done((f32[72,128]{1,0:T(8,128)S(1)}, f32[72,128]{1,0:T(8,128)S(1)}, u32[]{:S(2)}, u32[]{:S(2)}) %collective-permute-start.4) | collective-permute-done | bytes 36896 | tf_op jit(solution)/shard_map/ppermute | solution.py:365
  26.8 3.0 %collective-permute-done.5.refs_3_ = f32[72,128]{1,0:T(8,128)S(1)} collective-permute-done((f32[72,128]{1,0:T(8,128)S(1)}, f32[72,128]{1,0:T(8,128)S(1)}, u32[]{:S(2)}, u32[]{:S(2)}) %collective-permute-start.5) | collective-permute-done | bytes 36896 | tf_op jit(solution)/shard_map/ppermute | solution.py:365
  29.7 0.7 %shard_map.91 = (f32[8,8,128]{2,1,0:T(8,128)}, f32[1,8,8]{2,1,0:T(8,128)}) custom-call(f32[72,128]{1,0:T(8,128)S(1)} %get-tuple-element.29.refs_0_, f32[72,128]{1,0:T(8,128)S(1)} %collective-permute-done.3.refs_1_, f32[72,128]{1,0:T(8,128)S(1)} %collective-permute-done.4.refs_2_, f32[72,128]{1,0:T(8,128)S(1)} %collective-permute-done.5.refs_3_, ...), custom_call_target="tpu_custom_call" | custom-call | tf_op jit(solution)/shard_map/pallas_call | solution.py:371
  (1 shorter events, 0.0 us)
Async XLA Ops:
  2.2 15.6 %all-to-all-start = ((f32[32,1,1152]{2,1,0:T(1,128)}), f32[32,1,1152]{2,1,0:T(1,128)S(1)}, u32[]{:S(2)}, u32[]{:S(2)}) async-start(f32[32,1,1152]{2,1,0:T(1,128)} %bitcast), calls=%async_computation | async-start | bytes 294912 | tf_op jit(solution)/shard_map/all_to_all | solution.py:332
  10.6 8.0 %collective-permute-start = (bf16[32,1024]{1,0:T(8,128)(2,1)S(1)}, bf16[32,1024]{1,0:T(8,128)(2,1)S(1)}, u32[]{:S(2)}, u32[]{:S(2)}) collective-permute-start(bf16[32,1024]{1,0:T(8,128)(2,1)S(1)} %get-tuple-element.24), channel_id=1, source_target_pairs={{0,8},{8,0},{16,24},{24,16},{1,9},{9,1},{17,25},{25,17},{2,10},{10... | collective-permute-start | bytes 196616 | tf_op jit(solution)/shard_map/ppermute | solution.py:337
  12.5 6.2 %collective-permute-start.1 = (bf16[32,1024]{1,0:T(8,128)(2,1)S(1)}, bf16[32,1024]{1,0:T(8,128)(2,1)S(1)}, u32[]{:S(2)}, u32[]{:S(2)}) collective-permute-start(bf16[32,1024]{1,0:T(8,128)(2,1)S(1)} %get-tuple-element.25), channel_id=1, source_target_pairs={{0,24},{8,16},{16,8},{24,0},{1,25},{9,17},{17,9},{25,1},{2,26},{10... | collective-permute-start | bytes 196616 | tf_op jit(solution)/shard_map/ppermute | solution.py:338
  20.1 1.5 %collective-permute-start.2 = (f32[4,72,128]{2,1,0:T(8,128)S(1)}, f32[4,72,128]{2,1,0:T(8,128)S(1)}, u32[]{:S(2)}, u32[]{:S(2)}) collective-permute-start(f32[4,72,128]{2,1,0:T(8,128)S(1)} %get-tuple-element.28), channel_id=1, source_target_pairs={{0,1},{1,0},{2,3},{3,2},{4,5},{5,4},{6,7},{7,6},{8,9},{9,8},{10,11... | collective-permute-start | bytes 442376 | tf_op jit(solution)/shard_map/ppermute | solution.py:365
  21.6 4.1 %collective-permute-start.3 = (f32[72,128]{1,0:T(8,128)S(1)}, f32[72,128]{1,0:T(8,128)S(1)}, u32[]{:S(2)}, u32[]{:S(2)}) collective-permute-start(f32[72,128]{1,0:T(8,128)S(1)} %get-tuple-element.30), channel_id=1, source_target_pairs={{0,3},{1,2},{2,1},{3,0},{4,7},{5,6},{6,5},{7,4},{8,11},{9,10},{10,... | collective-permute-start | bytes 110600 | tf_op jit(solution)/shard_map/ppermute | solution.py:365
  22.5 4.3 %collective-permute-start.4 = (f32[72,128]{1,0:T(8,128)S(1)}, f32[72,128]{1,0:T(8,128)S(1)}, u32[]{:S(2)}, u32[]{:S(2)}) collective-permute-start(f32[72,128]{1,0:T(8,128)S(1)} %get-tuple-element.31), channel_id=1, source_target_pairs={{0,5},{1,4},{2,7},{3,6},{4,1},{5,0},{6,3},{7,2},{8,13},{9,12},{10,... | collective-permute-start | bytes 110600 | tf_op jit(solution)/shard_map/ppermute | solution.py:365
  24.5 5.2 %collective-permute-start.5 = (f32[72,128]{1,0:T(8,128)S(1)}, f32[72,128]{1,0:T(8,128)S(1)}, u32[]{:S(2)}, u32[]{:S(2)}) collective-permute-start(f32[72,128]{1,0:T(8,128)S(1)} %get-tuple-element.32), channel_id=1, source_target_pairs={{0,7},{1,6},{2,5},{3,4},{4,3},{5,2},{6,1},{7,0},{8,15},{9,14},{10,... | collective-permute-start | bytes 110600 | tf_op jit(solution)/shard_map/ppermute | solution.py:365

commit v4 on v2

v4 whole, which is shorter than its diff:
```python
import functools

import jax
import jax.numpy as jnp
from jax import lax
from jax.experimental import pallas as pl
from jax.experimental.pallas import tpu as pltpu
from jax.sharding import PartitionSpec as P

STEPS = 4
BAND = 2
LANES = 128
GROUP = 8
F32, BF16 = jnp.float32, jnp.bfloat16
VMEM = pl.BlockSpec(memory_space=pltpu.VMEM)
HBM = pl.BlockSpec(memory_space=pltpu.HBM)


def round_up(n, m):
    return -(-n // m) * m


def log2(n):
    assert n & (n - 1) == 0
    return n.bit_length() - 1


def iota(shape, axis):
    return lax.broadcasted_iota(jnp.int32, shape, axis)


def pieces(x):
    high = x.astype(BF16).astype(F32)
    rest = x - high
    middle = rest.astype(BF16).astype(F32)
    return high, middle, rest - middle


def stagger(x):
    return pltpu.roll(x, 0, 1, stride=GROUP, stride_axis=0)


def pick(x, place):
    if isinstance(place, int):
        shift = (-GROUP * place) % LANES
    else:
        shift = lax.rem(LANES - GROUP * place, LANES)
    rolled = pltpu.roll(x, shift, 1)
    own = iota(x.shape, 1) // GROUP == iota(x.shape, 0)
    return jnp.sum(jnp.where(own, rolled, 0.0), axis=0, keepdims=True)


def live_mask(count_ref, slots):
    tiles = count_ref.shape[1]
    count = jnp.broadcast_to(count_ref[...].astype(F32), (tiles, tiles))
    diagonal = iota((tiles, tiles), 0) == iota((tiles, tiles), 1)
    column = jnp.sum(jnp.where(diagonal, count, 0.0), axis=1, keepdims=True)
    return iota((tiles, slots), 1).astype(F32) < column


def copy_in(sources, targets, sems):
    moves = [pltpu.make_async_copy(x, y, sems.at[i]) for i, (x, y) in enumerate(zip(sources, targets))]
    for move in moves:
        move.start()
    return moves


def first_kernel(
    value_hbm, cell_hbm, count_hbm, diff_hbm, ens_hbm, vertical_hbm, weights_hbm,
    packet, turned_ref, a_ref, b_ref, factors_ref, live_ref,
    value_ref, cell_ref, count_ref, diff_ref, ens_ref, vertical_ref, weights_ref, wide, part, tall, sems,
):
    moves = copy_in(
        (value_hbm, cell_hbm, count_hbm, diff_hbm, ens_hbm, vertical_hbm, weights_hbm),
        (value_ref, cell_ref, count_ref, diff_ref, ens_ref, vertical_ref, weights_ref),
        sems,
    )
    wide[...] = jnp.zeros_like(wide)
    for move in moves[:4]:
        move.wait()
    _, tiles, slots = value_ref.shape
    rows = diff_ref.shape[0]
    block = min(tiles, LANES // GROUP)
    live = live_mask(count_ref, slots)
    wide[0, :, 0:slots] = jnp.where(live, value_ref[0], 0.0)
    wide[1, :, 0:slots] = cell_ref[0].astype(F32)
    live_ref[...] = jnp.zeros_like(live_ref)
    live_ref[:, 0:slots] = jnp.where(live, 1.0, 0.0)
    packet[0:rows, :] = diff_ref[...]
    lines = [pick(stagger(wide[q, b : b + block, :]), 0) for q in range(2) for b in range(0, tiles, block)]
    if block * GROUP < LANES:
        lines = [lines[0] + pltpu.roll(lines[1], block * GROUP, 1)]
    packet[rows:, :] = jnp.zeros((packet.shape[0] - rows, LANES), F32)
    for i, line in enumerate(lines):
        packet[rows + i : rows + i + 1, :] = line
    deep, levels = STEPS - 1, ens_ref.shape[1]
    half = STEPS * levels
    even = lax.rem(lax.axis_index("ty"), 2) == 0
    top, low = diff_ref[...], pltpu.roll(diff_ref[...], deep, 0)
    for out, chosen in ((a_ref, jnp.where(even, low, top)), (b_ref, jnp.where(even, top, low))):
        part[...] = chosen
        for i, line in enumerate(lines):
            part[deep + i : deep + i + 1, :] = line
        split = jnp.concatenate([*pieces(part[...]), jnp.zeros((rows, LANES), F32)], axis=0)
        out[tiles * half :, :] = split.astype(BF16)

    for move in moves[4:]:
        move.wait()
    off_a, off_b = jnp.where(even, half, 0), jnp.where(even, 0, half)
    for t in range(tiles):
        at = slice(t * LANES, (t + 1) * LANES)
        tall[t] = ens_ref[0, :, :, at].astype(F32).reshape(levels * rows, LANES)
        for r in range(0, rows, 2):
            both = [tall[t, pl.ds(r + i, levels, stride=rows), :] for i in range(2)]
            turned_ref[t, r * levels : (r + 2) * levels, :] = jnp.concatenate(both, axis=0).astype(BF16)
        a_ref[t * half : (t + 1) * half, :] = turned_ref[t, pl.ds(pl.multiple_of(off_a, half), half), :]
        b_ref[t * half : (t + 1) * half, :] = turned_ref[t, pl.ds(pl.multiple_of(off_b, half), half), :]
    vertical = vertical_ref[...] * weights_ref[lax.axis_index("tx")]
    gap = iota((levels, levels), 1) - iota((levels, levels), 0)
    for i in range(2 * BAND + 1):
        factor = jnp.sum(jnp.where(gap == i - BAND, vertical, 0.0), axis=1, keepdims=True)
        factors_ref[i] = jnp.broadcast_to(factor, (levels, LANES))


def join_kernel(size, at, packet_ref, a_ref, b_ref, out_ref):
    band, last = lax.axis_index("ty"), lax.axis_size("ty") - 1
    even = lax.rem(band, 2) == 0
    own, halo = size
    got = [ref[at:, :].astype(F32) for ref in (a_ref, b_ref)]
    step = got[0].shape[0] // 4
    got_a, got_b = (x[0:step] + x[step : 2 * step] + x[2 * step : 3 * step] for x in got)
    above = jnp.where(band == 0, 0.0, jnp.where(even, got_b, got_a))
    below = jnp.where(band == last, 0.0, jnp.where(even, got_a, got_b))
    out_ref[0:own, :] = packet_ref[0:own, :]
    out_ref[own : own + halo, :] = above[0:halo]
    out_ref[own + halo : own + 2 * halo, :] = below[0:halo]
    rest = out_ref.shape[0] - own - 2 * halo
    if rest:
        out_ref[own + 2 * halo :, :] = jnp.zeros((rest, LANES), F32)


def lines_of(staggered, place, tiles):
    size = staggered[0][0].shape[0]
    groups = LANES // GROUP
    return jnp.concatenate([pick(part, place % groups) for part in staggered[place // groups]], axis=1)


def spread(line_value, line_key, hits, count, first):
    key = line_key - first
    on = iota((count, line_key.shape[1]), 0).astype(F32) == key
    stacked = jnp.concatenate([jnp.where(on, piece, 0.0) for piece in pieces(line_value)], axis=0)
    found = lax.dot_general(
        stacked.astype(BF16), hits, (((1,), (1,)), ((), ())), preferred_element_type=F32
    )
    return found[0:count] + found[count : 2 * count] + found[2 * count :]


def hits_of(line_column):
    shape = (LANES, line_column.shape[1])
    return jnp.where(iota(shape, 0).astype(F32) == line_column, 1.0, 0.0).astype(BF16)


def fill(lines, rows, levels, base, count, write):
    tiles = lines[0].shape[0]
    block = min(tiles, LANES // GROUP)
    values, keys, columns = [], [], []
    for x in lines:
        cell = x.astype(jnp.int32)
        flat = lax.shift_right_logical(cell, log2(LANES))
        key = (flat & (rows - 1)) * levels + lax.shift_right_logical(flat, log2(rows))
        for out, part in ((values, x), (keys, key.astype(F32)), (columns, (cell & (LANES - 1)).astype(F32))):
            out.append([stagger(part[q : q + block]) for q in range(0, tiles, block)])
    for t in range(tiles):
        value = lines_of(values, t, tiles)
        key, column = lines_of(keys, tiles + t, tiles), lines_of(columns, tiles + t, tiles)
        hits = hits_of(column)
        write(t, spread(value, key, hits, count, float(base)), hits, key)


def main_kernel(
    near, rows, levels, lines, *refs,
):
    got, refs = refs[:near], refs[near:]
    turned_ref, a_ref, b_ref, factors_ref, mine_ref, other_ref = refs[:6]
    packs, member, d_all, hits_all, key_all, first, second, back = refs[6:]
    tiles = packs.shape[0]
    blocks = -(-tiles * GROUP // LANES)
    block = min(tiles, LANES // GROUP)
    columns = tiles * LANES
    band, me = lax.axis_index("ty"), lax.axis_index("tx")
    chip, core = me // 2, lax.rem(me, 2)
    even = lax.rem(band, 2) == 0
    half, own, deep = STEPS * levels, rows * levels, STEPS - 1

    own_rows, halo_rows = rows + lines, deep + lines
    for far, ref in enumerate(got):
        for side in range(2):
            packs[2 * (chip ^ far) + (core ^ side ^ (far > 0))] = ref[side]

    for t in range(tiles):
        at = slice(t * LANES, (t + 1) * LANES)
        member[half : half + own, at] = turned_ref[t].astype(F32)
        got_a, got_b = (ref[t * half : (t + 1) * half, :].astype(F32) for ref in (a_ref, b_ref))
        member[0:half, at] = jnp.where(even, got_b, got_a)
        member[half + own :, at] = jnp.where(even, got_a, got_b)
    sides = (
        (half, own, 0, 0, rows, STEPS),
        (0, half, own - half, own_rows, deep, 1),
        (half + own, half, 0, own_rows + halo_rows, deep, STEPS + rows),
    )
    for side, (begin, count, base, at_row, d_count, d_begin) in enumerate(sides):
        found = [packs[:, at_row + d_count + i, :] for i in range(lines)]

        def write(t, field, hits, key, side=side, begin=begin, count=count, at_row=at_row, d_count=d_count, d_begin=d_begin):
            at = slice(t * LANES, (t + 1) * LANES)
            d_all[d_begin : d_begin + d_count, at] = packs[t, at_row : at_row + d_count, :]
            first[begin : begin + count, at] = field * member[begin : begin + count, at]
            if side == 0:
                hits_all[t] = hits
                key_all[t] = jnp.broadcast_to(key, (8, key.shape[1]))

        fill(found, rows, levels, base, count, write)

    source, target = first, second
    left_end = iota((levels, columns), 1) == 0
    right_end = iota((levels, columns), 1) == columns - 1
    for step in range(STEPS):
        for r in range(step + 1, 2 * STEPS + rows - 1 - step):
            mid = source[r * levels : (r + 1) * levels, :]
            beside = (
                source[(r - 1) * levels : r * levels, :]
                + source[(r + 1) * levels : (r + 2) * levels, :]
                + jnp.where(left_end, 0.0, pltpu.roll(mid, 1, 1))
                + jnp.where(right_end, 0.0, pltpu.roll(mid, columns - 1, 1))
            )
            d = jnp.broadcast_to(d_all[r : r + 1, :], (levels, columns))
            target[r * levels : (r + 1) * levels, :] = mid + d * (beside - 4.0 * mid)
        source, target = target, source

    factors = [(i - BAND, factors_ref[i]) for i in range(2 * BAND + 1)]
    chips = mine_ref.shape[0]
    for z in range(chips):
        for side, out in enumerate((mine_ref, other_ref)):
            t = 2 * z + (core ^ side ^ (chip != z).astype(jnp.int32))
            mirror = 2 * (2 * z // block * block) + block - 1
            at = pl.ds(pl.multiple_of(t * LANES, LANES), LANES)
            parts = []
            for r in range(rows):
                x = source[half + r * levels : half + (r + 1) * levels, at]
                mixed = sum(f * (pltpu.roll(x, -o % levels, 0) if o else x) for o, f in factors)
                part = mixed * member[half + r * levels : half + (r + 1) * levels, at]
                out[z, r * levels : (r + 1) * levels, :] = part
                parts.append(part)
            stacked = jnp.concatenate(pieces(jnp.concatenate(parts, axis=0)), axis=0).astype(BF16)
            found = jnp.dot(stacked, hits_all[t], preferred_element_type=F32)
            found = found[0:own] + found[own : 2 * own] + found[2 * own :]
            on = iota(found.shape, 0).astype(F32) == key_all[t][0:1]
            line = jnp.sum(jnp.where(on, found, 0.0), axis=0, keepdims=True)
            for q in range(tiles // block):
                back[q, pl.ds(mirror - t, 1), :] = line[:, q * LANES : (q + 1) * LANES]
    turned = [
        [stagger(back[q, b * block : (b + 1) * block, :]) for b in range(blocks)] for q in range(tiles // block)
    ]
    for z in range(chips):
        for side, out in enumerate((mine_ref, other_ref)):
            out[z, own:, :] = jnp.zeros((out.shape[1] - own, LANES), F32)
            place = 2 * z % block + (core ^ side ^ (chip != z).astype(jnp.int32))
            for b in range(blocks):
                out[z, own + b : own + b + 1, :] = pick(turned[2 * z // block][b], place)


def pair_kernel(mine_ref, got_ref, *outs):
    chip = lax.axis_index("tx") // 2
    for far, out in enumerate(outs):
        out[...] = mine_ref[chip ^ far] + got_ref[chip ^ far]


def final_kernel(near, *refs):
    got, (live_ref, inc_ref, proj_ref, total, wide) = refs[:near], refs[near:]
    levels, rows, _ = inc_ref.shape
    _, tiles, slots = proj_ref.shape
    block = min(tiles, LANES // GROUP)
    sums = got[0][...]
    for ref in got[1:]:
        sums = sums + ref[...]
    total[...] = sums
    for level in range(levels):
        inc_ref[level] = total[pl.ds(level, rows, stride=levels), :]
    for b in range(tiles // block):
        line = jnp.broadcast_to(total[rows * levels + b : rows * levels + b + 1, :], (block, LANES))
        line = pltpu.roll(line, (LANES - GROUP * (block - 1)) % LANES, 1)
        wide[b * block : (b + 1) * block, :] = stagger(line)
    proj_ref[0] = jnp.where(live_ref[:, 0:slots] > 0.0, wide[:, 0:slots], 0.0)


def call(kernel, out_shape, ins, scratch, flops=0, moved=0):
    return pl.pallas_call(
        kernel,
        out_shape=out_shape,
        in_specs=ins,
        out_specs=jax.tree.map(lambda _: VMEM, out_shape),
        scratch_shapes=scratch,
        compiler_params=pltpu.CompilerParams(vmem_limit_bytes=48 << 20),
        cost_estimate=pl.CostEstimate(flops=flops, bytes_accessed=moved, transcendentals=0),
    )


def shards(ensemble, diffusivity, vertical, weights, obs_value, obs_cell, obs_count):
    _, levels, rows, columns = ensemble.shape
    tiles, slots = obs_value.shape[1:]
    chips = tiles // 2
    bands = lax.axis_size("ty")
    assert diffusivity.shape == (rows, LANES) and slots == GROUP and rows == 2 * STEPS
    block = min(tiles, LANES // GROUP)
    shape = jax.ShapeDtypeStruct
    lines = -(-2 * tiles * GROUP // LANES)
    half, own = STEPS * levels, rows * levels
    own_rows, halo_rows = rows + lines, STEPS - 1 + lines
    height, joined = round_up(own_rows, 8), round_up(own_rows + 2 * halo_rows, 8)
    lanes = tiles // block * LANES
    assert halo_rows <= rows

    def in_hbm(*arrays):
        return [pltpu.with_memory_space_constraint(x, pltpu.HBM) for x in arrays]

    def swap(x, far):
        return lax.ppermute(x, "tx", [(i, i ^ far) for i in range(tiles)])

    def swap_bands(x, low):
        mate = [i ^ 1 if low else i + 1 if i % 2 else i - 1 for i in range(bands)]
        pairs = [
            (i * tiles + k, mate[i] * tiles + k if 0 <= mate[i] < bands else i * tiles + (k ^ 1))
            for i in range(bands)
            for k in range(tiles)
        ]
        return lax.ppermute(x, ("ty", "tx"), pairs)

    sent = shape((tiles * half + 4 * rows, LANES), BF16)
    packet, turned, to_a, to_b, factors, live = call(
        first_kernel,
        (
            shape((height, LANES), F32),
            shape((tiles, own, LANES), BF16),
            sent,
            sent,
            shape((2 * BAND + 1, levels, LANES), F32),
            shape((tiles, LANES), F32),
        ),
        [HBM] * 7,
        [
            pltpu.VMEM(obs_value.shape, F32),
            pltpu.VMEM(obs_cell.shape, jnp.int32),
            pltpu.VMEM(obs_count.shape, jnp.int32),
            pltpu.VMEM(diffusivity.shape, F32),
            pltpu.VMEM(ensemble.shape, BF16),
            pltpu.VMEM(vertical.shape, F32),
            pltpu.SMEM(weights.shape, F32),
            pltpu.VMEM((2, tiles, LANES), F32),
            pltpu.VMEM((rows, LANES), F32),
            pltpu.VMEM((tiles, own, LANES), F32),
            pltpu.SemaphoreType.DMA((7,)),
        ],
    )(*in_hbm(obs_value, obs_cell, obs_count, diffusivity, ensemble, vertical, weights))
    from_a, from_b = swap_bands(to_a, True), swap_bands(to_b, False)
    mine = call(
        functools.partial(join_kernel, (own_rows, halo_rows), tiles * half),
        shape((joined, LANES), F32),
        [VMEM] * 3,
        [],
    )(packet, from_a, from_b)
    pair = jnp.stack([mine, swap(mine, 1)])
    row = [pair] + [swap(pair, 2 * far + 1) for far in range(1, chips)]

    chunk = own + 8
    mine, other = call(
        functools.partial(main_kernel, chips, rows, levels, lines),
        (shape((chips, chunk, LANES), F32), shape((chips, chunk, LANES), F32)),
        [VMEM] * (chips + 4),
        [
            pltpu.VMEM((tiles, joined, LANES), F32),
            pltpu.VMEM((2 * half + own, columns), F32),
            pltpu.VMEM((2 * STEPS + rows, columns), F32),
            pltpu.VMEM((tiles, LANES, lanes), BF16),
            pltpu.VMEM((tiles, 8, lanes), F32),
            pltpu.VMEM((2 * half + own, columns), F32),
            pltpu.VMEM((2 * half + own, columns), F32),
            pltpu.VMEM((tiles // block, tiles, LANES), F32),
        ],
    )(*row, turned, from_a, from_b, factors)

    sums = call(
        pair_kernel, tuple(shape((chunk, LANES), F32) for _ in range(chips)), [VMEM] * 2, []
    )(mine, swap(other, 1))
    sums = [sums[0]] + [swap(sums[far], 2 * far + 1) for far in range(1, chips)]
    return call(
        functools.partial(final_kernel, chips),
        (shape((levels, rows, LANES), F32), shape((1, tiles, slots), F32)),
        [VMEM] * (chips + 1),
        [pltpu.VMEM((chunk, LANES), F32), pltpu.VMEM((tiles, LANES), F32)],
    )(*sums, live)


def solution(mesh):
    placed = (
        P("tx", None, "ty", None),
        P("ty", "tx"),
        P(),
        P(),
        P(("ty", "tx"), None, None),
        P(("ty", "tx"), None, None),
        P(("ty", "tx"), None),
    )
    return jax.shard_map(
        shards,
        mesh=mesh,
        in_specs=placed,
        out_specs=(P(None, "ty", "tx"), P(("ty", "tx"), None, None)),
        check_vma=False,
    )
```

time: 31.4 us -> 29.3 us (0.933)
  the two profiles are of different devices: /device:TPU:0 before, /device:TPU:5 now
where the time goes in v4:
time: 29.3 us; the launch traced here: 29.1 us
  waiting for transfers between devices  13 us (44%)
  starting transfers between devices  11.7 us (40%)
  Pallas kernels  3.73 us (13%)
  between operations  0.66 us (2%)
    ppermute x8, starting transfers between devices, swap(): return lax.ppermute(x, 'tx', [(i, i ^ far) for i in range(tiles)])  10.4 us
    ppermute x8, waiting for transfers between devices, swap(): return lax.ppermute(x, 'tx', [(i, i ^ far) for i in range(tiles)])  8.96 us
    ppermute x2, waiting for transfers between devices, swap_bands(): return lax.ppermute(x, ('ty', 'tx'), pairs)  4.08 us
    pallas_call x1, Pallas kernels, shards(): call(functools.partial(main_kernel, chips, rows, levels, lines), (shape((...  1.83 us
    ppermute x2, starting transfers between devices, swap_bands(): return lax.ppermute(x, ('ty', 'tx'), pairs)  1.3 us
    pallas_call x1, Pallas kernels, shards(): call(first_kernel, (shape((height, LANES), F32), shape((tiles, own, LANES...  1.14 us
    pallas_call x1, Pallas kernels, shards(): call(functools.partial(final_kernel, chips), (shape((levels, rows, LANES)...  0.74 us
  transfers between devices with their start and end apart: 10, of which 8 were waited for; matrix products, arithmetic and copies ran while one was open for 0% of the time, Pallas kernels for 0%

profile of v4, /device:TPU:5, one launch (start us, length us, event | category | flops | bytes accessed | tf_op | source)
XLA Modules:
  0.0 29.1 jit_solution(4082013344743702736)
XLA Ops:
  0.6 1.1 %shard_map.86 = (f32[16,128]{1,0:T(8,128)S(1)}, bf16[8,64,128]{2,1,0:T(8,128)(2,1)S(1)}, bf16[288,128]{1,0:T(8,128)(2,1)S(1)}, bf16[288,128]{1,0:T(8,128)(2,1)S(...) custom-call(f32[1,8,8]{2,1,0:T(8,128)} %value_hbm.1, s32[1,8,8]{2,1,0:T(8,128)} %cell_hbm.1, s32[1,8]{1,0:T(1,128)} %count_hbm.1, ...), custom_call_target="tpu_custom_call" | custom-call | tf_op jit(solution)/shard_map/pallas_call | solution.py:339
  1.8 1.3 %collective-permute-start = (bf16[288,128]{1,0:T(8,128)(2,1)S(1)}, bf16[288,128]{1,0:T(8,128)(2,1)S(1)}, u32[]{:S(2)}, u32[]{:S(2)}) collective-permute-start(bf16[288,128]{1,0:T(8,128)(2,1)S(1)} %get-tuple-element.15), channel_id=1, source_target_pairs={{0,8},{1,9},{2,10},{3,11},{4,12},{5,13},{6,14},{7,15},{8,0},{9,1},... | collective-permute-start | bytes 221192 | tf_op jit(solution)/shard_map/ppermute | solution.py:336
  3.1 0.0 collective-permute-start.1
  3.1 2.0 %collective-permute-done.a_ref.refs_5_ = bf16[288,128]{1,0:T(8,128)(2,1)S(1)} collective-permute-done((bf16[288,128]{1,0:T(8,128)(2,1)S(1)}, bf16[288,128]{1,0:T(8,128)(2,1)S(1)}, u32[]{:S(2)}, u32[]{:S(2)}) %collective-permute-start) | collective-permute-done | bytes 73760 | tf_op jit(solution)/shard_map/ppermute | solution.py:336
  5.0 2.1 %collective-permute-done.1.b_ref.refs_6_ = bf16[288,128]{1,0:T(8,128)(2,1)S(1)} collective-permute-done((bf16[288,128]{1,0:T(8,128)(2,1)S(1)}, bf16[288,128]{1,0:T(8,128)(2,1)S(1)}, u32[]{:S(2)}, u32[]{:S(2)}) %collective-permute-start.1) | collective-permute-done | bytes 73760 | tf_op jit(solution)/shard_map/ppermute | solution.py:336
  7.2 2.2 %collective-permute-start.2 = (f32[24,128]{1,0:T(8,128)S(1)}, f32[24,128]{1,0:T(8,128)S(1)}, u32[]{:S(2)}, u32[]{:S(2)}) collective-permute-start(f32[24,128]{1,0:T(8,128)S(1)} %shard_map.87), channel_id=1, source_target_pairs={{0,1},{1,0},{2,3},{3,2},{4,5},{5,4},{6,7},{7,6},{8,9},{9,8},{10,11... | collective-permute-start | bytes 36872 | tf_op jit(solution)/shard_map/ppermute | solution.py:327
  9.3 0.8 %collective-permute-done.2 = f32[24,128]{1,0:T(8,128)S(1)} collective-permute-done((f32[24,128]{1,0:T(8,128)S(1)}, f32[24,128]{1,0:T(8,128)S(1)}, u32[]{:S(2)}, u32[]{:S(2)}) %collective-permute-start.2) | collective-permute-done | bytes 12320 | tf_op jit(solution)/shard_map/ppermute | solution.py:327
  10.2 3.6 %collective-permute-start.5 = (f32[2,24,128]{2,1,0:T(8,128)S(1)}, f32[2,24,128]{2,1,0:T(8,128)S(1)}, u32[]{:S(2)}, u32[]{:S(2)}) collective-permute-start(f32[2,24,128]{2,1,0:T(8,128)S(1)} %pad_maximum_fusion.refs_0_), channel_id=1, source_target_pairs={{0,7},{1,6},{2,5},{3,4},{4,3},{5,2},{6,1},{7,0},{8,15},{9,14},{10,... | collective-permute-start | bytes 73736 | tf_op jit(solution)/shard_map/ppermute | solution.py:327
  13.7 0.0 collective-permute-start.4
  13.7 0.5 %collective-permute-start.3 = (f32[2,24,128]{2,1,0:T(8,128)S(1)}, f32[2,24,128]{2,1,0:T(8,128)S(1)}, u32[]{:S(2)}, u32[]{:S(2)}) collective-permute-start(f32[2,24,128]{2,1,0:T(8,128)S(1)} %pad_maximum_fusion.refs_0_), channel_id=1, source_target_pairs={{0,3},{1,2},{2,1},{3,0},{4,7},{5,6},{6,5},{7,4},{8,11},{9,10},{10,... | collective-permute-start | bytes 73736 | tf_op jit(solution)/shard_map/ppermute | solution.py:327
  14.2 1.0 %collective-permute-done.5.refs_3_ = f32[2,24,128]{2,1,0:T(8,128)S(1)} collective-permute-done((f32[2,24,128]{2,1,0:T(8,128)S(1)}, f32[2,24,128]{2,1,0:T(8,128)S(1)}, u32[]{:S(2)}, u32[]{:S(2)}) %collective-permute-start.5) | collective-permute-done | bytes 24608 | tf_op jit(solution)/shard_map/ppermute | solution.py:327
  15.2 2.6 %collective-permute-done.4.refs_2_ = f32[2,24,128]{2,1,0:T(8,128)S(1)} collective-permute-done((f32[2,24,128]{2,1,0:T(8,128)S(1)}, f32[2,24,128]{2,1,0:T(8,128)S(1)}, u32[]{:S(2)}, u32[]{:S(2)}) %collective-permute-start.4) | collective-permute-done | bytes 24608 | tf_op jit(solution)/shard_map/ppermute | solution.py:327
  17.9 0.0 collective-permute-done.3.refs_1_
  17.9 1.8 %shard_map.88 = (f32[4,72,128]{2,1,0:T(8,128)S(1)}, f32[4,72,128]{2,1,0:T(8,128)S(1)}) custom-call(f32[2,24,128]{2,1,0:T(8,128)S(1)} %pad_maximum_fusion.refs_0_, f32[2,24,128]{2,1,0:T(8,128)S(1)} %collective-permute-done.3.refs_1_, f32[2,24,128]{2,1,0:T(8,128)S(1)} %collective-permute-done.4.refs_2_, f32[2,24,128]{2,1,0:T(8,128)S(1)} %collective-permute-done.5.refs_3_, ...), custom_call_target="tpu_custom_call" | custom-call | tf_op jit(solution)/shard_map/pallas_call | solution.py:375
  19.7 0.2 collective-permute-start.6
  20.0 1.2 %collective-permute-done.6.got_ref = f32[4,72,128]{2,1,0:T(8,128)S(1)} collective-permute-done((f32[4,72,128]{2,1,0:T(8,128)S(1)}, f32[4,72,128]{2,1,0:T(8,128)S(1)}, u32[]{:S(2)}, u32[]{:S(2)}) %collective-permute-start.6) | collective-permute-done | bytes 147488 | tf_op jit(solution)/shard_map/ppermute | solution.py:327
  21.2 0.1 collective-permute-start.7
  21.3 1.8 %collective-permute-start.8 = (f32[72,128]{1,0:T(8,128)S(1)}, f32[72,128]{1,0:T(8,128)S(1)}, u32[]{:S(2)}, u32[]{:S(2)}) collective-permute-start(f32[72,128]{1,0:T(8,128)S(1)} %get-tuple-element.23), channel_id=1, source_target_pairs={{0,5},{1,4},{2,7},{3,6},{4,1},{5,0},{6,3},{7,2},{8,13},{9,12},{10,... | collective-permute-start | bytes 110600 | tf_op jit(solution)/shard_map/ppermute | solution.py:327
  23.1 2.1 %collective-permute-start.9 = (f32[72,128]{1,0:T(8,128)S(1)}, f32[72,128]{1,0:T(8,128)S(1)}, u32[]{:S(2)}, u32[]{:S(2)}) collective-permute-start(f32[72,128]{1,0:T(8,128)S(1)} %get-tuple-element.24), channel_id=1, source_target_pairs={{0,7},{1,6},{2,5},{3,4},{4,3},{5,2},{6,1},{7,0},{8,15},{9,14},{10,... | collective-permute-start | bytes 110600 | tf_op jit(solution)/shard_map/ppermute | solution.py:327
  25.1 0.0 collective-permute-done.7.refs_1_
  25.1 0.5 %collective-permute-done.8.refs_2_ = f32[72,128]{1,0:T(8,128)S(1)} collective-permute-done((f32[72,128]{1,0:T(8,128)S(1)}, f32[72,128]{1,0:T(8,128)S(1)}, u32[]{:S(2)}, u32[]{:S(2)}) %collective-permute-start.8) | collective-permute-done | bytes 36896 | tf_op jit(solution)/shard_map/ppermute | solution.py:327
  25.6 2.8 %collective-permute-done.9.refs_3_ = f32[72,128]{1,0:T(8,128)S(1)} collective-permute-done((f32[72,128]{1,0:T(8,128)S(1)}, f32[72,128]{1,0:T(8,128)S(1)}, u32[]{:S(2)}, u32[]{:S(2)}) %collective-permute-start.9) | collective-permute-done | bytes 36896 | tf_op jit(solution)/shard_map/ppermute | solution.py:327
  28.4 0.7 %shard_map.90 = (f32[8,8,128]{2,1,0:T(8,128)}, f32[1,8,8]{2,1,0:T(8,128)}) custom-call(f32[72,128]{1,0:T(8,128)S(1)} %get-tuple-element.21.refs_0_, f32[72,128]{1,0:T(8,128)S(1)} %collective-permute-done.7.refs_1_, f32[72,128]{1,0:T(8,128)S(1)} %collective-permute-done.8.refs_2_, f32[72,128]{1,0:T(8,128)S(1)} %collective-permute-done.9.refs_3_, ...), custom_call_target="tpu_custom_call" | custom-call | tf_op jit(solution)/shard_map/pallas_call | solution.py:395
  (3 shorter events, 0.0 us)
Async XLA Ops:
  1.8 3.3 %collective-permute-start = (bf16[288,128]{1,0:T(8,128)(2,1)S(1)}, bf16[288,128]{1,0:T(8,128)(2,1)S(1)}, u32[]{:S(2)}, u32[]{:S(2)}) collective-permute-start(bf16[288,128]{1,0:T(8,128)(2,1)S(1)} %get-tuple-element.15), channel_id=1, source_target_pairs={{0,8},{1,9},{2,10},{3,11},{4,12},{5,13},{6,14},{7,15},{8,0},{9,1},... | collective-permute-start | bytes 221192 | tf_op jit(solution)/shard_map/ppermute | solution.py:336
  3.1 4.1 %collective-permute-start.1 = (bf16[288,128]{1,0:T(8,128)(2,1)S(1)}, bf16[288,128]{1,0:T(8,128)(2,1)S(1)}, u32[]{:S(2)}, u32[]{:S(2)}) collective-permute-start(bf16[288,128]{1,0:T(8,128)(2,1)S(1)} %get-tuple-element.16), channel_id=1, source_target_pairs={{0,1},{1,0},{2,3},{3,2},{4,5},{5,4},{6,7},{7,6},{8,16},{9,17},{10,... | collective-permute-start | bytes 221192 | tf_op jit(solution)/shard_map/ppermute | solution.py:336
  7.2 3.0 %collective-permute-start.2 = (f32[24,128]{1,0:T(8,128)S(1)}, f32[24,128]{1,0:T(8,128)S(1)}, u32[]{:S(2)}, u32[]{:S(2)}) collective-permute-start(f32[24,128]{1,0:T(8,128)S(1)} %shard_map.87), channel_id=1, source_target_pairs={{0,1},{1,0},{2,3},{3,2},{4,5},{5,4},{6,7},{7,6},{8,9},{9,8},{10,11... | collective-permute-start | bytes 36872 | tf_op jit(solution)/shard_map/ppermute | solution.py:327
  10.2 5.1 %collective-permute-start.5 = (f32[2,24,128]{2,1,0:T(8,128)S(1)}, f32[2,24,128]{2,1,0:T(8,128)S(1)}, u32[]{:S(2)}, u32[]{:S(2)}) collective-permute-start(f32[2,24,128]{2,1,0:T(8,128)S(1)} %pad_maximum_fusion.refs_0_), channel_id=1, source_target_pairs={{0,7},{1,6},{2,5},{3,4},{4,3},{5,2},{6,1},{7,0},{8,15},{9,14},{10,... | collective-permute-start | bytes 73736 | tf_op jit(solution)/shard_map/ppermute | solution.py:327
  13.7 4.2 %collective-permute-start.4 = (f32[2,24,128]{2,1,0:T(8,128)S(1)}, f32[2,24,128]{2,1,0:T(8,128)S(1)}, u32[]{:S(2)}, u32[]{:S(2)}) collective-permute-start(f32[2,24,128]{2,1,0:T(8,128)S(1)} %pad_maximum_fusion.refs_0_), channel_id=1, source_target_pairs={{0,5},{1,4},{2,7},{3,6},{4,1},{5,0},{6,3},{7,2},{8,13},{9,12},{10,... | collective-permute-start | bytes 73736 | tf_op jit(solution)/shard_map/ppermute | solution.py:327
  13.7 4.2 %collective-permute-start.3 = (f32[2,24,128]{2,1,0:T(8,128)S(1)}, f32[2,24,128]{2,1,0:T(8,128)S(1)}, u32[]{:S(2)}, u32[]{:S(2)}) collective-permute-start(f32[2,24,128]{2,1,0:T(8,128)S(1)} %pad_maximum_fusion.refs_0_), channel_id=1, source_target_pairs={{0,3},{1,2},{2,1},{3,0},{4,7},{5,6},{6,5},{7,4},{8,11},{9,10},{10,... | collective-permute-start | bytes 73736 | tf_op jit(solution)/shard_map/ppermute | solution.py:327
  19.7 1.4 %collective-permute-start.6 = (f32[4,72,128]{2,1,0:T(8,128)S(1)}, f32[4,72,128]{2,1,0:T(8,128)S(1)}, u32[]{:S(2)}, u32[]{:S(2)}) collective-permute-start(f32[4,72,128]{2,1,0:T(8,128)S(1)} %get-tuple-element.20), channel_id=1, source_target_pairs={{0,1},{1,0},{2,3},{3,2},{4,5},{5,4},{6,7},{7,6},{8,9},{9,8},{10,11... | collective-permute-start | bytes 442376 | tf_op jit(solution)/shard_map/ppermute | solution.py:327
  21.2 3.9 %collective-permute-start.7 = (f32[72,128]{1,0:T(8,128)S(1)}, f32[72,128]{1,0:T(8,128)S(1)}, u32[]{:S(2)}, u32[]{:S(2)}) collective-permute-start(f32[72,128]{1,0:T(8,128)S(1)} %get-tuple-element.22), channel_id=1, source_target_pairs={{0,3},{1,2},{2,1},{3,0},{4,7},{5,6},{6,5},{7,4},{8,11},{9,10},{10,... | collective-permute-start | bytes 110600 | tf_op jit(solution)/shard_map/ppermute | solution.py:327
  21.3 4.3 %collective-permute-start.8 = (f32[72,128]{1,0:T(8,128)S(1)}, f32[72,128]{1,0:T(8,128)S(1)}, u32[]{:S(2)}, u32[]{:S(2)}) collective-permute-start(f32[72,128]{1,0:T(8,128)S(1)} %get-tuple-element.23), channel_id=1, source_target_pairs={{0,5},{1,4},{2,7},{3,6},{4,1},{5,0},{6,3},{7,2},{8,13},{9,12},{10,... | collective-permute-start | bytes 110600 | tf_op jit(solution)/shard_map/ppermute | solution.py:327
  23.1 5.3 %collective-permute-start.9 = (f32[72,128]{1,0:T(8,128)S(1)}, f32[72,128]{1,0:T(8,128)S(1)}, u32[]{:S(2)}, u32[]{:S(2)}) collective-permute-start(f32[72,128]{1,0:T(8,128)S(1)} %get-tuple-element.24), channel_id=1, source_target_pairs={{0,7},{1,6},{2,5},{3,4},{4,3},{5,2},{6,1},{7,0},{8,15},{9,14},{10,... | collective-permute-start | bytes 110600 | tf_op jit(solution)/shard_map/ppermute | solution.py:327

commit v5 on v4

--- a/solution.py
+++ b/solution.py
@@ -182,9 +182,8 @@
 ):
     got, refs = refs[:near], refs[near:]
     turned_ref, a_ref, b_ref, factors_ref, mine_ref, other_ref = refs[:6]
-    packs, member, d_all, hits_all, key_all, first, second, back = refs[6:]
+    packs, member, d_all, keep, hits_all, key_all, first, second, made, back = refs[6:]
     tiles = packs.shape[0]
-    blocks = -(-tiles * GROUP // LANES)
     block = min(tiles, LANES // GROUP)
     columns = tiles * LANES
     band, me = lax.axis_index("ty"), lax.axis_index("tx")
@@ -221,52 +220,45 @@
 
         fill(found, rows, levels, base, count, write)
 
+    first[:, columns:] = jnp.zeros((first.shape[0], LANES), F32)
+    second[:, columns:] = jnp.zeros((second.shape[0], LANES), F32)
+    keep[...] = 1.0 - 4.0 * d_all[...]
     source, target = first, second
-    left_end = iota((levels, columns), 1) == 0
-    right_end = iota((levels, columns), 1) == columns - 1
     for step in range(STEPS):
         for r in range(step + 1, 2 * STEPS + rows - 1 - step):
             mid = source[r * levels : (r + 1) * levels, :]
             beside = (
-                source[(r - 1) * levels : r * levels, :]
-                + source[(r + 1) * levels : (r + 2) * levels, :]
-                + jnp.where(left_end, 0.0, pltpu.roll(mid, 1, 1))
-                + jnp.where(right_end, 0.0, pltpu.roll(mid, columns - 1, 1))
+                source[(r - 1) * levels : r * levels, 0:columns]
+                + source[(r + 1) * levels : (r + 2) * levels, 0:columns]
+                + pltpu.roll(mid, 1, 1)[:, 0:columns]
+                + pltpu.roll(mid, columns + LANES - 1, 1)[:, 0:columns]
             )
-            d = jnp.broadcast_to(d_all[r : r + 1, :], (levels, columns))
-            target[r * levels : (r + 1) * levels, :] = mid + d * (beside - 4.0 * mid)
+            d, c = (jnp.broadcast_to(x[r : r + 1, :], (levels, columns)) for x in (d_all, keep))
+            target[r * levels : (r + 1) * levels, 0:columns] = c * mid[:, 0:columns] + d * beside
         source, target = target, source
 
     factors = [(i - BAND, factors_ref[i]) for i in range(2 * BAND + 1)]
-    chips = mine_ref.shape[0]
-    for z in range(chips):
+    for t in range(tiles):
+        at = slice(t * LANES, (t + 1) * LANES)
+        parts = []
+        for r in range(rows):
+            x = source[half + r * levels : half + (r + 1) * levels, at]
+            mixed = sum(f * (pltpu.roll(x, -o % levels, 0) if o else x) for o, f in factors)
+            part = mixed * member[half + r * levels : half + (r + 1) * levels, at]
+            made[t, r * levels : (r + 1) * levels, :] = part
+            parts.append(part)
+        stacked = jnp.concatenate(pieces(jnp.concatenate(parts, axis=0)), axis=0).astype(BF16)
+        found = jnp.dot(stacked, hits_all[t], preferred_element_type=F32)
+        found = found[0:own] + found[own : 2 * own] + found[2 * own :]
+        on = iota(found.shape, 0).astype(F32) == key_all[t][0:1]
+        line = jnp.sum(jnp.where(on, found, 0.0), axis=0, keepdims=True)
+        for q in range(tiles // block):
+            back[q, t : t + 1, :] = line[:, q * LANES : (q + 1) * LANES]
+    for t in range(tiles):
+        made[t, own:, :] = back[t // block]
+    for z in range(mine_ref.shape[0]):
         for side, out in enumerate((mine_ref, other_ref)):
-            t = 2 * z + (core ^ side ^ (chip != z).astype(jnp.int32))
-            mirror = 2 * (2 * z // block * block) + block - 1
-            at = pl.ds(pl.multiple_of(t * LANES, LANES), LANES)
-            parts = []
-            for r in range(rows):
-                x = source[half + r * levels : half + (r + 1) * levels, at]
-                mixed = sum(f * (pltpu.roll(x, -o % levels, 0) if o else x) for o, f in factors)
-                part = mixed * member[half + r * levels : half + (r + 1) * levels, at]
-                out[z, r * levels : (r + 1) * levels, :] = part
-                parts.append(part)
-            stacked = jnp.concatenate(pieces(jnp.concatenate(parts, axis=0)), axis=0).astype(BF16)
-            found = jnp.dot(stacked, hits_all[t], preferred_element_type=F32)
-            found = found[0:own] + found[own : 2 * own] + found[2 * own :]
-            on = iota(found.shape, 0).astype(F32) == key_all[t][0:1]
-            line = jnp.sum(jnp.where(on, found, 0.0), axis=0, keepdims=True)
-            for q in range(tiles // block):
-                back[q, pl.ds(mirror - t, 1), :] = line[:, q * LANES : (q + 1) * LANES]
-    turned = [
-        [stagger(back[q, b * block : (b + 1) * block, :]) for b in range(blocks)] for q in range(tiles // block)
-    ]
-    for z in range(chips):
-        for side, out in enumerate((mine_ref, other_ref)):
-            out[z, own:, :] = jnp.zeros((out.shape[1] - own, LANES), F32)
-            place = 2 * z % block + (core ^ side ^ (chip != z).astype(jnp.int32))
-            for b in range(blocks):
-                out[z, own + b : own + b + 1, :] = pick(turned[2 * z // block][b], place)
+            out[z] = made[2 * z + (core ^ side ^ (chip != z).astype(jnp.int32))]
 
 
 def pair_kernel(mine_ref, got_ref, *outs):
@@ -276,21 +268,18 @@
 
 
 def final_kernel(near, *refs):
-    got, (live_ref, inc_ref, proj_ref, total, wide) = refs[:near], refs[near:]
+    got, (live_ref, inc_ref, proj_ref, total) = refs[:near], refs[near:]
     levels, rows, _ = inc_ref.shape
     _, tiles, slots = proj_ref.shape
-    block = min(tiles, LANES // GROUP)
     sums = got[0][...]
     for ref in got[1:]:
         sums = sums + ref[...]
     total[...] = sums
     for level in range(levels):
         inc_ref[level] = total[pl.ds(level, rows, stride=levels), :]
-    for b in range(tiles // block):
-        line = jnp.broadcast_to(total[rows * levels + b : rows * levels + b + 1, :], (block, LANES))
-        line = pltpu.roll(line, (LANES - GROUP * (block - 1)) % LANES, 1)
-        wide[b * block : (b + 1) * block, :] = stagger(line)
-    proj_ref[0] = jnp.where(live_ref[:, 0:slots] > 0.0, wide[:, 0:slots], 0.0)
+    place = lax.rem(lax.axis_index("tx"), LANES // GROUP)
+    lines = pltpu.roll(sums[rows * levels :], lax.rem(LANES - GROUP * place, LANES), 1)
+    proj_ref[0] = jnp.where(live_ref[:, 0:slots] > 0.0, lines[:, 0:slots], 0.0)
 
 
 def call(kernel, out_shape, ins, scratch, flops=0, moved=0):
@@ -371,7 +360,7 @@
     pair = jnp.stack([mine, swap(mine, 1)])
     row = [pair] + [swap(pair, 2 * far + 1) for far in range(1, chips)]
 
-    chunk = own + 8
+    chunk = own + tiles
     mine, other = call(
         functools.partial(main_kernel, chips, rows, levels, lines),
         (shape((chips, chunk, LANES), F32), shape((chips, chunk, LANES), F32)),
@@ -380,10 +369,12 @@
             pltpu.VMEM((tiles, joined, LANES), F32),
             pltpu.VMEM((2 * half + own, columns), F32),
             pltpu.VMEM((2 * STEPS + rows, columns), F32),
+            pltpu.VMEM((2 * STEPS + rows, columns), F32),
             pltpu.VMEM((tiles, LANES, lanes), BF16),
             pltpu.VMEM((tiles, 8, lanes), F32),
-            pltpu.VMEM((2 * half + own, columns), F32),
-            pltpu.VMEM((2 * half + own, columns), F32),
+            pltpu.VMEM((2 * half + own, columns + LANES), F32),
+            pltpu.VMEM((2 * half + own, columns + LANES), F32),
+            pltpu.VMEM((tiles, chunk, LANES), F32),
             pltpu.VMEM((tiles // block, tiles, LANES), F32),
         ],
     )(*row, turned, from_a, from_b, factors)
@@ -396,8 +387,8 @@
         functools.partial(final_kernel, chips),
         (shape((levels, rows, LANES), F32), shape((1, tiles, slots), F32)),
         [VMEM] * (chips + 1),
-        [pltpu.VMEM((chunk, LANES), F32), pltpu.VMEM((tiles, LANES), F32)],
-    )(*sums, live)
+        [pltpu.VMEM((chunk, LANES), F32)],
+    )(sums[0], *sums[:0:-1], live)
 
 
 def solution(mesh):

time: 29.3 us -> 28.9 us (0.986)
  no operation moved by 1% of the time
where the time goes in v5:
time: 28.9 us; the launch traced here: 28.7 us
  waiting for transfers between devices  12.9 us (45%)
  starting transfers between devices  11.7 us (40%)
  Pallas kernels  3.46 us (12%)
  between operations  0.67 us (2%)
    ppermute x8, starting transfers between devices, swap(): return lax.ppermute(x, 'tx', [(i, i ^ far) for i in range(tiles)])  10.4 us
    ppermute x8, waiting for transfers between devices, swap(): return lax.ppermute(x, 'tx', [(i, i ^ far) for i in range(tiles)])  8.81 us
    ppermute x2, waiting for transfers between devices, swap_bands(): return lax.ppermute(x, ('ty', 'tx'), pairs)  4.08 us
    pallas_call x1, Pallas kernels, shards(): call(functools.partial(main_kernel, chips, rows, levels, lines), (shape((...  1.62 us
    ppermute x2, starting transfers between devices, swap_bands(): return lax.ppermute(x, ('ty', 'tx'), pairs)  1.3 us
    pallas_call x1, Pallas kernels, shards(): call(first_kernel, (shape((height, LANES), F32), shape((tiles, own, LANES...  1.14 us
    pallas_call x1, Pallas kernels, shards(): call(functools.partial(final_kernel, chips), (shape((levels, rows, LANES)...  0.68 us
  transfers between devices with their start and end apart: 10, of which 8 were waited for; matrix products, arithmetic and copies ran while one was open for 0% of the time, Pallas kernels for 0%

profile of v5, /device:TPU:5, one launch (start us, length us, event | category | flops | bytes accessed | tf_op | source)
XLA Modules:
  0.0 28.7 jit_solution(7914260152805582233)
XLA Ops:
  0.6 1.1 %shard_map.86 = (f32[16,128]{1,0:T(8,128)S(1)}, bf16[8,64,128]{2,1,0:T(8,128)(2,1)S(1)}, bf16[288,128]{1,0:T(8,128)(2,1)S(1)}, bf16[288,128]{1,0:T(8,128)(2,1)S(...) custom-call(f32[1,8,8]{2,1,0:T(8,128)} %value_hbm.1, s32[1,8,8]{2,1,0:T(8,128)} %cell_hbm.1, s32[1,8]{1,0:T(1,128)} %count_hbm.1, ...), custom_call_target="tpu_custom_call" | custom-call | tf_op jit(solution)/shard_map/pallas_call | solution.py:328
  1.8 1.3 %collective-permute-start = (bf16[288,128]{1,0:T(8,128)(2,1)S(1)}, bf16[288,128]{1,0:T(8,128)(2,1)S(1)}, u32[]{:S(2)}, u32[]{:S(2)}) collective-permute-start(bf16[288,128]{1,0:T(8,128)(2,1)S(1)} %get-tuple-element.15), channel_id=1, source_target_pairs={{0,8},{1,9},{2,10},{3,11},{4,12},{5,13},{6,14},{7,15},{8,0},{9,1},... | collective-permute-start | bytes 221192 | tf_op jit(solution)/shard_map/ppermute | solution.py:325
  3.1 0.0 collective-permute-start.1
  3.1 2.0 %collective-permute-done.a_ref.refs_5_ = bf16[288,128]{1,0:T(8,128)(2,1)S(1)} collective-permute-done((bf16[288,128]{1,0:T(8,128)(2,1)S(1)}, bf16[288,128]{1,0:T(8,128)(2,1)S(1)}, u32[]{:S(2)}, u32[]{:S(2)}) %collective-permute-start) | collective-permute-done | bytes 73760 | tf_op jit(solution)/shard_map/ppermute | solution.py:325
  5.0 2.1 %collective-permute-done.1.b_ref.refs_6_ = bf16[288,128]{1,0:T(8,128)(2,1)S(1)} collective-permute-done((bf16[288,128]{1,0:T(8,128)(2,1)S(1)}, bf16[288,128]{1,0:T(8,128)(2,1)S(1)}, u32[]{:S(2)}, u32[]{:S(2)}) %collective-permute-start.1) | collective-permute-done | bytes 73760 | tf_op jit(solution)/shard_map/ppermute | solution.py:325
  7.2 2.2 %collective-permute-start.2 = (f32[24,128]{1,0:T(8,128)S(1)}, f32[24,128]{1,0:T(8,128)S(1)}, u32[]{:S(2)}, u32[]{:S(2)}) collective-permute-start(f32[24,128]{1,0:T(8,128)S(1)} %shard_map.87), channel_id=1, source_target_pairs={{0,1},{1,0},{2,3},{3,2},{4,5},{5,4},{6,7},{7,6},{8,9},{9,8},{10,11... | collective-permute-start | bytes 36872 | tf_op jit(solution)/shard_map/ppermute | solution.py:316
  9.3 0.8 %collective-permute-done.2 = f32[24,128]{1,0:T(8,128)S(1)} collective-permute-done((f32[24,128]{1,0:T(8,128)S(1)}, f32[24,128]{1,0:T(8,128)S(1)}, u32[]{:S(2)}, u32[]{:S(2)}) %collective-permute-start.2) | collective-permute-done | bytes 12320 | tf_op jit(solution)/shard_map/ppermute | solution.py:316
  10.2 3.6 %collective-permute-start.5 = (f32[2,24,128]{2,1,0:T(8,128)S(1)}, f32[2,24,128]{2,1,0:T(8,128)S(1)}, u32[]{:S(2)}, u32[]{:S(2)}) collective-permute-start(f32[2,24,128]{2,1,0:T(8,128)S(1)} %pad_maximum_fusion.refs_0_), channel_id=1, source_target_pairs={{0,7},{1,6},{2,5},{3,4},{4,3},{5,2},{6,1},{7,0},{8,15},{9,14},{10,... | collective-permute-start | bytes 73736 | tf_op jit(solution)/shard_map/ppermute | solution.py:316
  13.7 0.0 collective-permute-start.4
  13.7 0.5 %collective-permute-start.3 = (f32[2,24,128]{2,1,0:T(8,128)S(1)}, f32[2,24,128]{2,1,0:T(8,128)S(1)}, u32[]{:S(2)}, u32[]{:S(2)}) collective-permute-start(f32[2,24,128]{2,1,0:T(8,128)S(1)} %pad_maximum_fusion.refs_0_), channel_id=1, source_target_pairs={{0,3},{1,2},{2,1},{3,0},{4,7},{5,6},{6,5},{7,4},{8,11},{9,10},{10,... | collective-permute-start | bytes 73736 | tf_op jit(solution)/shard_map/ppermute | solution.py:316
  14.2 1.0 %collective-permute-done.5.refs_3_ = f32[2,24,128]{2,1,0:T(8,128)S(1)} collective-permute-done((f32[2,24,128]{2,1,0:T(8,128)S(1)}, f32[2,24,128]{2,1,0:T(8,128)S(1)}, u32[]{:S(2)}, u32[]{:S(2)}) %collective-permute-start.5) | collective-permute-done | bytes 24608 | tf_op jit(solution)/shard_map/ppermute | solution.py:316
  15.2 2.6 %collective-permute-done.4.refs_2_ = f32[2,24,128]{2,1,0:T(8,128)S(1)} collective-permute-done((f32[2,24,128]{2,1,0:T(8,128)S(1)}, f32[2,24,128]{2,1,0:T(8,128)S(1)}, u32[]{:S(2)}, u32[]{:S(2)}) %collective-permute-start.4) | collective-permute-done | bytes 24608 | tf_op jit(solution)/shard_map/ppermute | solution.py:316
  17.9 0.0 collective-permute-done.3.refs_1_
  17.9 1.6 %shard_map.88 = (f32[4,72,128]{2,1,0:T(8,128)S(1)}, f32[4,72,128]{2,1,0:T(8,128)S(1)}) custom-call(f32[2,24,128]{2,1,0:T(8,128)S(1)} %pad_maximum_fusion.refs_0_, f32[2,24,128]{2,1,0:T(8,128)S(1)} %collective-permute-done.3.refs_1_, f32[2,24,128]{2,1,0:T(8,128)S(1)} %collective-permute-done.4.refs_2_, f32[2,24,128]{2,1,0:T(8,128)S(1)} %collective-permute-done.5.refs_3_, ...), custom_call_target="tpu_custom_call" | custom-call | tf_op jit(solution)/shard_map/pallas_call | solution.py:364
  19.5 0.2 collective-permute-start.6
  19.7 1.2 %collective-permute-done.6.got_ref = f32[4,72,128]{2,1,0:T(8,128)S(1)} collective-permute-done((f32[4,72,128]{2,1,0:T(8,128)S(1)}, f32[4,72,128]{2,1,0:T(8,128)S(1)}, u32[]{:S(2)}, u32[]{:S(2)}) %collective-permute-start.6) | collective-permute-done | bytes 147488 | tf_op jit(solution)/shard_map/ppermute | solution.py:316
  21.0 1.5 %collective-permute-start.7 = (f32[72,128]{1,0:T(8,128)S(1)}, f32[72,128]{1,0:T(8,128)S(1)}, u32[]{:S(2)}, u32[]{:S(2)}) collective-permute-start(f32[72,128]{1,0:T(8,128)S(1)} %get-tuple-element.22), channel_id=1, source_target_pairs={{0,7},{1,6},{2,5},{3,4},{4,3},{5,2},{6,1},{7,0},{8,15},{9,14},{10,... | collective-permute-start | bytes 110600 | tf_op jit(solution)/shard_map/ppermute | solution.py:316
  22.5 0.3 %collective-permute-start.8 = (f32[72,128]{1,0:T(8,128)S(1)}, f32[72,128]{1,0:T(8,128)S(1)}, u32[]{:S(2)}, u32[]{:S(2)}) collective-permute-start(f32[72,128]{1,0:T(8,128)S(1)} %get-tuple-element.23), channel_id=1, source_target_pairs={{0,5},{1,4},{2,7},{3,6},{4,1},{5,0},{6,3},{7,2},{8,13},{9,12},{10,... | collective-permute-start | bytes 110600 | tf_op jit(solution)/shard_map/ppermute | solution.py:316
  22.9 2.1 %collective-permute-start.9 = (f32[72,128]{1,0:T(8,128)S(1)}, f32[72,128]{1,0:T(8,128)S(1)}, u32[]{:S(2)}, u32[]{:S(2)}) collective-permute-start(f32[72,128]{1,0:T(8,128)S(1)} %get-tuple-element.24), channel_id=1, source_target_pairs={{0,3},{1,2},{2,1},{3,0},{4,7},{5,6},{6,5},{7,4},{8,11},{9,10},{10,... | collective-permute-start | bytes 110600 | tf_op jit(solution)/shard_map/ppermute | solution.py:316
  24.9 1.4 %collective-permute-done.7.refs_1_ = f32[72,128]{1,0:T(8,128)S(1)} collective-permute-done((f32[72,128]{1,0:T(8,128)S(1)}, f32[72,128]{1,0:T(8,128)S(1)}, u32[]{:S(2)}, u32[]{:S(2)}) %collective-permute-start.7) | collective-permute-done | bytes 36896 | tf_op jit(solution)/shard_map/ppermute | solution.py:316
  26.4 1.7 %collective-permute-done.8.refs_2_ = f32[72,128]{1,0:T(8,128)S(1)} collective-permute-done((f32[72,128]{1,0:T(8,128)S(1)}, f32[72,128]{1,0:T(8,128)S(1)}, u32[]{:S(2)}, u32[]{:S(2)}) %collective-permute-start.8) | collective-permute-done | bytes 36896 | tf_op jit(solution)/shard_map/ppermute | solution.py:316
  28.0 0.0 collective-permute-done.9.refs_3_
  28.0 0.7 %shard_map.90 = (f32[8,8,128]{2,1,0:T(8,128)}, f32[1,8,8]{2,1,0:T(8,128)}) custom-call(f32[72,128]{1,0:T(8,128)S(1)} %get-tuple-element.21.refs_0_, f32[72,128]{1,0:T(8,128)S(1)} %collective-permute-done.7.refs_1_, f32[72,128]{1,0:T(8,128)S(1)} %collective-permute-done.8.refs_2_, f32[72,128]{1,0:T(8,128)S(1)} %collective-permute-done.9.refs_3_, ...), custom_call_target="tpu_custom_call" | custom-call | tf_op jit(solution)/shard_map/pallas_call | solution.py:386
  (3 shorter events, 0.0 us)
Async XLA Ops:
  1.8 3.3 %collective-permute-start = (bf16[288,128]{1,0:T(8,128)(2,1)S(1)}, bf16[288,128]{1,0:T(8,128)(2,1)S(1)}, u32[]{:S(2)}, u32[]{:S(2)}) collective-permute-start(bf16[288,128]{1,0:T(8,128)(2,1)S(1)} %get-tuple-element.15), channel_id=1, source_target_pairs={{0,8},{1,9},{2,10},{3,11},{4,12},{5,13},{6,14},{7,15},{8,0},{9,1},... | collective-permute-start | bytes 221192 | tf_op jit(solution)/shard_map/ppermute | solution.py:325
  3.1 4.1 %collective-permute-start.1 = (bf16[288,128]{1,0:T(8,128)(2,1)S(1)}, bf16[288,128]{1,0:T(8,128)(2,1)S(1)}, u32[]{:S(2)}, u32[]{:S(2)}) collective-permute-start(bf16[288,128]{1,0:T(8,128)(2,1)S(1)} %get-tuple-element.16), channel_id=1, source_target_pairs={{0,1},{1,0},{2,3},{3,2},{4,5},{5,4},{6,7},{7,6},{8,16},{9,17},{10,... | collective-permute-start | bytes 221192 | tf_op jit(solution)/shard_map/ppermute | solution.py:325
  7.2 3.0 %collective-permute-start.2 = (f32[24,128]{1,0:T(8,128)S(1)}, f32[24,128]{1,0:T(8,128)S(1)}, u32[]{:S(2)}, u32[]{:S(2)}) collective-permute-start(f32[24,128]{1,0:T(8,128)S(1)} %shard_map.87), channel_id=1, source_target_pairs={{0,1},{1,0},{2,3},{3,2},{4,5},{5,4},{6,7},{7,6},{8,9},{9,8},{10,11... | collective-permute-start | bytes 36872 | tf_op jit(solution)/shard_map/ppermute | solution.py:316
  10.2 5.1 %collective-permute-start.5 = (f32[2,24,128]{2,1,0:T(8,128)S(1)}, f32[2,24,128]{2,1,0:T(8,128)S(1)}, u32[]{:S(2)}, u32[]{:S(2)}) collective-permute-start(f32[2,24,128]{2,1,0:T(8,128)S(1)} %pad_maximum_fusion.refs_0_), channel_id=1, source_target_pairs={{0,7},{1,6},{2,5},{3,4},{4,3},{5,2},{6,1},{7,0},{8,15},{9,14},{10,... | collective-permute-start | bytes 73736 | tf_op jit(solution)/shard_map/ppermute | solution.py:316
  13.7 4.2 %collective-permute-start.4 = (f32[2,24,128]{2,1,0:T(8,128)S(1)}, f32[2,24,128]{2,1,0:T(8,128)S(1)}, u32[]{:S(2)}, u32[]{:S(2)}) collective-permute-start(f32[2,24,128]{2,1,0:T(8,128)S(1)} %pad_maximum_fusion.refs_0_), channel_id=1, source_target_pairs={{0,5},{1,4},{2,7},{3,6},{4,1},{5,0},{6,3},{7,2},{8,13},{9,12},{10,... | collective-permute-start | bytes 73736 | tf_op jit(solution)/shard_map/ppermute | solution.py:316
  13.7 4.2 %collective-permute-start.3 = (f32[2,24,128]{2,1,0:T(8,128)S(1)}, f32[2,24,128]{2,1,0:T(8,128)S(1)}, u32[]{:S(2)}, u32[]{:S(2)}) collective-permute-start(f32[2,24,128]{2,1,0:T(8,128)S(1)} %pad_maximum_fusion.refs_0_), channel_id=1, source_target_pairs={{0,3},{1,2},{2,1},{3,0},{4,7},{5,6},{6,5},{7,4},{8,11},{9,10},{10,... | collective-permute-start | bytes 73736 | tf_op jit(solution)/shard_map/ppermute | solution.py:316
  19.5 1.4 %collective-permute-start.6 = (f32[4,72,128]{2,1,0:T(8,128)S(1)}, f32[4,72,128]{2,1,0:T(8,128)S(1)}, u32[]{:S(2)}, u32[]{:S(2)}) collective-permute-start(f32[4,72,128]{2,1,0:T(8,128)S(1)} %get-tuple-element.20), channel_id=1, source_target_pairs={{0,1},{1,0},{2,3},{3,2},{4,5},{5,4},{6,7},{7,6},{8,9},{9,8},{10,11... | collective-permute-start | bytes 442376 | tf_op jit(solution)/shard_map/ppermute | solution.py:316
  21.0 5.4 %collective-permute-start.7 = (f32[72,128]{1,0:T(8,128)S(1)}, f32[72,128]{1,0:T(8,128)S(1)}, u32[]{:S(2)}, u32[]{:S(2)}) collective-permute-start(f32[72,128]{1,0:T(8,128)S(1)} %get-tuple-element.22), channel_id=1, source_target_pairs={{0,7},{1,6},{2,5},{3,4},{4,3},{5,2},{6,1},{7,0},{8,15},{9,14},{10,... | collective-permute-start | bytes 110600 | tf_op jit(solution)/shard_map/ppermute | solution.py:316
  22.5 5.5 %collective-permute-start.8 = (f32[72,128]{1,0:T(8,128)S(1)}, f32[72,128]{1,0:T(8,128)S(1)}, u32[]{:S(2)}, u32[]{:S(2)}) collective-permute-start(f32[72,128]{1,0:T(8,128)S(1)} %get-tuple-element.23), channel_id=1, source_target_pairs={{0,5},{1,4},{2,7},{3,6},{4,1},{5,0},{6,3},{7,2},{8,13},{9,12},{10,... | collective-permute-start | bytes 110600 | tf_op jit(solution)/shard_map/ppermute | solution.py:316
  22.9 5.2 %collective-permute-start.9 = (f32[72,128]{1,0:T(8,128)S(1)}, f32[72,128]{1,0:T(8,128)S(1)}, u32[]{:S(2)}, u32[]{:S(2)}) collective-permute-start(f32[72,128]{1,0:T(8,128)S(1)} %get-tuple-element.24), channel_id=1, source_target_pairs={{0,3},{1,2},{2,1},{3,0},{4,7},{5,6},{6,5},{7,4},{8,11},{9,10},{10,... | collective-permute-start | bytes 110600 | tf_op jit(solution)/shard_map/ppermute | solution.py:316

commit v6 on v5

--- a/solution.py
+++ b/solution.py
@@ -11,6 +11,7 @@
 BAND = 2
 LANES = 128
 GROUP = 8
+CODES, FULL, LEAST = 128, 32700.0, 1.2e-38
 F32, BF16 = jnp.float32, jnp.bfloat16
 VMEM = pl.BlockSpec(memory_space=pltpu.VMEM)
 HBM = pl.BlockSpec(memory_space=pltpu.HBM)
@@ -261,24 +262,44 @@
             out[z] = made[2 * z + (core ^ side ^ (chip != z).astype(jnp.int32))]
 
 
-def pair_kernel(mine_ref, got_ref, *outs):
+def scale_of(code):
+    return jnp.exp2(code.astype(F32) * (1.0 / CODES))
+
+
+def pair_kernel(split, mine_ref, got_ref, near_ref, *outs):
     chip = lax.axis_index("tx") // 2
-    for far, out in enumerate(outs):
-        out[...] = mine_ref[chip ^ far] + got_ref[chip ^ far]
-
-
-def final_kernel(near, *refs):
-    got, (live_ref, inc_ref, proj_ref, total) = refs[:near], refs[near:]
+    near_ref[...] = mine_ref[chip] + got_ref[chip]
+    for far, out in enumerate(outs, 1):
+        x = mine_ref[chip ^ far] + got_ref[chip ^ far]
+        whole, codes = [], []
+        for part in (x[0:split], x[split:]):
+            largest = jnp.maximum(jnp.max(jnp.abs(part), axis=0, keepdims=True), LEAST)
+            code = jnp.minimum(jnp.ceil(jnp.log2(largest) * CODES).astype(jnp.int32), CODES * 128 - 1)
+            sized = jnp.clip(part * (1.0 / scale_of(code)), -1.0, 1.0)
+            whole.append(jnp.floor(sized * FULL + 0.5).astype(jnp.int32))
+            codes.append(code)
+        rest = out.shape[0] - x.shape[0]
+        row = iota((rest, LANES), 0)
+        tail = jnp.where(row == 0, codes[0], jnp.where(row == 1, codes[1], 0))
+        out[...] = jnp.concatenate([*whole, tail], axis=0).astype(jnp.int16)
+
+
+def final_kernel(split, *refs):
+    got, (live_ref, inc_ref, proj_ref, total) = refs[:-4], refs[-4:]
     levels, rows, _ = inc_ref.shape
     _, tiles, slots = proj_ref.shape
-    sums = got[0][...]
+    size = got[0].shape[0]
+    top, low = got[0][0:split, :], got[0][split:, :]
     for ref in got[1:]:
-        sums = sums + ref[...]
-    total[...] = sums
+        x = ref[...].astype(jnp.int32)
+        sent = x[0:size].astype(F32) * (1.0 / FULL)
+        top = top + sent[0:split] * scale_of(x[size : size + 1])
+        low = low + sent[split:] * scale_of(x[size + 1 : size + 2])
+    total[...] = top
     for level in range(levels):
         inc_ref[level] = total[pl.ds(level, rows, stride=levels), :]
     place = lax.rem(lax.axis_index("tx"), LANES // GROUP)
-    lines = pltpu.roll(sums[rows * levels :], lax.rem(LANES - GROUP * place, LANES), 1)
+    lines = pltpu.roll(low, lax.rem(LANES - GROUP * place, LANES), 1)
     proj_ref[0] = jnp.where(live_ref[:, 0:slots] > 0.0, lines[:, 0:slots], 0.0)
 
 
@@ -379,15 +400,16 @@
         ],
     )(*row, turned, from_a, from_b, factors)
 
+    coded = shape((round_up(chunk + 2, 16), LANES), jnp.int16)
     sums = call(
-        pair_kernel, tuple(shape((chunk, LANES), F32) for _ in range(chips)), [VMEM] * 2, []
+        functools.partial(pair_kernel, own), (shape((chunk, LANES), F32), *[coded] * (chips - 1)), [VMEM] * 2, []
     )(mine, swap(other, 1))
     sums = [sums[0]] + [swap(sums[far], 2 * far + 1) for far in range(1, chips)]
     return call(
-        functools.partial(final_kernel, chips),
+        functools.partial(final_kernel, own),
         (shape((levels, rows, LANES), F32), shape((1, tiles, slots), F32)),
         [VMEM] * (chips + 1),
-        [pltpu.VMEM((chunk, LANES), F32)],
+        [pltpu.VMEM((own, LANES), F32)],
     )(sums[0], *sums[:0:-1], live)
 
 

time: 28.9 us -> 28 us (0.969)
  waiting for transfers between devices: 12.9 us -> 11.9 us
    ppermute x8, waiting for transfers between devices: 8.81 us -> 7.83 us  [swap(): return lax.ppermute(x, 'tx', [(i, i ^ far) for i in range(tiles)])]
  transfers between devices with their start and end apart: 10 -> 10, of which waited for: 8 -> 9; matrix products, arithmetic and copies ran while one was open for 0% -> 0% of each run, Pallas kernels for 0% -> 0%
where the time goes in v6:
time: 28 us; the launch traced here: 27.8 us
  waiting for transfers between devices  11.9 us (42%)
  starting transfers between devices  11.7 us (42%)
  Pallas kernels  3.54 us (13%)
  between operations  0.66 us (2%)
    ppermute x8, starting transfers between devices, swap(): return lax.ppermute(x, 'tx', [(i, i ^ far) for i in range(tiles)])  10.4 us
    ppermute x8, waiting for transfers between devices, swap(): return lax.ppermute(x, 'tx', [(i, i ^ far) for i in range(tiles)])  7.83 us
    ppermute x2, waiting for transfers between devices, swap_bands(): return lax.ppermute(x, ('ty', 'tx'), pairs)  4.08 us
    pallas_call x1, Pallas kernels, shards(): call(functools.partial(main_kernel, chips, rows, levels, lines), (shape((...  1.62 us
    ppermute x2, starting transfers between devices, swap_bands(): return lax.ppermute(x, ('ty', 'tx'), pairs)  1.3 us
    pallas_call x1, Pallas kernels, shards(): call(first_kernel, (shape((height, LANES), F32), shape((tiles, own, LANES...  1.14 us
    pallas_call x1, Pallas kernels, shards(): call(functools.partial(final_kernel, own), (shape((levels, rows, LANES),...  0.68 us
  transfers between devices with their start and end apart: 10, of which 9 were waited for; matrix products, arithmetic and copies ran while one was open for 0% of the time, Pallas kernels for 0%

profile of v6, /device:TPU:5, one launch (start us, length us, event | category | flops | bytes accessed | tf_op | source)
XLA Modules:
  0.0 27.8 jit_solution(211129321996639812)
XLA Ops:
  0.6 1.1 %shard_map.86 = (f32[16,128]{1,0:T(8,128)S(1)}, bf16[8,64,128]{2,1,0:T(8,128)(2,1)S(1)}, bf16[288,128]{1,0:T(8,128)(2,1)S(1)}, bf16[288,128]{1,0:T(8,128)(2,1)S(...) custom-call(f32[1,8,8]{2,1,0:T(8,128)} %value_hbm.1, s32[1,8,8]{2,1,0:T(8,128)} %cell_hbm.1, s32[1,8]{1,0:T(1,128)} %count_hbm.1, ...), custom_call_target="tpu_custom_call" | custom-call | tf_op jit(solution)/shard_map/pallas_call | solution.py:349
  1.8 1.3 %collective-permute-start = (bf16[288,128]{1,0:T(8,128)(2,1)S(1)}, bf16[288,128]{1,0:T(8,128)(2,1)S(1)}, u32[]{:S(2)}, u32[]{:S(2)}) collective-permute-start(bf16[288,128]{1,0:T(8,128)(2,1)S(1)} %get-tuple-element.15), channel_id=1, source_target_pairs={{0,8},{1,9},{2,10},{3,11},{4,12},{5,13},{6,14},{7,15},{8,0},{9,1},... | collective-permute-start | bytes 221192 | tf_op jit(solution)/shard_map/ppermute | solution.py:346
  3.1 0.0 collective-permute-start.1
  3.1 2.0 %collective-permute-done.a_ref.refs_5_ = bf16[288,128]{1,0:T(8,128)(2,1)S(1)} collective-permute-done((bf16[288,128]{1,0:T(8,128)(2,1)S(1)}, bf16[288,128]{1,0:T(8,128)(2,1)S(1)}, u32[]{:S(2)}, u32[]{:S(2)}) %collective-permute-start) | collective-permute-done | bytes 73760 | tf_op jit(solution)/shard_map/ppermute | solution.py:346
  5.0 2.1 %collective-permute-done.1.b_ref.refs_6_ = bf16[288,128]{1,0:T(8,128)(2,1)S(1)} collective-permute-done((bf16[288,128]{1,0:T(8,128)(2,1)S(1)}, bf16[288,128]{1,0:T(8,128)(2,1)S(1)}, u32[]{:S(2)}, u32[]{:S(2)}) %collective-permute-start.1) | collective-permute-done | bytes 73760 | tf_op jit(solution)/shard_map/ppermute | solution.py:346
  7.2 2.2 %collective-permute-start.2 = (f32[24,128]{1,0:T(8,128)S(1)}, f32[24,128]{1,0:T(8,128)S(1)}, u32[]{:S(2)}, u32[]{:S(2)}) collective-permute-start(f32[24,128]{1,0:T(8,128)S(1)} %shard_map.87), channel_id=1, source_target_pairs={{0,1},{1,0},{2,3},{3,2},{4,5},{5,4},{6,7},{7,6},{8,9},{9,8},{10,11... | collective-permute-start | bytes 36872 | tf_op jit(solution)/shard_map/ppermute | solution.py:337
  9.3 0.8 %collective-permute-done.2 = f32[24,128]{1,0:T(8,128)S(1)} collective-permute-done((f32[24,128]{1,0:T(8,128)S(1)}, f32[24,128]{1,0:T(8,128)S(1)}, u32[]{:S(2)}, u32[]{:S(2)}) %collective-permute-start.2) | collective-permute-done | bytes 12320 | tf_op jit(solution)/shard_map/ppermute | solution.py:337
  10.2 3.6 %collective-permute-start.5 = (f32[2,24,128]{2,1,0:T(8,128)S(1)}, f32[2,24,128]{2,1,0:T(8,128)S(1)}, u32[]{:S(2)}, u32[]{:S(2)}) collective-permute-start(f32[2,24,128]{2,1,0:T(8,128)S(1)} %pad_maximum_fusion.refs_0_), channel_id=1, source_target_pairs={{0,7},{1,6},{2,5},{3,4},{4,3},{5,2},{6,1},{7,0},{8,15},{9,14},{10,... | collective-permute-start | bytes 73736 | tf_op jit(solution)/shard_map/ppermute | solution.py:337
  13.7 0.0 collective-permute-start.4
  13.7 0.5 %collective-permute-start.3 = (f32[2,24,128]{2,1,0:T(8,128)S(1)}, f32[2,24,128]{2,1,0:T(8,128)S(1)}, u32[]{:S(2)}, u32[]{:S(2)}) collective-permute-start(f32[2,24,128]{2,1,0:T(8,128)S(1)} %pad_maximum_fusion.refs_0_), channel_id=1, source_target_pairs={{0,3},{1,2},{2,1},{3,0},{4,7},{5,6},{6,5},{7,4},{8,11},{9,10},{10,... | collective-permute-start | bytes 73736 | tf_op jit(solution)/shard_map/ppermute | solution.py:337
  14.2 1.0 %collective-permute-done.5.refs_3_ = f32[2,24,128]{2,1,0:T(8,128)S(1)} collective-permute-done((f32[2,24,128]{2,1,0:T(8,128)S(1)}, f32[2,24,128]{2,1,0:T(8,128)S(1)}, u32[]{:S(2)}, u32[]{:S(2)}) %collective-permute-start.5) | collective-permute-done | bytes 24608 | tf_op jit(solution)/shard_map/ppermute | solution.py:337
  15.2 2.6 %collective-permute-done.4.refs_2_ = f32[2,24,128]{2,1,0:T(8,128)S(1)} collective-permute-done((f32[2,24,128]{2,1,0:T(8,128)S(1)}, f32[2,24,128]{2,1,0:T(8,128)S(1)}, u32[]{:S(2)}, u32[]{:S(2)}) %collective-permute-start.4) | collective-permute-done | bytes 24608 | tf_op jit(solution)/shard_map/ppermute | solution.py:337
  17.9 0.0 collective-permute-done.3.refs_1_
  17.9 1.6 %shard_map.88 = (f32[4,72,128]{2,1,0:T(8,128)S(1)}, f32[4,72,128]{2,1,0:T(8,128)S(1)}) custom-call(f32[2,24,128]{2,1,0:T(8,128)S(1)} %pad_maximum_fusion.refs_0_, f32[2,24,128]{2,1,0:T(8,128)S(1)} %collective-permute-done.3.refs_1_, f32[2,24,128]{2,1,0:T(8,128)S(1)} %collective-permute-done.4.refs_2_, f32[2,24,128]{2,1,0:T(8,128)S(1)} %collective-permute-done.5.refs_3_, ...), custom_call_target="tpu_custom_call" | custom-call | tf_op jit(solution)/shard_map/pallas_call | solution.py:385
  19.5 0.2 collective-permute-start.6
  19.7 1.2 %collective-permute-done.6.got_ref = f32[4,72,128]{2,1,0:T(8,128)S(1)} collective-permute-done((f32[4,72,128]{2,1,0:T(8,128)S(1)}, f32[4,72,128]{2,1,0:T(8,128)S(1)}, u32[]{:S(2)}, u32[]{:S(2)}) %collective-permute-start.6) | collective-permute-done | bytes 147488 | tf_op jit(solution)/shard_map/ppermute | solution.py:337
  20.9 0.1 shard_map.89
  21.0 1.5 %collective-permute-start.7 = (s16[80,128]{1,0:T(8,128)(2,1)S(1)}, s16[80,128]{1,0:T(8,128)(2,1)S(1)}, u32[]{:S(2)}, u32[]{:S(2)}) collective-permute-start(s16[80,128]{1,0:T(8,128)(2,1)S(1)} %get-tuple-element.22), channel_id=1, source_target_pairs={{0,7},{1,6},{2,5},{3,4},{4,3},{5,2},{6,1},{7,0},{8,15},{9,14},{10,... | collective-permute-start | bytes 61448 | tf_op jit(solution)/shard_map/ppermute | solution.py:337
  22.6 0.3 %collective-permute-start.8 = (s16[80,128]{1,0:T(8,128)(2,1)S(1)}, s16[80,128]{1,0:T(8,128)(2,1)S(1)}, u32[]{:S(2)}, u32[]{:S(2)}) collective-permute-start(s16[80,128]{1,0:T(8,128)(2,1)S(1)} %get-tuple-element.23), channel_id=1, source_target_pairs={{0,5},{1,4},{2,7},{3,6},{4,1},{5,0},{6,3},{7,2},{8,13},{9,12},{10,... | collective-permute-start | bytes 61448 | tf_op jit(solution)/shard_map/ppermute | solution.py:337
  22.9 2.1 %collective-permute-start.9 = (s16[80,128]{1,0:T(8,128)(2,1)S(1)}, s16[80,128]{1,0:T(8,128)(2,1)S(1)}, u32[]{:S(2)}, u32[]{:S(2)}) collective-permute-start(s16[80,128]{1,0:T(8,128)(2,1)S(1)} %get-tuple-element.24), channel_id=1, source_target_pairs={{0,3},{1,2},{2,1},{3,0},{4,7},{5,6},{6,5},{7,4},{8,11},{9,10},{10,... | collective-permute-start | bytes 61448 | tf_op jit(solution)/shard_map/ppermute | solution.py:337
  25.0 1.2 %collective-permute-done.7.refs_1_ = s16[80,128]{1,0:T(8,128)(2,1)S(1)} collective-permute-done((s16[80,128]{1,0:T(8,128)(2,1)S(1)}, s16[80,128]{1,0:T(8,128)(2,1)S(1)}, u32[]{:S(2)}, u32[]{:S(2)}) %collective-permute-start.7) | collective-permute-done | bytes 20512 | tf_op jit(solution)/shard_map/ppermute | solution.py:337
  26.2 0.8 %collective-permute-done.8.refs_2_ = s16[80,128]{1,0:T(8,128)(2,1)S(1)} collective-permute-done((s16[80,128]{1,0:T(8,128)(2,1)S(1)}, s16[80,128]{1,0:T(8,128)(2,1)S(1)}, u32[]{:S(2)}, u32[]{:S(2)}) %collective-permute-start.8) | collective-permute-done | bytes 20512 | tf_op jit(solution)/shard_map/ppermute | solution.py:337
  27.0 0.1 collective-permute-done.9.refs_3_
  27.1 0.7 %shard_map.90 = (f32[8,8,128]{2,1,0:T(8,128)}, f32[1,8,8]{2,1,0:T(8,128)}) custom-call(f32[72,128]{1,0:T(8,128)S(1)} %get-tuple-element.21.refs_0_, s16[80,128]{1,0:T(8,128)(2,1)S(1)} %collective-permute-done.7.refs_1_, s16[80,128]{1,0:T(8,128)(2,1)S(1)} %collective-permute-done.8.refs_2_, s16[80,128]{1,0:T(8,128)(2,1)S(1)} %collective-permute-done.9.refs_3_, ...), custom_call_target="tpu_custom_call" | custom-call | tf_op jit(solution)/shard_map/pallas_call | solution.py:408
  (2 shorter events, 0.0 us)
Async XLA Ops:
  1.8 3.3 %collective-permute-start = (bf16[288,128]{1,0:T(8,128)(2,1)S(1)}, bf16[288,128]{1,0:T(8,128)(2,1)S(1)}, u32[]{:S(2)}, u32[]{:S(2)}) collective-permute-start(bf16[288,128]{1,0:T(8,128)(2,1)S(1)} %get-tuple-element.15), channel_id=1, source_target_pairs={{0,8},{1,9},{2,10},{3,11},{4,12},{5,13},{6,14},{7,15},{8,0},{9,1},... | collective-permute-start | bytes 221192 | tf_op jit(solution)/shard_map/ppermute | solution.py:346
  3.1 4.1 %collective-permute-start.1 = (bf16[288,128]{1,0:T(8,128)(2,1)S(1)}, bf16[288,128]{1,0:T(8,128)(2,1)S(1)}, u32[]{:S(2)}, u32[]{:S(2)}) collective-permute-start(bf16[288,128]{1,0:T(8,128)(2,1)S(1)} %get-tuple-element.16), channel_id=1, source_target_pairs={{0,1},{1,0},{2,3},{3,2},{4,5},{5,4},{6,7},{7,6},{8,16},{9,17},{10,... | collective-permute-start | bytes 221192 | tf_op jit(solution)/shard_map/ppermute | solution.py:346
  7.2 3.0 %collective-permute-start.2 = (f32[24,128]{1,0:T(8,128)S(1)}, f32[24,128]{1,0:T(8,128)S(1)}, u32[]{:S(2)}, u32[]{:S(2)}) collective-permute-start(f32[24,128]{1,0:T(8,128)S(1)} %shard_map.87), channel_id=1, source_target_pairs={{0,1},{1,0},{2,3},{3,2},{4,5},{5,4},{6,7},{7,6},{8,9},{9,8},{10,11... | collective-permute-start | bytes 36872 | tf_op jit(solution)/shard_map/ppermute | solution.py:337
  10.2 5.1 %collective-permute-start.5 = (f32[2,24,128]{2,1,0:T(8,128)S(1)}, f32[2,24,128]{2,1,0:T(8,128)S(1)}, u32[]{:S(2)}, u32[]{:S(2)}) collective-permute-start(f32[2,24,128]{2,1,0:T(8,128)S(1)} %pad_maximum_fusion.refs_0_), channel_id=1, source_target_pairs={{0,7},{1,6},{2,5},{3,4},{4,3},{5,2},{6,1},{7,0},{8,15},{9,14},{10,... | collective-permute-start | bytes 73736 | tf_op jit(solution)/shard_map/ppermute | solution.py:337
  13.7 4.2 %collective-permute-start.4 = (f32[2,24,128]{2,1,0:T(8,128)S(1)}, f32[2,24,128]{2,1,0:T(8,128)S(1)}, u32[]{:S(2)}, u32[]{:S(2)}) collective-permute-start(f32[2,24,128]{2,1,0:T(8,128)S(1)} %pad_maximum_fusion.refs_0_), channel_id=1, source_target_pairs={{0,5},{1,4},{2,7},{3,6},{4,1},{5,0},{6,3},{7,2},{8,13},{9,12},{10,... | collective-permute-start | bytes 73736 | tf_op jit(solution)/shard_map/ppermute | solution.py:337
  13.7 4.2 %collective-permute-start.3 = (f32[2,24,128]{2,1,0:T(8,128)S(1)}, f32[2,24,128]{2,1,0:T(8,128)S(1)}, u32[]{:S(2)}, u32[]{:S(2)}) collective-permute-start(f32[2,24,128]{2,1,0:T(8,128)S(1)} %pad_maximum_fusion.refs_0_), channel_id=1, source_target_pairs={{0,3},{1,2},{2,1},{3,0},{4,7},{5,6},{6,5},{7,4},{8,11},{9,10},{10,... | collective-permute-start | bytes 73736 | tf_op jit(solution)/shard_map/ppermute | solution.py:337
  19.5 1.4 %collective-permute-start.6 = (f32[4,72,128]{2,1,0:T(8,128)S(1)}, f32[4,72,128]{2,1,0:T(8,128)S(1)}, u32[]{:S(2)}, u32[]{:S(2)}) collective-permute-start(f32[4,72,128]{2,1,0:T(8,128)S(1)} %get-tuple-element.20), channel_id=1, source_target_pairs={{0,1},{1,0},{2,3},{3,2},{4,5},{5,4},{6,7},{7,6},{8,9},{9,8},{10,11... | collective-permute-start | bytes 442376 | tf_op jit(solution)/shard_map/ppermute | solution.py:337
  21.0 5.2 %collective-permute-start.7 = (s16[80,128]{1,0:T(8,128)(2,1)S(1)}, s16[80,128]{1,0:T(8,128)(2,1)S(1)}, u32[]{:S(2)}, u32[]{:S(2)}) collective-permute-start(s16[80,128]{1,0:T(8,128)(2,1)S(1)} %get-tuple-element.22), channel_id=1, source_target_pairs={{0,7},{1,6},{2,5},{3,4},{4,3},{5,2},{6,1},{7,0},{8,15},{9,14},{10,... | collective-permute-start | bytes 61448 | tf_op jit(solution)/shard_map/ppermute | solution.py:337
  22.6 4.4 %collective-permute-start.8 = (s16[80,128]{1,0:T(8,128)(2,1)S(1)}, s16[80,128]{1,0:T(8,128)(2,1)S(1)}, u32[]{:S(2)}, u32[]{:S(2)}) collective-permute-start(s16[80,128]{1,0:T(8,128)(2,1)S(1)} %get-tuple-element.23), channel_id=1, source_target_pairs={{0,5},{1,4},{2,7},{3,6},{4,1},{5,0},{6,3},{7,2},{8,13},{9,12},{10,... | collective-permute-start | bytes 61448 | tf_op jit(solution)/shard_map/ppermute | solution.py:337
  22.9 4.2 %collective-permute-start.9 = (s16[80,128]{1,0:T(8,128)(2,1)S(1)}, s16[80,128]{1,0:T(8,128)(2,1)S(1)}, u32[]{:S(2)}, u32[]{:S(2)}) collective-permute-start(s16[80,128]{1,0:T(8,128)(2,1)S(1)} %get-tuple-element.24), channel_id=1, source_target_pairs={{0,3},{1,2},{2,1},{3,0},{4,7},{5,6},{6,5},{7,4},{8,11},{9,10},{10,... | collective-permute-start | bytes 61448 | tf_op jit(solution)/shard_map/ppermute | solution.py:337

commit v7 on v6

v7 whole, which is shorter than its diff:
```python
import functools

import jax
import jax.numpy as jnp
from jax import lax
from jax.experimental import pallas as pl
from jax.experimental.pallas import tpu as pltpu
from jax.sharding import PartitionSpec as P

STEPS = 4
BAND = 2
LANES = 128
GROUP = 8
CODES, FULL, LEAST = 128, 32700.0, 1.2e-38
F32, BF16 = jnp.float32, jnp.bfloat16
VMEM = pl.BlockSpec(memory_space=pltpu.VMEM)
HBM = pl.BlockSpec(memory_space=pltpu.HBM)


def round_up(n, m):
    return -(-n // m) * m


def log2(n):
    assert n & (n - 1) == 0
    return n.bit_length() - 1


def iota(shape, axis):
    return lax.broadcasted_iota(jnp.int32, shape, axis)


def pieces(x):
    high = x.astype(BF16).astype(F32)
    rest = x - high
    middle = rest.astype(BF16).astype(F32)
    return high, middle, rest - middle


def stagger(x):
    return pltpu.roll(x, 0, 1, stride=GROUP, stride_axis=0)


def pick(x, place):
    if isinstance(place, int):
        shift = (-GROUP * place) % LANES
    else:
        shift = lax.rem(LANES - GROUP * place, LANES)
    rolled = pltpu.roll(x, shift, 1)
    own = iota(x.shape, 1) // GROUP == iota(x.shape, 0)
    return jnp.sum(jnp.where(own, rolled, 0.0), axis=0, keepdims=True)


def live_mask(count_ref, slots):
    tiles = count_ref.shape[1]
    count = jnp.broadcast_to(count_ref[...].astype(F32), (tiles, tiles))
    diagonal = iota((tiles, tiles), 0) == iota((tiles, tiles), 1)
    column = jnp.sum(jnp.where(diagonal, count, 0.0), axis=1, keepdims=True)
    return iota((tiles, slots), 1).astype(F32) < column


def copy_in(sources, targets, sems):
    moves = [pltpu.make_async_copy(x, y, sems.at[i]) for i, (x, y) in enumerate(zip(sources, targets))]
    for move in moves:
        move.start()
    return moves


def packet_kernel(
    value_hbm, cell_hbm, count_hbm, diff_hbm, packet, live_ref,
    value_ref, cell_ref, count_ref, diff_ref, wide, sems,
):
    moves = copy_in(
        (value_hbm, cell_hbm, count_hbm, diff_hbm), (value_ref, cell_ref, count_ref, diff_ref), sems
    )
    wide[...] = jnp.zeros_like(wide)
    for move in moves:
        move.wait()
    _, tiles, slots = value_ref.shape
    rows = diff_ref.shape[0]
    block = min(tiles, LANES // GROUP)
    live = live_mask(count_ref, slots)
    wide[0, :, 0:slots] = jnp.where(live, value_ref[0], 0.0)
    wide[1, :, 0:slots] = cell_ref[0].astype(F32)
    live_ref[...] = jnp.zeros_like(live_ref)
    live_ref[:, 0:slots] = jnp.where(live, 1.0, 0.0)
    packet[0:rows, :] = diff_ref[...]
    lines = [pick(stagger(wide[q, b : b + block, :]), 0) for q in range(2) for b in range(0, tiles, block)]
    if block * GROUP < LANES:
        lines = [lines[0] + pltpu.roll(lines[1], block * GROUP, 1)]
    packet[rows:, :] = jnp.zeros((packet.shape[0] - rows, LANES), F32)
    for i, line in enumerate(lines):
        packet[rows + i : rows + i + 1, :] = line


def member_kernel(
    ens_hbm, vertical_hbm, weights_hbm, turned_ref, factors_ref,
    ens_ref, vertical_ref, weights_ref, tall, sems,
):
    moves = copy_in((vertical_hbm, weights_hbm, ens_hbm), (vertical_ref, weights_ref, ens_ref), sems)
    for move in moves:
        move.wait()
    _, levels, rows, columns = ens_ref.shape
    for t in range(columns // LANES):
        at = slice(t * LANES, (t + 1) * LANES)
        tall[t] = ens_ref[0, :, :, at].astype(F32).reshape(levels * rows, LANES)
        for r in range(0, rows, 2):
            both = [tall[t, pl.ds(r + i, levels, stride=rows), :] for i in range(2)]
            turned_ref[t, r * levels : (r + 2) * levels, :] = jnp.concatenate(both, axis=0).astype(BF16)
    vertical = vertical_ref[...] * weights_ref[lax.axis_index("tx")]
    gap = iota((levels, levels), 1) - iota((levels, levels), 0)
    for i in range(2 * BAND + 1):
        factor = jnp.sum(jnp.where(gap == i - BAND, vertical, 0.0), axis=1, keepdims=True)
        factors_ref[i] = jnp.broadcast_to(factor, (levels, LANES))


def lines_of(staggered, place, tiles):
    size = staggered[0][0].shape[0]
    groups = LANES // GROUP
    return jnp.concatenate([pick(part, place % groups) for part in staggered[place // groups]], axis=1)


def spread(line_value, line_key, hits, count, first):
    key = line_key - first
    on = iota((count, line_key.shape[1]), 0).astype(F32) == key
    stacked = jnp.concatenate([jnp.where(on, piece, 0.0) for piece in pieces(line_value)], axis=0)
    found = lax.dot_general(
        stacked.astype(BF16), hits, (((1,), (1,)), ((), ())), preferred_element_type=F32
    )
    return found[0:count] + found[count : 2 * count] + found[2 * count :]


def hits_of(line_column):
    shape = (LANES, line_column.shape[1])
    return jnp.where(iota(shape, 0).astype(F32) == line_column, 1.0, 0.0).astype(BF16)


def gather_kernel(near, rows, lines, levels, *refs):
    got, (turned_ref, d_ref, slots_ref, hits_ref, a_ref, b_ref, packs) = refs[:near], refs[near:]
    tiles = packs.shape[0]
    size = min(tiles, LANES // GROUP)
    me, even = lax.axis_index("tx"), lax.rem(lax.axis_index("ty"), 2) == 0
    chip, core = me // 2, lax.rem(me, 2)
    for far, ref in enumerate(got):
        for side in range(2):
            packs[2 * (chip ^ far) + (core ^ side ^ (far > 0))] = ref[side]
    values, keys, columns = [], [], []
    for i in range(lines):
        x = packs[:, rows + i, :]
        cell = x.astype(jnp.int32)
        flat = lax.shift_right_logical(cell, log2(LANES))
        key = (flat & (rows - 1)) * levels + lax.shift_right_logical(flat, log2(rows))
        for out, part in ((values, x), (keys, key.astype(F32)), (columns, (cell & (LANES - 1)).astype(F32))):
            out.append([stagger(part[q : q + size]) for q in range(0, tiles, size)])
    deep = STEPS - 1
    for t in range(tiles):
        value = lines_of(values, t, tiles)
        key, column = lines_of(keys, tiles + t, tiles), lines_of(columns, tiles + t, tiles)
        hits = hits_of(column)
        hits_ref[t] = hits
        found = jnp.dot(turned_ref[t], hits, preferred_element_type=F32)
        on = iota(found.shape, 0).astype(F32) == key
        product = value * jnp.sum(jnp.where(on, found, 0.0), axis=0, keepdims=True)
        d = packs[t, 0:rows, :]
        d_ref[:, t * LANES : (t + 1) * LANES] = d
        low = pltpu.roll(d, deep, 0)
        for out, part in ((a_ref, jnp.where(even, low, d)), (b_ref, jnp.where(even, d, low))):
            out[t, 0:rows, :] = part
            for i, line in enumerate((product, key, column)):
                for q in range(tiles // size):
                    out[t, deep + 3 * q + i : deep + 3 * q + i + 1, :] = line[:, q * LANES : (q + 1) * LANES]
        for i, line in enumerate((product, key)):
            slots_ref[t, i : i + 1, :] = line


def own_kernel(slots_ref, hits_ref, start_ref):
    count = start_ref.shape[0]
    for t in range(slots_ref.shape[0]):
        at = slice(t * LANES, (t + 1) * LANES)
        start_ref[:, at] = spread(slots_ref[t, 0:1, :], slots_ref[t, 1:2, :], hits_ref[t], count, 0.0)


def main_kernel(
    rows, levels, start_ref, d_ref, slots_ref, hits_ref, turned_ref, a_ref, b_ref, factors_ref, mine_ref, other_ref,
    member, d_all, keep, first, second, made, back,
):
    tiles = hits_ref.shape[0]
    block = min(tiles, LANES // GROUP)
    columns = tiles * LANES
    band, last, me = lax.axis_index("ty"), lax.axis_size("ty") - 1, lax.axis_index("tx")
    chip, core = me // 2, lax.rem(me, 2)
    even = lax.rem(band, 2) == 0
    half, own, deep = STEPS * levels, rows * levels, STEPS - 1

    first[half : half + own, 0:columns] = start_ref[...]
    d_all[STEPS : STEPS + rows, :] = d_ref[...]
    for t in range(tiles):
        at = slice(t * LANES, (t + 1) * LANES)
        member[:, at] = turned_ref[t].astype(F32)
        got_a, got_b = a_ref[t], b_ref[t]
        above = jnp.where(band == 0, 0.0, jnp.where(even, got_b, got_a))
        below = jnp.where(band == last, 0.0, jnp.where(even, got_a, got_b))
        for got, begin, base, d_begin in ((above, 0, own - half, 1), (below, half + own, 0, STEPS + rows)):
            d_all[d_begin : d_begin + deep, at] = got[0:deep]
            product, key, column = (
                jnp.concatenate([got[deep + 3 * q + i : deep + 3 * q + i + 1] for q in range(tiles // block)], axis=1)
                for i in range(3)
            )
            first[begin : begin + half, at] = spread(product, key, hits_of(column), half, float(base))

    first[:, columns:] = jnp.zeros((first.shape[0], LANES), F32)
    second[:, columns:] = jnp.zeros((second.shape[0], LANES), F32)
    keep[...] = 1.0 - 4.0 * d_all[...]
    factors = [(i - BAND, factors_ref[i]) for i in range(2 * BAND + 1)]
    source, target = first, second
    for step in range(STEPS):
        for r in range(step + 1, 2 * STEPS + rows - 1 - step):
            mid = source[r * levels : (r + 1) * levels, :]
            beside = (
                source[(r - 1) * levels : r * levels, 0:columns]
                + source[(r + 1) * levels : (r + 2) * levels, 0:columns]
                + pltpu.roll(mid, 1, 1)[:, 0:columns]
                + pltpu.roll(mid, columns + LANES - 1, 1)[:, 0:columns]
            )
            d, c = (jnp.broadcast_to(x[r : r + 1, :], (levels, columns)) for x in (d_all, keep))
            x = c * mid[:, 0:columns] + d * beside
            if step < STEPS - 1:
                target[r * levels : (r + 1) * levels, 0:columns] = x
                continue
            row = slice((r - STEPS) * levels, (r - STEPS + 1) * levels)
            for t in range(tiles):
                at = slice(t * LANES, (t + 1) * LANES)
                mixed = sum(f * (pltpu.roll(x[:, at], -o % levels, 0) if o else x[:, at]) for o, f in factors)
                made[t, row, :] = mixed * member[row, at]
        source, target = target, source

    for t in range(tiles):
        stacked = jnp.concatenate(pieces(made[t]), axis=0).astype(BF16)
        found = jnp.dot(stacked, hits_ref[t], preferred_element_type=F32)
        found = found[0:own] + found[own : 2 * own] + found[2 * own :]
        on = iota(found.shape, 0).astype(F32) == slots_ref[t, 1:2, :]
        line = jnp.sum(jnp.where(on, found, 0.0), axis=0, keepdims=True)
        for q in range(tiles // block):
            back[q, t : t + 1, :] = line[:, q * LANES : (q + 1) * LANES]
    for z in range(mine_ref.shape[0]):
        for side, out in enumerate((mine_ref, other_ref)):
            out[z, 0:own, :] = made[2 * z + (core ^ side ^ (chip != z).astype(jnp.int32))]
            out[z, own:, :] = back[2 * z // block]


def scale_of(code):
    return jnp.exp2(code.astype(F32) * (1.0 / CODES))


def pair_kernel(split, mine_ref, got_ref, near_ref, *outs):
    chip = lax.axis_index("tx") // 2
    near_ref[...] = mine_ref[chip] + got_ref[chip]
    for far, out in enumerate(outs, 1):
        x = mine_ref[chip ^ far] + got_ref[chip ^ far]
        whole, codes = [], []
        for part in (x[0:split], x[split:]):
            largest = jnp.maximum(jnp.max(jnp.abs(part), axis=0, keepdims=True), LEAST)
            code = jnp.minimum(jnp.ceil(jnp.log2(largest) * CODES).astype(jnp.int32), CODES * 128 - 1)
            sized = jnp.clip(part * (1.0 / scale_of(code)), -1.0, 1.0)
            whole.append(jnp.floor(sized * FULL + 0.5).astype(jnp.int32))
            codes.append(code)
        rest = out.shape[0] - x.shape[0]
        row = iota((rest, LANES), 0)
        tail = jnp.where(row == 0, codes[0], jnp.where(row == 1, codes[1], 0))
        out[...] = jnp.concatenate([*whole, tail], axis=0).astype(jnp.int16)


def final_kernel(split, *refs):
    got, (live_ref, inc_ref, proj_ref, total) = refs[:-4], refs[-4:]
    levels, rows, _ = inc_ref.shape
    _, tiles, slots = proj_ref.shape
    size = got[0].shape[0]
    top, low = got[0][0:split, :], got[0][split:, :]
    for ref in got[1:]:
        x = ref[...].astype(jnp.int32)
        sent = x[0:size].astype(F32) * (1.0 / FULL)
        top = top + sent[0:split] * scale_of(x[size : size + 1])
        low = low + sent[split:] * scale_of(x[size + 1 : size + 2])
    total[...] = top
    for level in range(levels):
        inc_ref[level] = total[pl.ds(level, rows, stride=levels), :]
    place = lax.rem(lax.axis_index("tx"), LANES // GROUP)
    lines = pltpu.roll(low, lax.rem(LANES - GROUP * place, LANES), 1)
    proj_ref[0] = jnp.where(live_ref[:, 0:slots] > 0.0, lines[:, 0:slots], 0.0)


def call(kernel, out_shape, ins, scratch, flops=0, moved=0):
    return pl.pallas_call(
        kernel,
        out_shape=out_shape,
        in_specs=ins,
        out_specs=jax.tree.map(lambda _: VMEM, out_shape),
        scratch_shapes=scratch,
        compiler_params=pltpu.CompilerParams(vmem_limit_bytes=48 << 20),
        cost_estimate=pl.CostEstimate(flops=flops, bytes_accessed=moved, transcendentals=0),
    )


def shards(ensemble, diffusivity, vertical, weights, obs_value, obs_cell, obs_count):
    _, levels, rows, columns = ensemble.shape
    tiles, slots = obs_value.shape[1:]
    chips = tiles // 2
    bands = lax.axis_size("ty")
    assert diffusivity.shape == (rows, LANES) and slots == GROUP and rows == 2 * STEPS
    block = min(tiles, LANES // GROUP)
    shape = jax.ShapeDtypeStruct
    lines = -(-2 * tiles * GROUP // LANES)
    half, own = STEPS * levels, rows * levels
    height, halo_height = round_up(rows + lines, 8), round_up(max(rows, STEPS - 1 + 3 * (tiles // block)), 8)
    lanes = tiles // block * LANES

    def in_hbm(*arrays):
        return [pltpu.with_memory_space_constraint(x, pltpu.HBM) for x in arrays]

    def swap(x, far):
        return lax.ppermute(x, "tx", [(i, i ^ far) for i in range(tiles)])

    def swap_bands(x, low):
        mate = [i ^ 1 if low else i + 1 if i % 2 else i - 1 for i in range(bands)]
        pairs = [
            (i * tiles + k, mate[i] * tiles + k if 0 <= mate[i] < bands else i * tiles + (k ^ 1))
            for i in range(bands)
            for k in range(tiles)
        ]
        return lax.ppermute(x, ("ty", "tx"), pairs)

    packet, live = call(
        packet_kernel,
        (shape((height, LANES), F32), shape((tiles, LANES), F32)),
        [HBM] * 4,
        [
            pltpu.VMEM(obs_value.shape, F32),
            pltpu.VMEM(obs_cell.shape, jnp.int32),
            pltpu.VMEM(obs_count.shape, jnp.int32),
            pltpu.VMEM(diffusivity.shape, F32),
            pltpu.VMEM((2, tiles, LANES), F32),
            pltpu.SemaphoreType.DMA((4,)),
        ],
    )(*in_hbm(obs_value, obs_cell, obs_count, diffusivity))
    turned, factors = call(
        member_kernel,
        (shape((tiles, own, LANES), BF16), shape((2 * BAND + 1, levels, LANES), F32)),
        [HBM] * 3,
        [
            pltpu.VMEM(ensemble.shape, BF16),
            pltpu.VMEM(vertical.shape, F32),
            pltpu.SMEM(weights.shape, F32),
            pltpu.VMEM((tiles, own, LANES), F32),
            pltpu.SemaphoreType.DMA((3,)),
        ],
        1000000,
        1000000,
    )(*in_hbm(ensemble, vertical, weights))

    pair = jnp.stack([packet, swap(packet, 1)])
    row = [pair] + [swap(pair, 2 * far + 1) for far in range(1, chips)]
    halo = shape((tiles, halo_height, LANES), F32)
    d_row, slots_row, hits, to_a, to_b = call(
        functools.partial(gather_kernel, chips, rows, lines, levels),
        (
            shape((rows, columns), F32),
            shape((tiles, 8, lanes), F32),
            shape((tiles, LANES, lanes), BF16),
            halo,
            halo,
        ),
        [VMEM] * (chips + 1),
        [pltpu.VMEM((tiles, height, LANES), F32)],
    )(*row, turned)
    from_a, from_b = swap_bands(to_a, True), swap_bands(to_b, False)
    start = call(own_kernel, shape((own, columns), F32), [VMEM] * 2, [], 1000000, 1000000)(slots_row, hits)

    chunk = own + tiles
    mine, other = call(
        functools.partial(main_kernel, rows, levels),
        (shape((chips, chunk, LANES), F32), shape((chips, chunk, LANES), F32)),
        [VMEM] * 8,
        [
            pltpu.VMEM((own, columns), F32),
            pltpu.VMEM((2 * STEPS + rows, columns), F32),
            pltpu.VMEM((2 * STEPS + rows, columns), F32),
            pltpu.VMEM((2 * half + own, columns + LANES), F32),
            pltpu.VMEM((2 * half + own, columns + LANES), F32),
            pltpu.VMEM((tiles, own, LANES), F32),
            pltpu.VMEM((tiles // block, tiles, LANES), F32),
        ],
    )(start, d_row, slots_row, hits, turned, from_a, from_b, factors)

    coded = shape((round_up(chunk + 2, 16), LANES), jnp.int16)
    sums = call(
        functools.partial(pair_kernel, own), (shape((chunk, LANES), F32), *[coded] * (chips - 1)), [VMEM] * 2, []
    )(mine, swap(other, 1))
    sums = [sums[0]] + [swap(sums[far], 2 * far + 1) for far in range(1, chips)]
    return call(
        functools.partial(final_kernel, own),
        (shape((levels, rows, LANES), F32), shape((1, tiles, slots), F32)),
        [VMEM] * (chips + 1),
        [pltpu.VMEM((own, LANES), F32)],
    )(sums[0], *sums[:0:-1], live)


def solution(mesh):
    placed = (
        P("tx", None, "ty", None),
        P("ty", "tx"),
        P(),
        P(),
        P(("ty", "tx"), None, None),
        P(("ty", "tx"), None, None),
        P(("ty", "tx"), None),
    )
    return jax.shard_map(
        shards,
        mesh=mesh,
        in_specs=placed,
        out_specs=(P(None, "ty", "tx"), P(("ty", "tx"), None, None)),
        check_vma=False,
    )
```

time: 28 us -> 27.2 us (0.971)
  waiting for transfers between devices: 11.9 us -> 9.48 us
  Pallas kernels: 3.54 us -> 4.72 us
  starting transfers between devices: 11.7 us -> 12.1 us
    ppermute x8, waiting for transfers between devices: 7.83 us -> 6.3 us  [swap(): return lax.ppermute(x, 'tx', [(i, i ^ far) for i in range(tiles)])]
    pallas_call x3 -> x5, Pallas kernels: 2.77 us -> 3.95 us  [the longest x1 1.27 us: shards(): call(functools.partial(main_kernel, rows, levels), (shape((chips, chunk,...]
    ppermute x2, waiting for transfers between devices: 4.08 us -> 3.17 us  [swap_bands(): return lax.ppermute(x, ('ty', 'tx'), pairs)]
  transfers between devices with their start and end apart: 10 -> 10, of which waited for: 9 -> 8; matrix products, arithmetic and copies ran while one was open for 0% -> 0% of each run, Pallas kernels for 0% -> 5%
where the time goes in v7:
time: 27.2 us; the launch traced here: 26.9 us
  starting transfers between devices  12.1 us (44%)
  waiting for transfers between devices  9.48 us (35%)
  Pallas kernels  4.72 us (17%)
  between operations  0.67 us (2%)
    ppermute x8, starting transfers between devices, swap(): return lax.ppermute(x, 'tx', [(i, i ^ far) for i in range(tiles)])  10.6 us
    ppermute x8, waiting for transfers between devices, swap(): return lax.ppermute(x, 'tx', [(i, i ^ far) for i in range(tiles)])  6.3 us
    ppermute x2, waiting for transfers between devices, swap_bands(): return lax.ppermute(x, ('ty', 'tx'), pairs)  3.17 us
    ppermute x2, starting transfers between devices, swap_bands(): return lax.ppermute(x, ('ty', 'tx'), pairs)  1.47 us
    pallas_call x1, Pallas kernels, shards(): call(functools.partial(main_kernel, rows, levels), (shape((chips, chunk,...  1.27 us
    pallas_call x1, Pallas kernels, shards(): call(member_kernel, (shape((tiles, own, LANES), BF16), shape((2 * BAND +...  1.08 us
    pallas_call x1, Pallas kernels, shards(): call(packet_kernel, (shape((height, LANES), F32), shape((tiles, LANES), F...  0.93 us
    pallas_call x1, Pallas kernels, shards(): call(functools.partial(final_kernel, own), (shape((levels, rows, LANES),...  0.68 us
  transfers between devices with their start and end apart: 10, of which 8 were waited for; matrix products, arithmetic and copies ran while one was open for 0% of the time, Pallas kernels for 5%

profile of v7, /device:TPU:5, one launch (start us, length us, event | category | flops | bytes accessed | tf_op | source)
XLA Modules:
  0.0 26.9 jit_solution(15660306180259918319)
XLA Ops:
  0.6 0.9 %shard_map.86 = (f32[16,128]{1,0:T(8,128)S(1)}, f32[8,128]{1,0:T(8,128)S(1)}) custom-call(f32[1,8,8]{2,1,0:T(8,128)} %value_hbm.1, s32[1,8,8]{2,1,0:T(8,128)} %cell_hbm.1, s32[1,8]{1,0:T(1,128)} %count_hbm.1, f32[8,128]{1,0:T(8,128)} %diff_hbm.1), custom_call_target="tpu_custom_call" | custom-call | tf_op jit(solution)/shard_map/pallas_call | solution.py:332
  1.6 0.7 %collective-permute-start = (f32[16,128]{1,0:T(8,128)S(1)}, f32[16,128]{1,0:T(8,128)S(1)}, u32[]{:S(2)}, u32[]{:S(2)}) collective-permute-start(f32[16,128]{1,0:T(8,128)S(1)} %get-tuple-element.17), channel_id=1, source_target_pairs={{0,1},{1,0},{2,3},{3,2},{4,5},{5,4},{6,7},{7,6},{8,9},{9,8},{10,11... | collective-permute-start | bytes 24584 | tf_op jit(solution)/shard_map/ppermute | solution.py:321
  2.3 0.8 %collective-permute-done = f32[16,128]{1,0:T(8,128)S(1)} collective-permute-done((f32[16,128]{1,0:T(8,128)S(1)}, f32[16,128]{1,0:T(8,128)S(1)}, u32[]{:S(2)}, u32[]{:S(2)}) %collective-permute-start) | collective-permute-done | bytes 8224 | tf_op jit(solution)/shard_map/ppermute | solution.py:321
  3.1 3.6 %collective-permute-start.3 = (f32[2,16,128]{2,1,0:T(8,128)S(1)}, f32[2,16,128]{2,1,0:T(8,128)S(1)}, u32[]{:S(2)}, u32[]{:S(2)}) collective-permute-start(f32[2,16,128]{2,1,0:T(8,128)S(1)} %pad_maximum_fusion.refs_0_), channel_id=1, source_target_pairs={{0,7},{1,6},{2,5},{3,4},{4,3},{5,2},{6,1},{7,0},{8,15},{9,14},{10,... | collective-permute-start | bytes 49160 | tf_op jit(solution)/shard_map/ppermute | solution.py:321
  6.7 0.0 collective-permute-start.2
  6.7 0.5 %collective-permute-start.1 = (f32[2,16,128]{2,1,0:T(8,128)S(1)}, f32[2,16,128]{2,1,0:T(8,128)S(1)}, u32[]{:S(2)}, u32[]{:S(2)}) collective-permute-start(f32[2,16,128]{2,1,0:T(8,128)S(1)} %pad_maximum_fusion.refs_0_), channel_id=1, source_target_pairs={{0,3},{1,2},{2,1},{3,0},{4,7},{5,6},{6,5},{7,4},{8,11},{9,10},{10,... | collective-permute-start | bytes 49160 | tf_op jit(solution)/shard_map/ppermute | solution.py:321
  7.2 1.1 %shard_map.87 = (bf16[8,64,128]{2,1,0:T(8,128)(2,1)S(1)}, f32[5,8,128]{2,1,0:T(8,128)S(1)}) custom-call(bf16[1,8,8,1024]{3,2,1,0:T(8,128)(2,1)} %ens_hbm.1, f32[8,8]{1,0:T(8,128)} %vertical_hbm.1, f32[8]{0:T(128)} %weights_hbm.1), custom_call_target="tpu_custom_call" | custom-call | flops 1000000 | bytes 1000000 | tf_op jit(solution)/shard_map/pallas_call | solution.py:345
  8.3 0.0 collective-permute-done.3.refs_3_
  8.3 2.5 %collective-permute-done.2.refs_2_ = f32[2,16,128]{2,1,0:T(8,128)S(1)} collective-permute-done((f32[2,16,128]{2,1,0:T(8,128)S(1)}, f32[2,16,128]{2,1,0:T(8,128)S(1)}, u32[]{:S(2)}, u32[]{:S(2)}) %collective-permute-start.2) | collective-permute-done | bytes 16416 | tf_op jit(solution)/shard_map/ppermute | solution.py:321
  10.8 0.0 collective-permute-done.1.refs_1_
  10.8 0.4 %shard_map.88 = (f32[8,1024]{1,0:T(8,128)S(1)}, f32[8,8,128]{2,1,0:T(8,128)S(1)}, bf16[8,128,128]{2,1,0:T(8,128)(2,1)S(1)}, f32[8,8,128]{2,1,0:T(8,128)S(1)}, f32[8,8,128]{2,1,0:T(8,128)S(1)}) custom-call(f32[2,16,128]{2,1,0:T(8,128)S(1)} %pad_maximum_fusion.refs_0_, f32[2,16,128]{2,1,0:T(8,128)S(1)} %collective-permute-done.1.refs_1_, ...), custom_call_target="tpu_custom_call" | custom-call | tf_op jit(solution)/shard_map/pallas_call | solution.py:363
  11.1 1.3 %collective-permute-start.4 = (f32[8,8,128]{2,1,0:T(8,128)S(1)}, f32[8,8,128]{2,1,0:T(8,128)S(1)}, u32[]{:S(2)}, u32[]{:S(2)}) collective-permute-start(f32[8,8,128]{2,1,0:T(8,128)S(1)} %get-tuple-element.22), channel_id=1, source_target_pairs={{0,8},{1,9},{2,10},{3,11},{4,12},{5,13},{6,14},{7,15},{8,0},{9,1},... | collective-permute-start | bytes 98312 | tf_op jit(solution)/shard_map/ppermute | solution.py:330
  12.4 0.2 collective-permute-start.5
  12.6 0.3 %shard_map.89.start_ref = f32[64,1024]{1,0:T(8,128)S(1)} custom-call(f32[8,8,128]{2,1,0:T(8,128)S(1)} %get-tuple-element.19.slots_ref, bf16[8,128,128]{2,1,0:T(8,128)(2,1)S(1)} %get-tuple-element.20.hits_ref), custom_call_target="tpu_custom_call" | custom-call | flops 1000000 | bytes 1000000 | tf_op jit(solution)/shard_map/pallas_call | solution.py:376
  12.9 1.1 %collective-permute-done.4.a_ref = f32[8,8,128]{2,1,0:T(8,128)S(1)} collective-permute-done((f32[8,8,128]{2,1,0:T(8,128)S(1)}, f32[8,8,128]{2,1,0:T(8,128)S(1)}, u32[]{:S(2)}, u32[]{:S(2)}) %collective-permute-start.4) | collective-permute-done | bytes 32800 | tf_op jit(solution)/shard_map/ppermute | solution.py:330
  14.0 2.1 %collective-permute-done.5.b_ref = f32[8,8,128]{2,1,0:T(8,128)S(1)} collective-permute-done((f32[8,8,128]{2,1,0:T(8,128)S(1)}, f32[8,8,128]{2,1,0:T(8,128)S(1)}, u32[]{:S(2)}, u32[]{:S(2)}) %collective-permute-start.5) | collective-permute-done | bytes 32800 | tf_op jit(solution)/shard_map/ppermute | solution.py:330
  16.1 1.3 %shard_map.90 = (f32[4,72,128]{2,1,0:T(8,128)S(1)}, f32[4,72,128]{2,1,0:T(8,128)S(1)}) custom-call(f32[64,1024]{1,0:T(8,128)S(1)} %shard_map.89.start_ref, f32[8,1024]{1,0:T(8,128)S(1)} %get-tuple-element.21.d_ref, f32[8,8,128]{2,1,0:T(8,128)S(1)} %get-tuple-element.19.slots_ref, bf16[8,128,128]{2,1,0:T(8,128)(2,1)S(1)} %get-tuple-element.20.hits_ref, ...), custom_call_target="tpu_custom_call" | custom-call | tf_op jit(solution)/shard_map/pallas_call | solution.py:379
  17.4 1.7 %collective-permute-start.6 = (f32[4,72,128]{2,1,0:T(8,128)S(1)}, f32[4,72,128]{2,1,0:T(8,128)S(1)}, u32[]{:S(2)}, u32[]{:S(2)}) collective-permute-start(f32[4,72,128]{2,1,0:T(8,128)S(1)} %get-tuple-element.26), channel_id=1, source_target_pairs={{0,1},{1,0},{2,3},{3,2},{4,5},{5,4},{6,7},{7,6},{8,9},{9,8},{10,11... | collective-permute-start | bytes 442376 | tf_op jit(solution)/shard_map/ppermute | solution.py:321
  19.0 1.0 %collective-permute-done.6.got_ref = f32[4,72,128]{2,1,0:T(8,128)S(1)} collective-permute-done((f32[4,72,128]{2,1,0:T(8,128)S(1)}, f32[4,72,128]{2,1,0:T(8,128)S(1)}, u32[]{:S(2)}, u32[]{:S(2)}) %collective-permute-start.6) | collective-permute-done | bytes 147488 | tf_op jit(solution)/shard_map/ppermute | solution.py:321
  20.0 0.1 shard_map.91
  20.1 1.7 %collective-permute-start.7 = (s16[80,128]{1,0:T(8,128)(2,1)S(1)}, s16[80,128]{1,0:T(8,128)(2,1)S(1)}, u32[]{:S(2)}, u32[]{:S(2)}) collective-permute-start(s16[80,128]{1,0:T(8,128)(2,1)S(1)} %get-tuple-element.28), channel_id=1, source_target_pairs={{0,7},{1,6},{2,5},{3,4},{4,3},{5,2},{6,1},{7,0},{8,15},{9,14},{10,... | collective-permute-start | bytes 61448 | tf_op jit(solution)/shard_map/ppermute | solution.py:321
  21.8 0.4 %collective-permute-start.8 = (s16[80,128]{1,0:T(8,128)(2,1)S(1)}, s16[80,128]{1,0:T(8,128)(2,1)S(1)}, u32[]{:S(2)}, u32[]{:S(2)}) collective-permute-start(s16[80,128]{1,0:T(8,128)(2,1)S(1)} %get-tuple-element.29), channel_id=1, source_target_pairs={{0,5},{1,4},{2,7},{3,6},{4,1},{5,0},{6,3},{7,2},{8,13},{9,12},{10,... | collective-permute-start | bytes 61448 | tf_op jit(solution)/shard_map/ppermute | solution.py:321
  22.2 2.1 %collective-permute-start.9 = (s16[80,128]{1,0:T(8,128)(2,1)S(1)}, s16[80,128]{1,0:T(8,128)(2,1)S(1)}, u32[]{:S(2)}, u32[]{:S(2)}) collective-permute-start(s16[80,128]{1,0:T(8,128)(2,1)S(1)} %get-tuple-element.30), channel_id=1, source_target_pairs={{0,3},{1,2},{2,1},{3,0},{4,7},{5,6},{6,5},{7,4},{8,11},{9,10},{10,... | collective-permute-start | bytes 61448 | tf_op jit(solution)/shard_map/ppermute | solution.py:321
  24.3 0.9 %collective-permute-done.7.refs_1_ = s16[80,128]{1,0:T(8,128)(2,1)S(1)} collective-permute-done((s16[80,128]{1,0:T(8,128)(2,1)S(1)}, s16[80,128]{1,0:T(8,128)(2,1)S(1)}, u32[]{:S(2)}, u32[]{:S(2)}) %collective-permute-start.7) | collective-permute-done | bytes 20512 | tf_op jit(solution)/shard_map/ppermute | solution.py:321
  25.2 0.7 %collective-permute-done.8.refs_2_ = s16[80,128]{1,0:T(8,128)(2,1)S(1)} collective-permute-done((s16[80,128]{1,0:T(8,128)(2,1)S(1)}, s16[80,128]{1,0:T(8,128)(2,1)S(1)}, u32[]{:S(2)}, u32[]{:S(2)}) %collective-permute-start.8) | collective-permute-done | bytes 20512 | tf_op jit(solution)/shard_map/ppermute | solution.py:321
  25.9 0.3 %collective-permute-done.9.refs_3_ = s16[80,128]{1,0:T(8,128)(2,1)S(1)} collective-permute-done((s16[80,128]{1,0:T(8,128)(2,1)S(1)}, s16[80,128]{1,0:T(8,128)(2,1)S(1)}, u32[]{:S(2)}, u32[]{:S(2)}) %collective-permute-start.9) | collective-permute-done | bytes 20512 | tf_op jit(solution)/shard_map/ppermute | solution.py:321
  26.3 0.7 %shard_map.92 = (f32[8,8,128]{2,1,0:T(8,128)}, f32[1,8,8]{2,1,0:T(8,128)}) custom-call(f32[72,128]{1,0:T(8,128)S(1)} %get-tuple-element.27.refs_0_, s16[80,128]{1,0:T(8,128)(2,1)S(1)} %collective-permute-done.7.refs_1_, s16[80,128]{1,0:T(8,128)(2,1)S(1)} %collective-permute-done.8.refs_2_, s16[80,128]{1,0:T(8,128)(2,1)S(1)} %collective-permute-done.9.refs_3_, ...), custom_call_target="tpu_custom_call" | custom-call | tf_op jit(solution)/shard_map/pallas_call | solution.py:399
  (1 shorter events, 0.0 us)
Async XLA Ops:
  1.6 1.6 %collective-permute-start = (f32[16,128]{1,0:T(8,128)S(1)}, f32[16,128]{1,0:T(8,128)S(1)}, u32[]{:S(2)}, u32[]{:S(2)}) collective-permute-start(f32[16,128]{1,0:T(8,128)S(1)} %get-tuple-element.17), channel_id=1, source_target_pairs={{0,1},{1,0},{2,3},{3,2},{4,5},{5,4},{6,7},{7,6},{8,9},{9,8},{10,11... | collective-permute-start | bytes 24584 | tf_op jit(solution)/shard_map/ppermute | solution.py:321
  3.1 5.1 %collective-permute-start.3 = (f32[2,16,128]{2,1,0:T(8,128)S(1)}, f32[2,16,128]{2,1,0:T(8,128)S(1)}, u32[]{:S(2)}, u32[]{:S(2)}) collective-permute-start(f32[2,16,128]{2,1,0:T(8,128)S(1)} %pad_maximum_fusion.refs_0_), channel_id=1, source_target_pairs={{0,7},{1,6},{2,5},{3,4},{4,3},{5,2},{6,1},{7,0},{8,15},{9,14},{10,... | collective-permute-start | bytes 49160 | tf_op jit(solution)/shard_map/ppermute | solution.py:321
  6.7 4.1 %collective-permute-start.2 = (f32[2,16,128]{2,1,0:T(8,128)S(1)}, f32[2,16,128]{2,1,0:T(8,128)S(1)}, u32[]{:S(2)}, u32[]{:S(2)}) collective-permute-start(f32[2,16,128]{2,1,0:T(8,128)S(1)} %pad_maximum_fusion.refs_0_), channel_id=1, source_target_pairs={{0,5},{1,4},{2,7},{3,6},{4,1},{5,0},{6,3},{7,2},{8,13},{9,12},{10,... | collective-permute-start | bytes 49160 | tf_op jit(solution)/shard_map/ppermute | solution.py:321
  6.7 4.1 %collective-permute-start.1 = (f32[2,16,128]{2,1,0:T(8,128)S(1)}, f32[2,16,128]{2,1,0:T(8,128)S(1)}, u32[]{:S(2)}, u32[]{:S(2)}) collective-permute-start(f32[2,16,128]{2,1,0:T(8,128)S(1)} %pad_maximum_fusion.refs_0_), channel_id=1, source_target_pairs={{0,3},{1,2},{2,1},{3,0},{4,7},{5,6},{6,5},{7,4},{8,11},{9,10},{10,... | collective-permute-start | bytes 49160 | tf_op jit(solution)/shard_map/ppermute | solution.py:321
  11.1 2.8 %collective-permute-start.4 = (f32[8,8,128]{2,1,0:T(8,128)S(1)}, f32[8,8,128]{2,1,0:T(8,128)S(1)}, u32[]{:S(2)}, u32[]{:S(2)}) collective-permute-start(f32[8,8,128]{2,1,0:T(8,128)S(1)} %get-tuple-element.22), channel_id=1, source_target_pairs={{0,8},{1,9},{2,10},{3,11},{4,12},{5,13},{6,14},{7,15},{8,0},{9,1},... | collective-permute-start | bytes 98312 | tf_op jit(solution)/shard_map/ppermute | solution.py:330
  12.4 3.7 %collective-permute-start.5 = (f32[8,8,128]{2,1,0:T(8,128)S(1)}, f32[8,8,128]{2,1,0:T(8,128)S(1)}, u32[]{:S(2)}, u32[]{:S(2)}) collective-permute-start(f32[8,8,128]{2,1,0:T(8,128)S(1)} %get-tuple-element.23), channel_id=1, source_target_pairs={{0,1},{1,0},{2,3},{3,2},{4,5},{5,4},{6,7},{7,6},{8,16},{9,17},{10,... | collective-permute-start | bytes 98312 | tf_op jit(solution)/shard_map/ppermute | solution.py:330
  17.4 2.7 %collective-permute-start.6 = (f32[4,72,128]{2,1,0:T(8,128)S(1)}, f32[4,72,128]{2,1,0:T(8,128)S(1)}, u32[]{:S(2)}, u32[]{:S(2)}) collective-permute-start(f32[4,72,128]{2,1,0:T(8,128)S(1)} %get-tuple-element.26), channel_id=1, source_target_pairs={{0,1},{1,0},{2,3},{3,2},{4,5},{5,4},{6,7},{7,6},{8,9},{9,8},{10,11... | collective-permute-start | bytes 442376 | tf_op jit(solution)/shard_map/ppermute | solution.py:321
  20.1 5.1 %collective-permute-start.7 = (s16[80,128]{1,0:T(8,128)(2,1)S(1)}, s16[80,128]{1,0:T(8,128)(2,1)S(1)}, u32[]{:S(2)}, u32[]{:S(2)}) collective-permute-start(s16[80,128]{1,0:T(8,128)(2,1)S(1)} %get-tuple-element.28), channel_id=1, source_target_pairs={{0,7},{1,6},{2,5},{3,4},{4,3},{5,2},{6,1},{7,0},{8,15},{9,14},{10,... | collective-permute-start | bytes 61448 | tf_op jit(solution)/shard_map/ppermute | solution.py:321
  21.8 4.2 %collective-permute-start.8 = (s16[80,128]{1,0:T(8,128)(2,1)S(1)}, s16[80,128]{1,0:T(8,128)(2,1)S(1)}, u32[]{:S(2)}, u32[]{:S(2)}) collective-permute-start(s16[80,128]{1,0:T(8,128)(2,1)S(1)} %get-tuple-element.29), channel_id=1, source_target_pairs={{0,5},{1,4},{2,7},{3,6},{4,1},{5,0},{6,3},{7,2},{8,13},{9,12},{10,... | collective-permute-start | bytes 61448 | tf_op jit(solution)/shard_map/ppermute | solution.py:321
  22.2 4.1 %collective-permute-start.9 = (s16[80,128]{1,0:T(8,128)(2,1)S(1)}, s16[80,128]{1,0:T(8,128)(2,1)S(1)}, u32[]{:S(2)}, u32[]{:S(2)}) collective-permute-start(s16[80,128]{1,0:T(8,128)(2,1)S(1)} %get-tuple-element.30), channel_id=1, source_target_pairs={{0,3},{1,2},{2,1},{3,0},{4,7},{5,6},{6,5},{7,4},{8,11},{9,10},{10,... | collective-permute-start | bytes 61448 | tf_op jit(solution)/shard_map/ppermute | solution.py:321

commit v8 on v7

--- a/solution.py
+++ b/solution.py
@@ -135,27 +135,31 @@
     return jnp.where(iota(shape, 0).astype(F32) == line_column, 1.0, 0.0).astype(BF16)
 
 
-def gather_kernel(near, rows, lines, levels, *refs):
-    got, (turned_ref, d_ref, slots_ref, hits_ref, a_ref, b_ref, packs) = refs[:near], refs[near:]
+def places(cell, rows, levels):
+    cell = cell.astype(jnp.int32)
+    flat = lax.shift_right_logical(cell, log2(LANES))
+    key = (flat & (rows - 1)) * levels + lax.shift_right_logical(flat, log2(rows))
+    return key.astype(F32), (cell & (LANES - 1)).astype(F32)
+
+
+def gather_kernel(order, rows, lines, levels, *refs):
+    got, (turned_ref, d_ref, slots_ref, hits_ref, a_ref, b_ref, packs) = refs[: len(order)], refs[len(order) :]
     tiles = packs.shape[0]
     size = min(tiles, LANES // GROUP)
     me, even = lax.axis_index("tx"), lax.rem(lax.axis_index("ty"), 2) == 0
     chip, core = me // 2, lax.rem(me, 2)
-    for far, ref in enumerate(got):
+    for far, ref in zip(order, got):
         for side in range(2):
             packs[2 * (chip ^ far) + (core ^ side ^ (far > 0))] = ref[side]
-    values, keys, columns = [], [], []
+    slots = []
     for i in range(lines):
         x = packs[:, rows + i, :]
-        cell = x.astype(jnp.int32)
-        flat = lax.shift_right_logical(cell, log2(LANES))
-        key = (flat & (rows - 1)) * levels + lax.shift_right_logical(flat, log2(rows))
-        for out, part in ((values, x), (keys, key.astype(F32)), (columns, (cell & (LANES - 1)).astype(F32))):
-            out.append([stagger(part[q : q + size]) for q in range(0, tiles, size)])
+        slots.append([stagger(x[q : q + size]) for q in range(0, tiles, size)])
     deep = STEPS - 1
+    step = deep + lines
     for t in range(tiles):
-        value = lines_of(values, t, tiles)
-        key, column = lines_of(keys, tiles + t, tiles), lines_of(columns, tiles + t, tiles)
+        value, cell = lines_of(slots, t, tiles), lines_of(slots, tiles + t, tiles)
+        key, column = places(cell, rows, levels)
         hits = hits_of(column)
         hits_ref[t] = hits
         found = jnp.dot(turned_ref[t], hits, preferred_element_type=F32)
@@ -164,26 +168,49 @@
         d = packs[t, 0:rows, :]
         d_ref[:, t * LANES : (t + 1) * LANES] = d
         low = pltpu.roll(d, deep, 0)
+        sent = [line[:, q : q + LANES] for line in (product, cell) for q in range(0, line.shape[1], LANES)]
+        if len(sent) > lines:
+            sent = [sent[0] + pltpu.roll(sent[1], tiles * GROUP, 1)]
         for out, part in ((a_ref, jnp.where(even, low, d)), (b_ref, jnp.where(even, d, low))):
-            out[t, 0:rows, :] = part
-            for i, line in enumerate((product, key, column)):
-                for q in range(tiles // size):
-                    out[t, deep + 3 * q + i : deep + 3 * q + i + 1, :] = line[:, q * LANES : (q + 1) * LANES]
+            out[t * step : t * step + deep, :] = part[0:deep]
+            for i, line in enumerate(sent):
+                out[t * step + deep + i : t * step + deep + i + 1, :] = line
         for i, line in enumerate((product, key)):
             slots_ref[t, i : i + 1, :] = line
 
 
-def own_kernel(slots_ref, hits_ref, start_ref):
-    count = start_ref.shape[0]
-    for t in range(slots_ref.shape[0]):
+def step_row(rows3, d, c, columns):
+    above, mid, below = rows3
+    beside = (
+        above[:, 0:columns]
+        + below[:, 0:columns]
+        + pltpu.roll(mid, 1, 1)[:, 0:columns]
+        + pltpu.roll(mid, mid.shape[1] - 1, 1)[:, 0:columns]
+    )
+    return jnp.broadcast_to(c, beside.shape) * mid[:, 0:columns] + jnp.broadcast_to(d, beside.shape) * beside
+
+
+def own_kernel(slots_ref, hits_ref, turned_ref, d_ref, member_ref, keep_ref, *fields):
+    tiles, own, _ = turned_ref.shape
+    columns = tiles * LANES
+    rows = d_ref.shape[0]
+    levels = own // rows
+    for field in fields:
+        field[:, columns:] = jnp.zeros((own, LANES), F32)
+    keep_ref[...] = 1.0 - 4.0 * d_ref[...]
+    for t in range(tiles):
         at = slice(t * LANES, (t + 1) * LANES)
-        start_ref[:, at] = spread(slots_ref[t, 0:1, :], slots_ref[t, 1:2, :], hits_ref[t], count, 0.0)
-
-
-def main_kernel(
-    rows, levels, start_ref, d_ref, slots_ref, hits_ref, turned_ref, a_ref, b_ref, factors_ref, mine_ref, other_ref,
-    member, d_all, keep, first, second, made, back,
-):
+        member_ref[:, at] = turned_ref[t].astype(F32)
+        fields[0][:, at] = spread(slots_ref[t, 0:1, :], slots_ref[t, 1:2, :], hits_ref[t], own, 0.0)
+    for step in range(1, len(fields)):
+        for r in range(step, rows - step):
+            near = [fields[step - 1][i * levels : (i + 1) * levels, :] for i in (r - 1, r, r + 1)]
+            x = step_row(near, d_ref[r : r + 1, :], keep_ref[r : r + 1, :], columns)
+            fields[step][r * levels : (r + 1) * levels, 0:columns] = x
+
+
+def main_kernel(rows, levels, d_ref, slots_ref, hits_ref, b_ref, a_ref, factors_ref, member, keep_ref, *refs):
+    fields, (mine_ref, other_ref, d_all, keep, first, second, made, back) = refs[:STEPS], refs[STEPS:]
     tiles = hits_ref.shape[0]
     block = min(tiles, LANES // GROUP)
     columns = tiles * LANES
@@ -191,48 +218,51 @@
     chip, core = me // 2, lax.rem(me, 2)
     even = lax.rem(band, 2) == 0
     half, own, deep = STEPS * levels, rows * levels, STEPS - 1
-
-    first[half : half + own, 0:columns] = start_ref[...]
-    d_all[STEPS : STEPS + rows, :] = d_ref[...]
+    step = a_ref.shape[0] // tiles
+
     for t in range(tiles):
         at = slice(t * LANES, (t + 1) * LANES)
-        member[:, at] = turned_ref[t].astype(F32)
-        got_a, got_b = a_ref[t], b_ref[t]
+        got_a, got_b = (ref[t * step : (t + 1) * step, :] for ref in (a_ref, b_ref))
         above = jnp.where(band == 0, 0.0, jnp.where(even, got_b, got_a))
         below = jnp.where(band == last, 0.0, jnp.where(even, got_a, got_b))
         for got, begin, base, d_begin in ((above, 0, own - half, 1), (below, half + own, 0, STEPS + rows)):
             d_all[d_begin : d_begin + deep, at] = got[0:deep]
-            product, key, column = (
-                jnp.concatenate([got[deep + 3 * q + i : deep + 3 * q + i + 1] for q in range(tiles // block)], axis=1)
-                for i in range(3)
-            )
+            keep[d_begin : d_begin + deep, at] = 1.0 - 4.0 * got[0:deep]
+            parts = [got[deep + i : deep + i + 1] for i in range(step - deep)]
+            if len(parts) == 1:
+                parts.append(pltpu.roll(parts[0], LANES - tiles * GROUP, 1))
+                parts[0] = jnp.where(iota((1, LANES), 1) < tiles * GROUP, parts[0], 0.0)
+            product, cell = (jnp.concatenate(parts[i : i + len(parts) // 2], axis=1) for i in (0, len(parts) // 2))
+            key, column = places(cell, rows, levels)
             first[begin : begin + half, at] = spread(product, key, hits_of(column), half, float(base))
-
-    first[:, columns:] = jnp.zeros((first.shape[0], LANES), F32)
-    second[:, columns:] = jnp.zeros((second.shape[0], LANES), F32)
-    keep[...] = 1.0 - 4.0 * d_all[...]
+    for field in (first, second):
+        field[:, columns:] = jnp.zeros((field.shape[0], LANES), F32)
+
+    def inner(step, r):
+        return step <= r - STEPS < rows - step
+
+    def row_of(step, r):
+        ref, i = (fields[step], r - STEPS) if inner(step, r) else ((first, second)[step % 2], r)
+        return ref[i * levels : (i + 1) * levels, :]
+
     factors = [(i - BAND, factors_ref[i]) for i in range(2 * BAND + 1)]
-    source, target = first, second
-    for step in range(STEPS):
-        for r in range(step + 1, 2 * STEPS + rows - 1 - step):
-            mid = source[r * levels : (r + 1) * levels, :]
-            beside = (
-                source[(r - 1) * levels : r * levels, 0:columns]
-                + source[(r + 1) * levels : (r + 2) * levels, 0:columns]
-                + pltpu.roll(mid, 1, 1)[:, 0:columns]
-                + pltpu.roll(mid, columns + LANES - 1, 1)[:, 0:columns]
-            )
-            d, c = (jnp.broadcast_to(x[r : r + 1, :], (levels, columns)) for x in (d_all, keep))
-            x = c * mid[:, 0:columns] + d * beside
-            if step < STEPS - 1:
-                target[r * levels : (r + 1) * levels, 0:columns] = x
+    for step in range(1, STEPS + 1):
+        for r in range(step, 2 * STEPS + rows - step):
+            if step < STEPS and inner(step, r):
+                continue
+            if 0 <= r - STEPS < rows:
+                d, c = (ref[r - STEPS : r - STEPS + 1, :] for ref in (d_ref, keep_ref))
+            else:
+                d, c = (ref[r : r + 1, :] for ref in (d_all, keep))
+            x = step_row([row_of(step - 1, i) for i in (r - 1, r, r + 1)], d, c, columns)
+            if step < STEPS:
+                (first, second)[step % 2][r * levels : (r + 1) * levels, 0:columns] = x
                 continue
             row = slice((r - STEPS) * levels, (r - STEPS + 1) * levels)
             for t in range(tiles):
                 at = slice(t * LANES, (t + 1) * LANES)
                 mixed = sum(f * (pltpu.roll(x[:, at], -o % levels, 0) if o else x[:, at]) for o, f in factors)
                 made[t, row, :] = mixed * member[row, at]
-        source, target = target, source
 
     for t in range(tiles):
         stacked = jnp.concatenate(pieces(made[t]), axis=0).astype(BF16)
@@ -311,7 +341,7 @@
     shape = jax.ShapeDtypeStruct
     lines = -(-2 * tiles * GROUP // LANES)
     half, own = STEPS * levels, rows * levels
-    height, halo_height = round_up(rows + lines, 8), round_up(max(rows, STEPS - 1 + 3 * (tiles // block)), 8)
+    height = round_up(rows + lines, 8)
     lanes = tiles // block * LANES
 
     def in_hbm(*arrays):
@@ -358,10 +388,11 @@
     )(*in_hbm(ensemble, vertical, weights))
 
     pair = jnp.stack([packet, swap(packet, 1)])
-    row = [pair] + [swap(pair, 2 * far + 1) for far in range(1, chips)]
-    halo = shape((tiles, halo_height, LANES), F32)
+    order = [0] + sorted(range(1, chips), key=lambda far: (far % 2 == 0, far))
+    row = [swap(pair, 2 * far + 1) if far else pair for far in order]
+    halo = shape((tiles * (STEPS - 1 + lines), LANES), F32)
     d_row, slots_row, hits, to_a, to_b = call(
-        functools.partial(gather_kernel, chips, rows, lines, levels),
+        functools.partial(gather_kernel, order, rows, lines, levels),
         (
             shape((rows, columns), F32),
             shape((tiles, 8, lanes), F32),
@@ -373,15 +404,22 @@
         [pltpu.VMEM((tiles, height, LANES), F32)],
     )(*row, turned)
     from_a, from_b = swap_bands(to_a, True), swap_bands(to_b, False)
-    start = call(own_kernel, shape((own, columns), F32), [VMEM] * 2, [], 1000000, 1000000)(slots_row, hits)
+    wide = shape((own, columns + LANES), F32)
+    member, keep, *fields = call(
+        own_kernel,
+        (shape((own, columns), F32), shape((rows, columns), F32), *[wide] * STEPS),
+        [VMEM] * 4,
+        [],
+        1000000,
+        1000000,
+    )(slots_row, hits, turned, d_row)
 
     chunk = own + tiles
     mine, other = call(
         functools.partial(main_kernel, rows, levels),
         (shape((chips, chunk, LANES), F32), shape((chips, chunk, LANES), F32)),
-        [VMEM] * 8,
+        [VMEM] * (8 + STEPS),
         [
-            pltpu.VMEM((own, columns), F32),
             pltpu.VMEM((2 * STEPS + rows, columns), F32),
             pltpu.VMEM((2 * STEPS + rows, columns), F32),
             pltpu.VMEM((2 * half + own, columns + LANES), F32),
@@ -389,7 +427,7 @@
             pltpu.VMEM((tiles, own, LANES), F32),
             pltpu.VMEM((tiles // block, tiles, LANES), F32),
         ],
-    )(start, d_row, slots_row, hits, turned, from_a, from_b, factors)
+    )(d_row, slots_row, hits, from_b, from_a, factors, member, keep, *fields)
 
     coded = shape((round_up(chunk + 2, 16), LANES), jnp.int16)
     sums = call(

time: 27.2 us -> 26.5 us (0.974)
  the two profiles are of different devices: /device:TPU:5 before, /device:TPU:0 now
where the time goes in v8:
time: 26.5 us; the launch traced here: 26.2 us
  starting transfers between devices  12.8 us (48%)
  waiting for transfers between devices  7.91 us (30%)
  Pallas kernels  4.81 us (18%)
  between operations  0.69 us (3%)
    ppermute x8, starting transfers between devices, swap(): return lax.ppermute(x, 'tx', [(i, i ^ far) for i in range(tiles)])  9.75 us
    ppermute x8, waiting for transfers between devices, swap(): return lax.ppermute(x, 'tx', [(i, i ^ far) for i in range(tiles)])  6.58 us
    ppermute x2, starting transfers between devices, swap_bands(): return lax.ppermute(x, ('ty', 'tx'), pairs)  3.08 us
    ppermute x2, waiting for transfers between devices, swap_bands(): return lax.ppermute(x, ('ty', 'tx'), pairs)  1.33 us
    pallas_call x1, Pallas kernels, shards(): call(functools.partial(main_kernel, rows, levels), (shape((chips, chunk,...  1.09 us
    pallas_call x1, Pallas kernels, shards(): call(member_kernel, (shape((tiles, own, LANES), BF16), shape((2 * BAND +...  1.08 us
    pallas_call x1, Pallas kernels, shards(): call(packet_kernel, (shape((height, LANES), F32), shape((tiles, LANES), F...  0.93 us
    pallas_call x1, Pallas kernels, shards(): call(functools.partial(final_kernel, own), (shape((levels, rows, LANES),...  0.69 us
  transfers between devices with their start and end apart: 10, of which 6 were waited for; matrix products, arithmetic and copies ran while one was open for 0% of the time, Pallas kernels for 6%

profile of v8, /device:TPU:0, one launch (start us, length us, event | category | flops | bytes accessed | tf_op | source)
XLA Modules:
  0.0 26.2 jit_solution(4595838695544006688)
XLA Ops:
  0.6 0.9 %shard_map.86 = (f32[16,128]{1,0:T(8,128)S(1)}, f32[8,128]{1,0:T(8,128)S(1)}) custom-call(f32[1,8,8]{2,1,0:T(8,128)} %value_hbm.1, s32[1,8,8]{2,1,0:T(8,128)} %cell_hbm.1, s32[1,8]{1,0:T(1,128)} %count_hbm.1, f32[8,128]{1,0:T(8,128)} %diff_hbm.1), custom_call_target="tpu_custom_call" | custom-call | tf_op jit(solution)/shard_map/pallas_call | solution.py:362
  1.6 0.5 %collective-permute-start = (f32[16,128]{1,0:T(8,128)S(1)}, f32[16,128]{1,0:T(8,128)S(1)}, u32[]{:S(2)}, u32[]{:S(2)}) collective-permute-start(f32[16,128]{1,0:T(8,128)S(1)} %get-tuple-element.23), channel_id=1, source_target_pairs={{0,1},{1,0},{2,3},{3,2},{4,5},{5,4},{6,7},{7,6},{8,9},{9,8},{10,11... | collective-permute-start | bytes 24584 | tf_op jit(solution)/shard_map/ppermute | solution.py:351
  2.1 0.8 %collective-permute-done = f32[16,128]{1,0:T(8,128)S(1)} collective-permute-done((f32[16,128]{1,0:T(8,128)S(1)}, f32[16,128]{1,0:T(8,128)S(1)}, u32[]{:S(2)}, u32[]{:S(2)}) %collective-permute-start) | collective-permute-done | bytes 8224 | tf_op jit(solution)/shard_map/ppermute | solution.py:351
  2.9 3.7 %collective-permute-start.3 = (f32[2,16,128]{2,1,0:T(8,128)S(1)}, f32[2,16,128]{2,1,0:T(8,128)S(1)}, u32[]{:S(2)}, u32[]{:S(2)}) collective-permute-start(f32[2,16,128]{2,1,0:T(8,128)S(1)} %pad_maximum_fusion.refs_0_), channel_id=1, source_target_pairs={{0,5},{1,4},{2,7},{3,6},{4,1},{5,0},{6,3},{7,2},{8,13},{9,12},{10,... | collective-permute-start | bytes 49160 | tf_op jit(solution)/shard_map/ppermute | solution.py:351
  6.6 1.3 %collective-permute-start.2 = (f32[2,16,128]{2,1,0:T(8,128)S(1)}, f32[2,16,128]{2,1,0:T(8,128)S(1)}, u32[]{:S(2)}, u32[]{:S(2)}) collective-permute-start(f32[2,16,128]{2,1,0:T(8,128)S(1)} %pad_maximum_fusion.refs_0_), channel_id=1, source_target_pairs={{0,7},{1,6},{2,5},{3,4},{4,3},{5,2},{6,1},{7,0},{8,15},{9,14},{10,... | collective-permute-start | bytes 49160 | tf_op jit(solution)/shard_map/ppermute | solution.py:351
  7.9 0.2 collective-permute-start.1
  8.1 1.1 %shard_map.87 = (bf16[8,64,128]{2,1,0:T(8,128)(2,1)S(1)}, f32[5,8,128]{2,1,0:T(8,128)S(1)}) custom-call(bf16[1,8,8,1024]{3,2,1,0:T(8,128)(2,1)} %ens_hbm.1, f32[8,8]{1,0:T(8,128)} %vertical_hbm.1, f32[8]{0:T(128)} %weights_hbm.1), custom_call_target="tpu_custom_call" | custom-call | flops 1000000 | bytes 1000000 | tf_op jit(solution)/shard_map/pallas_call | solution.py:375
  9.2 0.0 collective-permute-done.3.refs_3_
  9.2 2.4 %collective-permute-done.2.refs_2_ = f32[2,16,128]{2,1,0:T(8,128)S(1)} collective-permute-done((f32[2,16,128]{2,1,0:T(8,128)S(1)}, f32[2,16,128]{2,1,0:T(8,128)S(1)}, u32[]{:S(2)}, u32[]{:S(2)}) %collective-permute-start.2) | collective-permute-done | bytes 16416 | tf_op jit(solution)/shard_map/ppermute | solution.py:351
  11.6 0.0 collective-permute-done.1.refs_1_
  11.6 0.4 %shard_map.88 = (f32[8,1024]{1,0:T(8,128)S(1)}, f32[8,8,128]{2,1,0:T(8,128)S(1)}, bf16[8,128,128]{2,1,0:T(8,128)(2,1)S(1)}, f32[32,128]{1,0:T(8,128)S(1)}, f32[32,128]{1,0:T(8,128)S(1)}) custom-call(f32[2,16,128]{2,1,0:T(8,128)S(1)} %pad_maximum_fusion.refs_0_, f32[2,16,128]{2,1,0:T(8,128)S(1)} %collective-permute-done.1.refs_1_, ...), custom_call_target="tpu_custom_call" | custom-call | tf_op jit(solution)/shard_map/pallas_call | solution.py:394
  12.0 0.5 %collective-permute-start.4 = (f32[32,128]{1,0:T(8,128)S(1)}, f32[32,128]{1,0:T(8,128)S(1)}, u32[]{:S(2)}, u32[]{:S(2)}) collective-permute-start(f32[32,128]{1,0:T(8,128)S(1)} %get-tuple-element.28), channel_id=1, source_target_pairs={{0,1},{1,0},{2,3},{3,2},{4,5},{5,4},{6,7},{7,6},{8,16},{9,17},{10,... | collective-permute-start | bytes 49160 | tf_op jit(solution)/shard_map/ppermute | solution.py:360
  12.5 2.6 %collective-permute-start.5 = (f32[32,128]{1,0:T(8,128)S(1)}, f32[32,128]{1,0:T(8,128)S(1)}, u32[]{:S(2)}, u32[]{:S(2)}) collective-permute-start(f32[32,128]{1,0:T(8,128)S(1)} %get-tuple-element.29), channel_id=1, source_target_pairs={{0,8},{1,9},{2,10},{3,11},{4,12},{5,13},{6,14},{7,15},{8,0},{9,1},... | collective-permute-start | bytes 49160 | tf_op jit(solution)/shard_map/ppermute | solution.py:360
  15.1 0.5 %shard_map.89 = (f32[64,1024]{1,0:T(8,128)S(1)}, f32[8,1024]{1,0:T(8,128)S(1)}, f32[64,1152]{1,0:T(8,128)S(1)}, f32[64,1152]{1,0:T(8,128)S(1)}, f32[64,1152]{1,0:T(8,128)S(1)}, /*index=5*/f32[64,1152]{1,0:T(8,128)S(1)}) custom-call(f32[8,8,128]{2,1,0:T(8,128)S(1)} %get-tuple-element.26.slots_ref, bf16[8,128,128]{2,1,0:T(8,128)(2,1)S(1)} %get-tuple-element.27.hits_ref, ...), custom_call_target="tpu_custom_call" | custom-call | flops 1000000 | bytes 1000000 | tf_op jit(solution)/shard_map/pallas_call | solution.py:408
  15.6 0.0 collective-permute-done.4.b_ref
  15.6 1.3 %collective-permute-done.5.a_ref = f32[32,128]{1,0:T(8,128)S(1)} collective-permute-done((f32[32,128]{1,0:T(8,128)S(1)}, f32[32,128]{1,0:T(8,128)S(1)}, u32[]{:S(2)}, u32[]{:S(2)}) %collective-permute-start.5) | collective-permute-done | bytes 16416 | tf_op jit(solution)/shard_map/ppermute | solution.py:360
  17.0 1.1 %shard_map.90 = (f32[4,72,128]{2,1,0:T(8,128)S(1)}, f32[4,72,128]{2,1,0:T(8,128)S(1)}) custom-call(f32[8,1024]{1,0:T(8,128)S(1)} %get-tuple-element.25.d_ref, f32[8,8,128]{2,1,0:T(8,128)S(1)} %get-tuple-element.26.slots_ref, bf16[8,128,128]{2,1,0:T(8,128)(2,1)S(1)} %get-tuple-element.27.hits_ref, f32[32,128]{1,0:T(8,128)S(1)} %collective-permute-done.4.b_ref, ...), custom_call_target="tpu_custom_call" | custom-call | tf_op jit(solution)/shard_map/pallas_call | solution.py:418
  18.1 0.1 collective-permute-start.6
  18.1 1.4 %collective-permute-done.6.got_ref = f32[4,72,128]{2,1,0:T(8,128)S(1)} collective-permute-done((f32[4,72,128]{2,1,0:T(8,128)S(1)}, f32[4,72,128]{2,1,0:T(8,128)S(1)}, u32[]{:S(2)}, u32[]{:S(2)}) %collective-permute-start.6) | collective-permute-done | bytes 147488 | tf_op jit(solution)/shard_map/ppermute | solution.py:351
  19.5 0.1 shard_map.91
  19.6 1.8 %collective-permute-start.7 = (s16[80,128]{1,0:T(8,128)(2,1)S(1)}, s16[80,128]{1,0:T(8,128)(2,1)S(1)}, u32[]{:S(2)}, u32[]{:S(2)}) collective-permute-start(s16[80,128]{1,0:T(8,128)(2,1)S(1)} %get-tuple-element.40), channel_id=1, source_target_pairs={{0,7},{1,6},{2,5},{3,4},{4,3},{5,2},{6,1},{7,0},{8,15},{9,14},{10,... | collective-permute-start | bytes 61448 | tf_op jit(solution)/shard_map/ppermute | solution.py:351
  21.4 0.0 collective-permute-start.8
  21.4 2.1 %collective-permute-start.9 = (s16[80,128]{1,0:T(8,128)(2,1)S(1)}, s16[80,128]{1,0:T(8,128)(2,1)S(1)}, u32[]{:S(2)}, u32[]{:S(2)}) collective-permute-start(s16[80,128]{1,0:T(8,128)(2,1)S(1)} %get-tuple-element.42), channel_id=1, source_target_pairs={{0,3},{1,2},{2,1},{3,0},{4,7},{5,6},{6,5},{7,4},{8,11},{9,10},{10,... | collective-permute-start | bytes 61448 | tf_op jit(solution)/shard_map/ppermute | solution.py:351
  23.5 1.1 %collective-permute-done.7.refs_1_ = s16[80,128]{1,0:T(8,128)(2,1)S(1)} collective-permute-done((s16[80,128]{1,0:T(8,128)(2,1)S(1)}, s16[80,128]{1,0:T(8,128)(2,1)S(1)}, u32[]{:S(2)}, u32[]{:S(2)}) %collective-permute-start.7) | collective-permute-done | bytes 20512 | tf_op jit(solution)/shard_map/ppermute | solution.py:351
  24.7 0.9 %collective-permute-done.8.refs_2_ = s16[80,128]{1,0:T(8,128)(2,1)S(1)} collective-permute-done((s16[80,128]{1,0:T(8,128)(2,1)S(1)}, s16[80,128]{1,0:T(8,128)(2,1)S(1)}, u32[]{:S(2)}, u32[]{:S(2)}) %collective-permute-start.8) | collective-permute-done | bytes 20512 | tf_op jit(solution)/shard_map/ppermute | solution.py:351
  25.6 0.0 collective-permute-done.9.refs_3_
  25.6 0.7 %shard_map.92 = (f32[8,8,128]{2,1,0:T(8,128)}, f32[1,8,8]{2,1,0:T(8,128)}) custom-call(f32[72,128]{1,0:T(8,128)S(1)} %get-tuple-element.39.refs_0_, s16[80,128]{1,0:T(8,128)(2,1)S(1)} %collective-permute-done.7.refs_1_, s16[80,128]{1,0:T(8,128)(2,1)S(1)} %collective-permute-done.8.refs_2_, s16[80,128]{1,0:T(8,128)(2,1)S(1)} %collective-permute-done.9.refs_3_, ...), custom_call_target="tpu_custom_call" | custom-call | tf_op jit(solution)/shard_map/pallas_call | solution.py:437
  (1 shorter events, 0.0 us)
Async XLA Ops:
  1.6 1.3 %collective-permute-start = (f32[16,128]{1,0:T(8,128)S(1)}, f32[16,128]{1,0:T(8,128)S(1)}, u32[]{:S(2)}, u32[]{:S(2)}) collective-permute-start(f32[16,128]{1,0:T(8,128)S(1)} %get-tuple-element.23), channel_id=1, source_target_pairs={{0,1},{1,0},{2,3},{3,2},{4,5},{5,4},{6,7},{7,6},{8,9},{9,8},{10,11... | collective-permute-start | bytes 24584 | tf_op jit(solution)/shard_map/ppermute | solution.py:351
  2.9 6.3 %collective-permute-start.3 = (f32[2,16,128]{2,1,0:T(8,128)S(1)}, f32[2,16,128]{2,1,0:T(8,128)S(1)}, u32[]{:S(2)}, u32[]{:S(2)}) collective-permute-start(f32[2,16,128]{2,1,0:T(8,128)S(1)} %pad_maximum_fusion.refs_0_), channel_id=1, source_target_pairs={{0,5},{1,4},{2,7},{3,6},{4,1},{5,0},{6,3},{7,2},{8,13},{9,12},{10,... | collective-permute-start | bytes 49160 | tf_op jit(solution)/shard_map/ppermute | solution.py:351
  6.6 5.0 %collective-permute-start.2 = (f32[2,16,128]{2,1,0:T(8,128)S(1)}, f32[2,16,128]{2,1,0:T(8,128)S(1)}, u32[]{:S(2)}, u32[]{:S(2)}) collective-permute-start(f32[2,16,128]{2,1,0:T(8,128)S(1)} %pad_maximum_fusion.refs_0_), channel_id=1, source_target_pairs={{0,7},{1,6},{2,5},{3,4},{4,3},{5,2},{6,1},{7,0},{8,15},{9,14},{10,... | collective-permute-start | bytes 49160 | tf_op jit(solution)/shard_map/ppermute | solution.py:351
  7.9 3.7 %collective-permute-start.1 = (f32[2,16,128]{2,1,0:T(8,128)S(1)}, f32[2,16,128]{2,1,0:T(8,128)S(1)}, u32[]{:S(2)}, u32[]{:S(2)}) collective-permute-start(f32[2,16,128]{2,1,0:T(8,128)S(1)} %pad_maximum_fusion.refs_0_), channel_id=1, source_target_pairs={{0,3},{1,2},{2,1},{3,0},{4,7},{5,6},{6,5},{7,4},{8,11},{9,10},{10,... | collective-permute-start | bytes 49160 | tf_op jit(solution)/shard_map/ppermute | solution.py:351
  12.0 3.6 %collective-permute-start.4 = (f32[32,128]{1,0:T(8,128)S(1)}, f32[32,128]{1,0:T(8,128)S(1)}, u32[]{:S(2)}, u32[]{:S(2)}) collective-permute-start(f32[32,128]{1,0:T(8,128)S(1)} %get-tuple-element.28), channel_id=1, source_target_pairs={{0,1},{1,0},{2,3},{3,2},{4,5},{5,4},{6,7},{7,6},{8,16},{9,17},{10,... | collective-permute-start | bytes 49160 | tf_op jit(solution)/shard_map/ppermute | solution.py:360
  12.5 4.5 %collective-permute-start.5 = (f32[32,128]{1,0:T(8,128)S(1)}, f32[32,128]{1,0:T(8,128)S(1)}, u32[]{:S(2)}, u32[]{:S(2)}) collective-permute-start(f32[32,128]{1,0:T(8,128)S(1)} %get-tuple-element.29), channel_id=1, source_target_pairs={{0,8},{1,9},{2,10},{3,11},{4,12},{5,13},{6,14},{7,15},{8,0},{9,1},... | collective-permute-start | bytes 49160 | tf_op jit(solution)/shard_map/ppermute | solution.py:360
  18.1 1.4 %collective-permute-start.6 = (f32[4,72,128]{2,1,0:T(8,128)S(1)}, f32[4,72,128]{2,1,0:T(8,128)S(1)}, u32[]{:S(2)}, u32[]{:S(2)}) collective-permute-start(f32[4,72,128]{2,1,0:T(8,128)S(1)} %get-tuple-element.38), channel_id=1, source_target_pairs={{0,1},{1,0},{2,3},{3,2},{4,5},{5,4},{6,7},{7,6},{8,9},{9,8},{10,11... | collective-permute-start | bytes 442376 | tf_op jit(solution)/shard_map/ppermute | solution.py:351
  19.6 5.1 %collective-permute-start.7 = (s16[80,128]{1,0:T(8,128)(2,1)S(1)}, s16[80,128]{1,0:T(8,128)(2,1)S(1)}, u32[]{:S(2)}, u32[]{:S(2)}) collective-permute-start(s16[80,128]{1,0:T(8,128)(2,1)S(1)} %get-tuple-element.40), channel_id=1, source_target_pairs={{0,7},{1,6},{2,5},{3,4},{4,3},{5,2},{6,1},{7,0},{8,15},{9,14},{10,... | collective-permute-start | bytes 61448 | tf_op jit(solution)/shard_map/ppermute | solution.py:351
  21.4 4.2 %collective-permute-start.8 = (s16[80,128]{1,0:T(8,128)(2,1)S(1)}, s16[80,128]{1,0:T(8,128)(2,1)S(1)}, u32[]{:S(2)}, u32[]{:S(2)}) collective-permute-start(s16[80,128]{1,0:T(8,128)(2,1)S(1)} %get-tuple-element.41), channel_id=1, source_target_pairs={{0,5},{1,4},{2,7},{3,6},{4,1},{5,0},{6,3},{7,2},{8,13},{9,12},{10,... | collective-permute-start | bytes 61448 | tf_op jit(solution)/shard_map/ppermute | solution.py:351
  21.4 4.2 %collective-permute-start.9 = (s16[80,128]{1,0:T(8,128)(2,1)S(1)}, s16[80,128]{1,0:T(8,128)(2,1)S(1)}, u32[]{:S(2)}, u32[]{:S(2)}) collective-permute-start(s16[80,128]{1,0:T(8,128)(2,1)S(1)} %get-tuple-element.42), channel_id=1, source_target_pairs={{0,3},{1,2},{2,1},{3,0},{4,7},{5,6},{6,5},{7,4},{8,11},{9,10},{10,... | collective-permute-start | bytes 61448 | tf_op jit(solution)/shard_map/ppermute | solution.py:351

commit v9 on v8

--- a/solution.py
+++ b/solution.py
@@ -147,10 +147,10 @@
     tiles = packs.shape[0]
     size = min(tiles, LANES // GROUP)
     me, even = lax.axis_index("tx"), lax.rem(lax.axis_index("ty"), 2) == 0
-    chip, core = me // 2, lax.rem(me, 2)
+    chip, core, used = me // 2, lax.rem(me, 2), rows + lines
     for far, ref in zip(order, got):
         for side in range(2):
-            packs[2 * (chip ^ far) + (core ^ side ^ (far > 0))] = ref[side]
+            packs[2 * (chip ^ far) + (core ^ side ^ (far > 0)), 0:used, :] = ref[side * used : (side + 1) * used, :]
     slots = []
     for i in range(lines):
         x = packs[:, rows + i, :]
@@ -246,26 +246,43 @@
         return ref[i * levels : (i + 1) * levels, :]
 
     factors = [(i - BAND, factors_ref[i]) for i in range(2 * BAND + 1)]
-    for step in range(1, STEPS + 1):
+    for step in range(1, STEPS):
         for r in range(step, 2 * STEPS + rows - step):
-            if step < STEPS and inner(step, r):
+            if inner(step, r):
                 continue
             if 0 <= r - STEPS < rows:
                 d, c = (ref[r - STEPS : r - STEPS + 1, :] for ref in (d_ref, keep_ref))
             else:
                 d, c = (ref[r : r + 1, :] for ref in (d_all, keep))
             x = step_row([row_of(step - 1, i) for i in (r - 1, r, r + 1)], d, c, columns)
-            if step < STEPS:
-                (first, second)[step % 2][r * levels : (r + 1) * levels, 0:columns] = x
-                continue
-            row = slice((r - STEPS) * levels, (r - STEPS + 1) * levels)
-            for t in range(tiles):
-                at = slice(t * LANES, (t + 1) * LANES)
-                mixed = sum(f * (pltpu.roll(x[:, at], -o % levels, 0) if o else x[:, at]) for o, f in factors)
-                made[t, row, :] = mixed * member[row, at]
-
+            (first, second)[step % 2][r * levels : (r + 1) * levels, 0:columns] = x
+
+    rowed = [row_of(STEPS - 1, r) for r in range(STEPS - 1, STEPS + rows + 1)]
+    lane = iota((levels, LANES), 1)
+    zero = jnp.zeros((levels, LANES), F32)
+
+    def piece(r, t):
+        return rowed[r + 1][:, t * LANES : (t + 1) * LANES] if 0 <= t < tiles else zero
+
+    before = [zero] * rows
+    here = [piece(r, 0) for r in range(rows)]
     for t in range(tiles):
-        stacked = jnp.concatenate(pieces(made[t]), axis=0).astype(BF16)
+        at = slice(t * LANES, (t + 1) * LANES)
+        after = [piece(r, t + 1) for r in range(rows)]
+        parts = []
+        for r in range(rows):
+            mid = here[r]
+            left = pltpu.roll(jnp.where(lane == LANES - 1, before[r], mid), 1, 1)
+            right = pltpu.roll(jnp.where(lane == 0, after[r], mid), LANES - 1, 1)
+            beside = piece(r - 1, t) + piece(r + 1, t) + left + right
+            d, c = (jnp.broadcast_to(ref[r : r + 1, at], mid.shape) for ref in (d_ref, keep_ref))
+            x = c * mid + d * beside
+            mixed = sum(f * (pltpu.roll(x, -o % levels, 0) if o else x) for o, f in factors)
+            row = slice(r * levels, (r + 1) * levels)
+            parts.append(mixed * member[row, at])
+            made[t, row, :] = parts[-1]
+        before, here = here, after
+        stacked = jnp.concatenate(pieces(jnp.concatenate(parts, axis=0)), axis=0).astype(BF16)
         found = jnp.dot(stacked, hits_ref[t], preferred_element_type=F32)
         found = found[0:own] + found[own : 2 * own] + found[2 * own :]
         on = iota(found.shape, 0).astype(F32) == slots_ref[t, 1:2, :]
@@ -387,7 +404,9 @@
         1000000,
     )(*in_hbm(ensemble, vertical, weights))
 
-    pair = jnp.stack([packet, swap(packet, 1)])
+    used = rows + lines
+    spare = jnp.zeros((round_up(2 * used, 8) - 2 * used, LANES), F32)
+    pair = jnp.concatenate([packet[:used], swap(packet, 1)[:used], spare])
     order = [0] + sorted(range(1, chips), key=lambda far: (far % 2 == 0, far))
     row = [swap(pair, 2 * far + 1) if far else pair for far in order]
     halo = shape((tiles * (STEPS - 1 + lines), LANES), F32)

time: 26.5 us -> 26.5 us (level)
  no operation moved by 1% of the time
where the time goes in v9:
time: 26.5 us; the launch traced here: 26.2 us
  starting transfers between devices  12.8 us (48%)
  waiting for transfers between devices  7.77 us (29%)
  Pallas kernels  4.79 us (18%)
  between operations  0.69 us (3%)
    ppermute x8, starting transfers between devices, swap(): return lax.ppermute(x, 'tx', [(i, i ^ far) for i in range(tiles)])  9.75 us
    ppermute x8, waiting for transfers between devices, swap(): return lax.ppermute(x, 'tx', [(i, i ^ far) for i in range(tiles)])  6.44 us
    ppermute x2, starting transfers between devices, swap_bands(): return lax.ppermute(x, ('ty', 'tx'), pairs)  3.06 us
    ppermute x2, waiting for transfers between devices, swap_bands(): return lax.ppermute(x, ('ty', 'tx'), pairs)  1.33 us
    pallas_call x1, Pallas kernels, shards(): call(member_kernel, (shape((tiles, own, LANES), BF16), shape((2 * BAND +...  1.08 us
    pallas_call x1, Pallas kernels, shards(): call(functools.partial(main_kernel, rows, levels), (shape((chips, chunk,...  1.07 us
    pallas_call x1, Pallas kernels, shards(): call(packet_kernel, (shape((height, LANES), F32), shape((tiles, LANES), F...  0.93 us
    pallas_call x1, Pallas kernels, shards(): call(functools.partial(final_kernel, own), (shape((levels, rows, LANES),...  0.69 us
  transfers between devices with their start and end apart: 10, of which 6 were waited for; matrix products, arithmetic and copies ran while one was open for 0% of the time, Pallas kernels for 6%

profile of v9, /device:TPU:0, one launch (start us, length us, event | category | flops | bytes accessed | tf_op | source)
XLA Modules:
  0.0 26.2 jit_solution(7562666593902407233)
XLA Ops:
  0.6 0.9 %shard_map.86 = (f32[16,128]{1,0:T(8,128)S(1)}, f32[8,128]{1,0:T(8,128)S(1)}) custom-call(f32[1,8,8]{2,1,0:T(8,128)} %value_hbm.1, s32[1,8,8]{2,1,0:T(8,128)} %cell_hbm.1, s32[1,8]{1,0:T(1,128)} %count_hbm.1, f32[8,128]{1,0:T(8,128)} %diff_hbm.1), custom_call_target="tpu_custom_call" | custom-call | tf_op jit(solution)/shard_map/pallas_call | solution.py:379
  1.6 0.5 %collective-permute-start = (f32[16,128]{1,0:T(8,128)S(1)}, f32[16,128]{1,0:T(8,128)S(1)}, u32[]{:S(2)}, u32[]{:S(2)}) collective-permute-start(f32[16,128]{1,0:T(8,128)S(1)} %get-tuple-element.23), channel_id=1, source_target_pairs={{0,1},{1,0},{2,3},{3,2},{4,5},{5,4},{6,7},{7,6},{8,9},{9,8},{10,11... | collective-permute-start | bytes 24584 | tf_op jit(solution)/shard_map/ppermute | solution.py:368
  2.1 0.1 pad.2.clone
  2.2 0.7 %collective-permute-done = f32[16,128]{1,0:T(8,128)S(1)} collective-permute-done((f32[16,128]{1,0:T(8,128)S(1)}, f32[16,128]{1,0:T(8,128)S(1)}, u32[]{:S(2)}, u32[]{:S(2)}) %collective-permute-start) | collective-permute-done | bytes 8224 | tf_op jit(solution)/shard_map/ppermute | solution.py:368
  2.9 0.1 maximum_maximum_fusion.refs_0_
  3.0 3.7 %collective-permute-start.3 = (f32[24,128]{1,0:T(8,128)S(1)}, f32[24,128]{1,0:T(8,128)S(1)}, u32[]{:S(2)}, u32[]{:S(2)}) collective-permute-start(f32[24,128]{1,0:T(8,128)S(1)} %maximum_maximum_fusion.refs_0_), channel_id=1, source_target_pairs={{0,5},{1,4},{2,7},{3,6},{4,1},{5,0},{6,3},{7,2},{8,13},{9,12},{10,... | collective-permute-start | bytes 36872 | tf_op jit(solution)/shard_map/ppermute | solution.py:368
  6.7 1.3 %collective-permute-start.2 = (f32[24,128]{1,0:T(8,128)S(1)}, f32[24,128]{1,0:T(8,128)S(1)}, u32[]{:S(2)}, u32[]{:S(2)}) collective-permute-start(f32[24,128]{1,0:T(8,128)S(1)} %maximum_maximum_fusion.refs_0_), channel_id=1, source_target_pairs={{0,7},{1,6},{2,5},{3,4},{4,3},{5,2},{6,1},{7,0},{8,15},{9,14},{10,... | collective-permute-start | bytes 36872 | tf_op jit(solution)/shard_map/ppermute | solution.py:368
  8.0 0.2 collective-permute-start.1
  8.2 1.1 %shard_map.87 = (bf16[8,64,128]{2,1,0:T(8,128)(2,1)S(1)}, f32[5,8,128]{2,1,0:T(8,128)S(1)}) custom-call(bf16[1,8,8,1024]{3,2,1,0:T(8,128)(2,1)} %ens_hbm.1, f32[8,8]{1,0:T(8,128)} %vertical_hbm.1, f32[8]{0:T(128)} %weights_hbm.1), custom_call_target="tpu_custom_call" | custom-call | flops 1000000 | bytes 1000000 | tf_op jit(solution)/shard_map/pallas_call | solution.py:392
  9.3 0.0 collective-permute-done.3.refs_3_
  9.3 2.3 %collective-permute-done.2.refs_2_ = f32[24,128]{1,0:T(8,128)S(1)} collective-permute-done((f32[24,128]{1,0:T(8,128)S(1)}, f32[24,128]{1,0:T(8,128)S(1)}, u32[]{:S(2)}, u32[]{:S(2)}) %collective-permute-start.2) | collective-permute-done | bytes 12320 | tf_op jit(solution)/shard_map/ppermute | solution.py:368
  11.6 0.0 collective-permute-done.1.refs_1_
  11.6 0.4 %shard_map.88 = (f32[8,1024]{1,0:T(8,128)S(1)}, f32[8,8,128]{2,1,0:T(8,128)S(1)}, bf16[8,128,128]{2,1,0:T(8,128)(2,1)S(1)}, f32[32,128]{1,0:T(8,128)S(1)}, f32[32,128]{1,0:T(8,128)S(1)}) custom-call(f32[24,128]{1,0:T(8,128)S(1)} %maximum_maximum_fusion.refs_0_, f32[24,128]{1,0:T(8,128)S(1)} %collective-permute-done.1.refs_1_, ...), custom_call_target="tpu_custom_call" | custom-call | tf_op jit(solution)/shard_map/pallas_call | solution.py:413
  12.0 0.4 %collective-permute-start.4 = (f32[32,128]{1,0:T(8,128)S(1)}, f32[32,128]{1,0:T(8,128)S(1)}, u32[]{:S(2)}, u32[]{:S(2)}) collective-permute-start(f32[32,128]{1,0:T(8,128)S(1)} %get-tuple-element.28), channel_id=1, source_target_pairs={{0,1},{1,0},{2,3},{3,2},{4,5},{5,4},{6,7},{7,6},{8,16},{9,17},{10,... | collective-permute-start | bytes 49160 | tf_op jit(solution)/shard_map/ppermute | solution.py:377
  12.5 2.6 %collective-permute-start.5 = (f32[32,128]{1,0:T(8,128)S(1)}, f32[32,128]{1,0:T(8,128)S(1)}, u32[]{:S(2)}, u32[]{:S(2)}) collective-permute-start(f32[32,128]{1,0:T(8,128)S(1)} %get-tuple-element.29), channel_id=1, source_target_pairs={{0,8},{1,9},{2,10},{3,11},{4,12},{5,13},{6,14},{7,15},{8,0},{9,1},... | collective-permute-start | bytes 49160 | tf_op jit(solution)/shard_map/ppermute | solution.py:377
  15.1 0.5 %shard_map.89 = (f32[64,1024]{1,0:T(8,128)S(1)}, f32[8,1024]{1,0:T(8,128)S(1)}, f32[64,1152]{1,0:T(8,128)S(1)}, f32[64,1152]{1,0:T(8,128)S(1)}, f32[64,1152]{1,0:T(8,128)S(1)}, /*index=5*/f32[64,1152]{1,0:T(8,128)S(1)}) custom-call(f32[8,8,128]{2,1,0:T(8,128)S(1)} %get-tuple-element.26.slots_ref, bf16[8,128,128]{2,1,0:T(8,128)(2,1)S(1)} %get-tuple-element.27.hits_ref, ...), custom_call_target="tpu_custom_call" | custom-call | flops 1000000 | bytes 1000000 | tf_op jit(solution)/shard_map/pallas_call | solution.py:427
  15.6 0.0 collective-permute-done.4.b_ref
  15.6 1.3 %collective-permute-done.5.a_ref = f32[32,128]{1,0:T(8,128)S(1)} collective-permute-done((f32[32,128]{1,0:T(8,128)S(1)}, f32[32,128]{1,0:T(8,128)S(1)}, u32[]{:S(2)}, u32[]{:S(2)}) %collective-permute-start.5) | collective-permute-done | bytes 16416 | tf_op jit(solution)/shard_map/ppermute | solution.py:377
  17.0 1.1 %shard_map.90 = (f32[4,72,128]{2,1,0:T(8,128)S(1)}, f32[4,72,128]{2,1,0:T(8,128)S(1)}) custom-call(f32[8,1024]{1,0:T(8,128)S(1)} %get-tuple-element.25.d_ref, f32[8,8,128]{2,1,0:T(8,128)S(1)} %get-tuple-element.26.slots_ref, bf16[8,128,128]{2,1,0:T(8,128)(2,1)S(1)} %get-tuple-element.27.hits_ref, f32[32,128]{1,0:T(8,128)S(1)} %collective-permute-done.4.b_ref, ...), custom_call_target="tpu_custom_call" | custom-call | tf_op jit(solution)/shard_map/pallas_call | solution.py:437
  18.0 0.1 collective-permute-start.6
  18.1 1.4 %collective-permute-done.6.got_ref = f32[4,72,128]{2,1,0:T(8,128)S(1)} collective-permute-done((f32[4,72,128]{2,1,0:T(8,128)S(1)}, f32[4,72,128]{2,1,0:T(8,128)S(1)}, u32[]{:S(2)}, u32[]{:S(2)}) %collective-permute-start.6) | collective-permute-done | bytes 147488 | tf_op jit(solution)/shard_map/ppermute | solution.py:368
  19.5 0.1 shard_map.91
  19.6 1.8 %collective-permute-start.7 = (s16[80,128]{1,0:T(8,128)(2,1)S(1)}, s16[80,128]{1,0:T(8,128)(2,1)S(1)}, u32[]{:S(2)}, u32[]{:S(2)}) collective-permute-start(s16[80,128]{1,0:T(8,128)(2,1)S(1)} %get-tuple-element.40), channel_id=1, source_target_pairs={{0,7},{1,6},{2,5},{3,4},{4,3},{5,2},{6,1},{7,0},{8,15},{9,14},{10,... | collective-permute-start | bytes 61448 | tf_op jit(solution)/shard_map/ppermute | solution.py:368
  21.4 0.0 collective-permute-start.8
  21.4 2.1 %collective-permute-start.9 = (s16[80,128]{1,0:T(8,128)(2,1)S(1)}, s16[80,128]{1,0:T(8,128)(2,1)S(1)}, u32[]{:S(2)}, u32[]{:S(2)}) collective-permute-start(s16[80,128]{1,0:T(8,128)(2,1)S(1)} %get-tuple-element.42), channel_id=1, source_target_pairs={{0,3},{1,2},{2,1},{3,0},{4,7},{5,6},{6,5},{7,4},{8,11},{9,10},{10,... | collective-permute-start | bytes 61448 | tf_op jit(solution)/shard_map/ppermute | solution.py:368
  23.5 1.1 %collective-permute-done.7.refs_1_ = s16[80,128]{1,0:T(8,128)(2,1)S(1)} collective-permute-done((s16[80,128]{1,0:T(8,128)(2,1)S(1)}, s16[80,128]{1,0:T(8,128)(2,1)S(1)}, u32[]{:S(2)}, u32[]{:S(2)}) %collective-permute-start.7) | collective-permute-done | bytes 20512 | tf_op jit(solution)/shard_map/ppermute | solution.py:368
  24.6 0.9 %collective-permute-done.8.refs_2_ = s16[80,128]{1,0:T(8,128)(2,1)S(1)} collective-permute-done((s16[80,128]{1,0:T(8,128)(2,1)S(1)}, s16[80,128]{1,0:T(8,128)(2,1)S(1)}, u32[]{:S(2)}, u32[]{:S(2)}) %collective-permute-start.8) | collective-permute-done | bytes 20512 | tf_op jit(solution)/shard_map/ppermute | solution.py:368
  25.5 0.0 collective-permute-done.9.refs_3_
  25.5 0.7 %shard_map.92 = (f32[8,8,128]{2,1,0:T(8,128)}, f32[1,8,8]{2,1,0:T(8,128)}) custom-call(f32[72,128]{1,0:T(8,128)S(1)} %get-tuple-element.39.refs_0_, s16[80,128]{1,0:T(8,128)(2,1)S(1)} %collective-permute-done.7.refs_1_, s16[80,128]{1,0:T(8,128)(2,1)S(1)} %collective-permute-done.8.refs_2_, s16[80,128]{1,0:T(8,128)(2,1)S(1)} %collective-permute-done.9.refs_3_, ...), custom_call_target="tpu_custom_call" | custom-call | tf_op jit(solution)/shard_map/pallas_call | solution.py:456
  (1 shorter events, 0.0 us)
Async XLA Ops:
  1.6 1.3 %collective-permute-start = (f32[16,128]{1,0:T(8,128)S(1)}, f32[16,128]{1,0:T(8,128)S(1)}, u32[]{:S(2)}, u32[]{:S(2)}) collective-permute-start(f32[16,128]{1,0:T(8,128)S(1)} %get-tuple-element.23), channel_id=1, source_target_pairs={{0,1},{1,0},{2,3},{3,2},{4,5},{5,4},{6,7},{7,6},{8,9},{9,8},{10,11... | collective-permute-start | bytes 24584 | tf_op jit(solution)/shard_map/ppermute | solution.py:368
  3.0 6.3 %collective-permute-start.3 = (f32[24,128]{1,0:T(8,128)S(1)}, f32[24,128]{1,0:T(8,128)S(1)}, u32[]{:S(2)}, u32[]{:S(2)}) collective-permute-start(f32[24,128]{1,0:T(8,128)S(1)} %maximum_maximum_fusion.refs_0_), channel_id=1, source_target_pairs={{0,5},{1,4},{2,7},{3,6},{4,1},{5,0},{6,3},{7,2},{8,13},{9,12},{10,... | collective-permute-start | bytes 36872 | tf_op jit(solution)/shard_map/ppermute | solution.py:368
  6.7 4.9 %collective-permute-start.2 = (f32[24,128]{1,0:T(8,128)S(1)}, f32[24,128]{1,0:T(8,128)S(1)}, u32[]{:S(2)}, u32[]{:S(2)}) collective-permute-start(f32[24,128]{1,0:T(8,128)S(1)} %maximum_maximum_fusion.refs_0_), channel_id=1, source_target_pairs={{0,7},{1,6},{2,5},{3,4},{4,3},{5,2},{6,1},{7,0},{8,15},{9,14},{10,... | collective-permute-start | bytes 36872 | tf_op jit(solution)/shard_map/ppermute | solution.py:368
  8.0 3.6 %collective-permute-start.1 = (f32[24,128]{1,0:T(8,128)S(1)}, f32[24,128]{1,0:T(8,128)S(1)}, u32[]{:S(2)}, u32[]{:S(2)}) collective-permute-start(f32[24,128]{1,0:T(8,128)S(1)} %maximum_maximum_fusion.refs_0_), channel_id=1, source_target_pairs={{0,3},{1,2},{2,1},{3,0},{4,7},{5,6},{6,5},{7,4},{8,11},{9,10},{10,... | collective-permute-start | bytes 36872 | tf_op jit(solution)/shard_map/ppermute | solution.py:368
  12.0 3.6 %collective-permute-start.4 = (f32[32,128]{1,0:T(8,128)S(1)}, f32[32,128]{1,0:T(8,128)S(1)}, u32[]{:S(2)}, u32[]{:S(2)}) collective-permute-start(f32[32,128]{1,0:T(8,128)S(1)} %get-tuple-element.28), channel_id=1, source_target_pairs={{0,1},{1,0},{2,3},{3,2},{4,5},{5,4},{6,7},{7,6},{8,16},{9,17},{10,... | collective-permute-start | bytes 49160 | tf_op jit(solution)/shard_map/ppermute | solution.py:377
  12.5 4.5 %collective-permute-start.5 = (f32[32,128]{1,0:T(8,128)S(1)}, f32[32,128]{1,0:T(8,128)S(1)}, u32[]{:S(2)}, u32[]{:S(2)}) collective-permute-start(f32[32,128]{1,0:T(8,128)S(1)} %get-tuple-element.29), channel_id=1, source_target_pairs={{0,8},{1,9},{2,10},{3,11},{4,12},{5,13},{6,14},{7,15},{8,0},{9,1},... | collective-permute-start | bytes 49160 | tf_op jit(solution)/shard_map/ppermute | solution.py:377
  18.0 1.4 %collective-permute-start.6 = (f32[4,72,128]{2,1,0:T(8,128)S(1)}, f32[4,72,128]{2,1,0:T(8,128)S(1)}, u32[]{:S(2)}, u32[]{:S(2)}) collective-permute-start(f32[4,72,128]{2,1,0:T(8,128)S(1)} %get-tuple-element.38), channel_id=1, source_target_pairs={{0,1},{1,0},{2,3},{3,2},{4,5},{5,4},{6,7},{7,6},{8,9},{9,8},{10,11... | collective-permute-start | bytes 442376 | tf_op jit(solution)/shard_map/ppermute | solution.py:368
  19.6 5.1 %collective-permute-start.7 = (s16[80,128]{1,0:T(8,128)(2,1)S(1)}, s16[80,128]{1,0:T(8,128)(2,1)S(1)}, u32[]{:S(2)}, u32[]{:S(2)}) collective-permute-start(s16[80,128]{1,0:T(8,128)(2,1)S(1)} %get-tuple-element.40), channel_id=1, source_target_pairs={{0,7},{1,6},{2,5},{3,4},{4,3},{5,2},{6,1},{7,0},{8,15},{9,14},{10,... | collective-permute-start | bytes 61448 | tf_op jit(solution)/shard_map/ppermute | solution.py:368
  21.4 4.2 %collective-permute-start.8 = (s16[80,128]{1,0:T(8,128)(2,1)S(1)}, s16[80,128]{1,0:T(8,128)(2,1)S(1)}, u32[]{:S(2)}, u32[]{:S(2)}) collective-permute-start(s16[80,128]{1,0:T(8,128)(2,1)S(1)} %get-tuple-element.41), channel_id=1, source_target_pairs={{0,5},{1,4},{2,7},{3,6},{4,1},{5,0},{6,3},{7,2},{8,13},{9,12},{10,... | collective-permute-start | bytes 61448 | tf_op jit(solution)/shard_map/ppermute | solution.py:368
  21.4 4.2 %collective-permute-start.9 = (s16[80,128]{1,0:T(8,128)(2,1)S(1)}, s16[80,128]{1,0:T(8,128)(2,1)S(1)}, u32[]{:S(2)}, u32[]{:S(2)}) collective-permute-start(s16[80,128]{1,0:T(8,128)(2,1)S(1)} %get-tuple-element.42), channel_id=1, source_target_pairs={{0,3},{1,2},{2,1},{3,0},{4,7},{5,6},{6,5},{7,4},{8,11},{9,10},{10,... | collective-permute-start | bytes 61448 | tf_op jit(solution)/shard_map/ppermute | solution.py:368

commit v10 on v9

--- a/solution.py
+++ b/solution.py
@@ -282,9 +282,9 @@
             parts.append(mixed * member[row, at])
             made[t, row, :] = parts[-1]
         before, here = here, after
-        stacked = jnp.concatenate(pieces(jnp.concatenate(parts, axis=0)), axis=0).astype(BF16)
+        stacked = jnp.concatenate(pieces(jnp.concatenate(parts, axis=0))[:2], axis=0).astype(BF16)
         found = jnp.dot(stacked, hits_ref[t], preferred_element_type=F32)
-        found = found[0:own] + found[own : 2 * own] + found[2 * own :]
+        found = found[0:own] + found[own:]
         on = iota(found.shape, 0).astype(F32) == slots_ref[t, 1:2, :]
         line = jnp.sum(jnp.where(on, found, 0.0), axis=0, keepdims=True)
         for q in range(tiles // block):

time: 26.5 us -> 26.5 us (level)
  no operation moved by 1% of the time
where the time goes in v10:
time: 26.5 us; the launch traced here: 26.2 us
  starting transfers between devices  12.8 us (48%)
  waiting for transfers between devices  7.77 us (29%)
  Pallas kernels  4.78 us (18%)
  between operations  0.69 us (3%)
    ppermute x8, starting transfers between devices, swap(): return lax.ppermute(x, 'tx', [(i, i ^ far) for i in range(tiles)])  9.75 us
    ppermute x8, waiting for transfers between devices, swap(): return lax.ppermute(x, 'tx', [(i, i ^ far) for i in range(tiles)])  6.44 us
    ppermute x2, starting transfers between devices, swap_bands(): return lax.ppermute(x, ('ty', 'tx'), pairs)  3.06 us
    ppermute x2, waiting for transfers between devices, swap_bands(): return lax.ppermute(x, ('ty', 'tx'), pairs)  1.33 us
    pallas_call x1, Pallas kernels, shards(): call(member_kernel, (shape((tiles, own, LANES), BF16), shape((2 * BAND +...  1.08 us
    pallas_call x1, Pallas kernels, shards(): call(functools.partial(main_kernel, rows, levels), (shape((chips, chunk,...  1.06 us
    pallas_call x1, Pallas kernels, shards(): call(packet_kernel, (shape((height, LANES), F32), shape((tiles, LANES), F...  0.93 us
    pallas_call x1, Pallas kernels, shards(): call(functools.partial(final_kernel, own), (shape((levels, rows, LANES),...  0.69 us
  transfers between devices with their start and end apart: 10, of which 6 were waited for; matrix products, arithmetic and copies ran while one was open for 0% of the time, Pallas kernels for 6%

profile of v10, /device:TPU:0, one launch (start us, length us, event | category | flops | bytes accessed | tf_op | source)
XLA Modules:
  0.0 26.2 jit_solution(197538867974552119)
XLA Ops:
  0.6 0.9 %shard_map.86 = (f32[16,128]{1,0:T(8,128)S(1)}, f32[8,128]{1,0:T(8,128)S(1)}) custom-call(f32[1,8,8]{2,1,0:T(8,128)} %value_hbm.1, s32[1,8,8]{2,1,0:T(8,128)} %cell_hbm.1, s32[1,8]{1,0:T(1,128)} %count_hbm.1, f32[8,128]{1,0:T(8,128)} %diff_hbm.1), custom_call_target="tpu_custom_call" | custom-call | tf_op jit(solution)/shard_map/pallas_call | solution.py:379
  1.6 0.5 %collective-permute-start = (f32[16,128]{1,0:T(8,128)S(1)}, f32[16,128]{1,0:T(8,128)S(1)}, u32[]{:S(2)}, u32[]{:S(2)}) collective-permute-start(f32[16,128]{1,0:T(8,128)S(1)} %get-tuple-element.23), channel_id=1, source_target_pairs={{0,1},{1,0},{2,3},{3,2},{4,5},{5,4},{6,7},{7,6},{8,9},{9,8},{10,11... | collective-permute-start | bytes 24584 | tf_op jit(solution)/shard_map/ppermute | solution.py:368
  2.1 0.1 pad.2.clone
  2.2 0.7 %collective-permute-done = f32[16,128]{1,0:T(8,128)S(1)} collective-permute-done((f32[16,128]{1,0:T(8,128)S(1)}, f32[16,128]{1,0:T(8,128)S(1)}, u32[]{:S(2)}, u32[]{:S(2)}) %collective-permute-start) | collective-permute-done | bytes 8224 | tf_op jit(solution)/shard_map/ppermute | solution.py:368
  2.9 0.1 maximum_maximum_fusion.refs_0_
  3.0 3.7 %collective-permute-start.3 = (f32[24,128]{1,0:T(8,128)S(1)}, f32[24,128]{1,0:T(8,128)S(1)}, u32[]{:S(2)}, u32[]{:S(2)}) collective-permute-start(f32[24,128]{1,0:T(8,128)S(1)} %maximum_maximum_fusion.refs_0_), channel_id=1, source_target_pairs={{0,5},{1,4},{2,7},{3,6},{4,1},{5,0},{6,3},{7,2},{8,13},{9,12},{10,... | collective-permute-start | bytes 36872 | tf_op jit(solution)/shard_map/ppermute | solution.py:368
  6.7 1.3 %collective-permute-start.2 = (f32[24,128]{1,0:T(8,128)S(1)}, f32[24,128]{1,0:T(8,128)S(1)}, u32[]{:S(2)}, u32[]{:S(2)}) collective-permute-start(f32[24,128]{1,0:T(8,128)S(1)} %maximum_maximum_fusion.refs_0_), channel_id=1, source_target_pairs={{0,7},{1,6},{2,5},{3,4},{4,3},{5,2},{6,1},{7,0},{8,15},{9,14},{10,... | collective-permute-start | bytes 36872 | tf_op jit(solution)/shard_map/ppermute | solution.py:368
  8.0 0.2 collective-permute-start.1
  8.2 1.1 %shard_map.87 = (bf16[8,64,128]{2,1,0:T(8,128)(2,1)S(1)}, f32[5,8,128]{2,1,0:T(8,128)S(1)}) custom-call(bf16[1,8,8,1024]{3,2,1,0:T(8,128)(2,1)} %ens_hbm.1, f32[8,8]{1,0:T(8,128)} %vertical_hbm.1, f32[8]{0:T(128)} %weights_hbm.1), custom_call_target="tpu_custom_call" | custom-call | flops 1000000 | bytes 1000000 | tf_op jit(solution)/shard_map/pallas_call | solution.py:392
  9.3 0.0 collective-permute-done.3.refs_3_
  9.3 2.3 %collective-permute-done.2.refs_2_ = f32[24,128]{1,0:T(8,128)S(1)} collective-permute-done((f32[24,128]{1,0:T(8,128)S(1)}, f32[24,128]{1,0:T(8,128)S(1)}, u32[]{:S(2)}, u32[]{:S(2)}) %collective-permute-start.2) | collective-permute-done | bytes 12320 | tf_op jit(solution)/shard_map/ppermute | solution.py:368
  11.6 0.0 collective-permute-done.1.refs_1_
  11.6 0.4 %shard_map.88 = (f32[8,1024]{1,0:T(8,128)S(1)}, f32[8,8,128]{2,1,0:T(8,128)S(1)}, bf16[8,128,128]{2,1,0:T(8,128)(2,1)S(1)}, f32[32,128]{1,0:T(8,128)S(1)}, f32[32,128]{1,0:T(8,128)S(1)}) custom-call(f32[24,128]{1,0:T(8,128)S(1)} %maximum_maximum_fusion.refs_0_, f32[24,128]{1,0:T(8,128)S(1)} %collective-permute-done.1.refs_1_, ...), custom_call_target="tpu_custom_call" | custom-call | tf_op jit(solution)/shard_map/pallas_call | solution.py:413
  12.0 0.4 %collective-permute-start.4 = (f32[32,128]{1,0:T(8,128)S(1)}, f32[32,128]{1,0:T(8,128)S(1)}, u32[]{:S(2)}, u32[]{:S(2)}) collective-permute-start(f32[32,128]{1,0:T(8,128)S(1)} %get-tuple-element.28), channel_id=1, source_target_pairs={{0,1},{1,0},{2,3},{3,2},{4,5},{5,4},{6,7},{7,6},{8,16},{9,17},{10,... | collective-permute-start | bytes 49160 | tf_op jit(solution)/shard_map/ppermute | solution.py:377
  12.5 2.6 %collective-permute-start.5 = (f32[32,128]{1,0:T(8,128)S(1)}, f32[32,128]{1,0:T(8,128)S(1)}, u32[]{:S(2)}, u32[]{:S(2)}) collective-permute-start(f32[32,128]{1,0:T(8,128)S(1)} %get-tuple-element.29), channel_id=1, source_target_pairs={{0,8},{1,9},{2,10},{3,11},{4,12},{5,13},{6,14},{7,15},{8,0},{9,1},... | collective-permute-start | bytes 49160 | tf_op jit(solution)/shard_map/ppermute | solution.py:377
  15.1 0.5 %shard_map.89 = (f32[64,1024]{1,0:T(8,128)S(1)}, f32[8,1024]{1,0:T(8,128)S(1)}, f32[64,1152]{1,0:T(8,128)S(1)}, f32[64,1152]{1,0:T(8,128)S(1)}, f32[64,1152]{1,0:T(8,128)S(1)}, /*index=5*/f32[64,1152]{1,0:T(8,128)S(1)}) custom-call(f32[8,8,128]{2,1,0:T(8,128)S(1)} %get-tuple-element.26.slots_ref, bf16[8,128,128]{2,1,0:T(8,128)(2,1)S(1)} %get-tuple-element.27.hits_ref, ...), custom_call_target="tpu_custom_call" | custom-call | flops 1000000 | bytes 1000000 | tf_op jit(solution)/shard_map/pallas_call | solution.py:427
  15.6 0.0 collective-permute-done.4.b_ref
  15.6 1.3 %collective-permute-done.5.a_ref = f32[32,128]{1,0:T(8,128)S(1)} collective-permute-done((f32[32,128]{1,0:T(8,128)S(1)}, f32[32,128]{1,0:T(8,128)S(1)}, u32[]{:S(2)}, u32[]{:S(2)}) %collective-permute-start.5) | collective-permute-done | bytes 16416 | tf_op jit(solution)/shard_map/ppermute | solution.py:377
  17.0 1.1 %shard_map.90 = (f32[4,72,128]{2,1,0:T(8,128)S(1)}, f32[4,72,128]{2,1,0:T(8,128)S(1)}) custom-call(f32[8,1024]{1,0:T(8,128)S(1)} %get-tuple-element.25.d_ref, f32[8,8,128]{2,1,0:T(8,128)S(1)} %get-tuple-element.26.slots_ref, bf16[8,128,128]{2,1,0:T(8,128)(2,1)S(1)} %get-tuple-element.27.hits_ref, f32[32,128]{1,0:T(8,128)S(1)} %collective-permute-done.4.b_ref, ...), custom_call_target="tpu_custom_call" | custom-call | tf_op jit(solution)/shard_map/pallas_call | solution.py:437
  18.0 0.1 collective-permute-start.6
  18.1 1.4 %collective-permute-done.6.got_ref = f32[4,72,128]{2,1,0:T(8,128)S(1)} collective-permute-done((f32[4,72,128]{2,1,0:T(8,128)S(1)}, f32[4,72,128]{2,1,0:T(8,128)S(1)}, u32[]{:S(2)}, u32[]{:S(2)}) %collective-permute-start.6) | collective-permute-done | bytes 147488 | tf_op jit(solution)/shard_map/ppermute | solution.py:368
  19.5 0.1 shard_map.91
  19.5 1.8 %collective-permute-start.7 = (s16[80,128]{1,0:T(8,128)(2,1)S(1)}, s16[80,128]{1,0:T(8,128)(2,1)S(1)}, u32[]{:S(2)}, u32[]{:S(2)}) collective-permute-start(s16[80,128]{1,0:T(8,128)(2,1)S(1)} %get-tuple-element.40), channel_id=1, source_target_pairs={{0,7},{1,6},{2,5},{3,4},{4,3},{5,2},{6,1},{7,0},{8,15},{9,14},{10,... | collective-permute-start | bytes 61448 | tf_op jit(solution)/shard_map/ppermute | solution.py:368
  21.4 0.0 collective-permute-start.8
  21.4 2.1 %collective-permute-start.9 = (s16[80,128]{1,0:T(8,128)(2,1)S(1)}, s16[80,128]{1,0:T(8,128)(2,1)S(1)}, u32[]{:S(2)}, u32[]{:S(2)}) collective-permute-start(s16[80,128]{1,0:T(8,128)(2,1)S(1)} %get-tuple-element.42), channel_id=1, source_target_pairs={{0,3},{1,2},{2,1},{3,0},{4,7},{5,6},{6,5},{7,4},{8,11},{9,10},{10,... | collective-permute-start | bytes 61448 | tf_op jit(solution)/shard_map/ppermute | solution.py:368
  23.5 1.1 %collective-permute-done.7.refs_1_ = s16[80,128]{1,0:T(8,128)(2,1)S(1)} collective-permute-done((s16[80,128]{1,0:T(8,128)(2,1)S(1)}, s16[80,128]{1,0:T(8,128)(2,1)S(1)}, u32[]{:S(2)}, u32[]{:S(2)}) %collective-permute-start.7) | collective-permute-done | bytes 20512 | tf_op jit(solution)/shard_map/ppermute | solution.py:368
  24.6 0.9 %collective-permute-done.8.refs_2_ = s16[80,128]{1,0:T(8,128)(2,1)S(1)} collective-permute-done((s16[80,128]{1,0:T(8,128)(2,1)S(1)}, s16[80,128]{1,0:T(8,128)(2,1)S(1)}, u32[]{:S(2)}, u32[]{:S(2)}) %collective-permute-start.8) | collective-permute-done | bytes 20512 | tf_op jit(solution)/shard_map/ppermute | solution.py:368
  25.5 0.0 collective-permute-done.9.refs_3_
  25.5 0.7 %shard_map.92 = (f32[8,8,128]{2,1,0:T(8,128)}, f32[1,8,8]{2,1,0:T(8,128)}) custom-call(f32[72,128]{1,0:T(8,128)S(1)} %get-tuple-element.39.refs_0_, s16[80,128]{1,0:T(8,128)(2,1)S(1)} %collective-permute-done.7.refs_1_, s16[80,128]{1,0:T(8,128)(2,1)S(1)} %collective-permute-done.8.refs_2_, s16[80,128]{1,0:T(8,128)(2,1)S(1)} %collective-permute-done.9.refs_3_, ...), custom_call_target="tpu_custom_call" | custom-call | tf_op jit(solution)/shard_map/pallas_call | solution.py:456
  (1 shorter events, 0.0 us)
Async XLA Ops:
  1.6 1.3 %collective-permute-start = (f32[16,128]{1,0:T(8,128)S(1)}, f32[16,128]{1,0:T(8,128)S(1)}, u32[]{:S(2)}, u32[]{:S(2)}) collective-permute-start(f32[16,128]{1,0:T(8,128)S(1)} %get-tuple-element.23), channel_id=1, source_target_pairs={{0,1},{1,0},{2,3},{3,2},{4,5},{5,4},{6,7},{7,6},{8,9},{9,8},{10,11... | collective-permute-start | bytes 24584 | tf_op jit(solution)/shard_map/ppermute | solution.py:368
  3.0 6.3 %collective-permute-start.3 = (f32[24,128]{1,0:T(8,128)S(1)}, f32[24,128]{1,0:T(8,128)S(1)}, u32[]{:S(2)}, u32[]{:S(2)}) collective-permute-start(f32[24,128]{1,0:T(8,128)S(1)} %maximum_maximum_fusion.refs_0_), channel_id=1, source_target_pairs={{0,5},{1,4},{2,7},{3,6},{4,1},{5,0},{6,3},{7,2},{8,13},{9,12},{10,... | collective-permute-start | bytes 36872 | tf_op jit(solution)/shard_map/ppermute | solution.py:368
  6.7 4.9 %collective-permute-start.2 = (f32[24,128]{1,0:T(8,128)S(1)}, f32[24,128]{1,0:T(8,128)S(1)}, u32[]{:S(2)}, u32[]{:S(2)}) collective-permute-start(f32[24,128]{1,0:T(8,128)S(1)} %maximum_maximum_fusion.refs_0_), channel_id=1, source_target_pairs={{0,7},{1,6},{2,5},{3,4},{4,3},{5,2},{6,1},{7,0},{8,15},{9,14},{10,... | collective-permute-start | bytes 36872 | tf_op jit(solution)/shard_map/ppermute | solution.py:368
  8.0 3.6 %collective-permute-start.1 = (f32[24,128]{1,0:T(8,128)S(1)}, f32[24,128]{1,0:T(8,128)S(1)}, u32[]{:S(2)}, u32[]{:S(2)}) collective-permute-start(f32[24,128]{1,0:T(8,128)S(1)} %maximum_maximum_fusion.refs_0_), channel_id=1, source_target_pairs={{0,3},{1,2},{2,1},{3,0},{4,7},{5,6},{6,5},{7,4},{8,11},{9,10},{10,... | collective-permute-start | bytes 36872 | tf_op jit(solution)/shard_map/ppermute | solution.py:368
  12.0 3.6 %collective-permute-start.4 = (f32[32,128]{1,0:T(8,128)S(1)}, f32[32,128]{1,0:T(8,128)S(1)}, u32[]{:S(2)}, u32[]{:S(2)}) collective-permute-start(f32[32,128]{1,0:T(8,128)S(1)} %get-tuple-element.28), channel_id=1, source_target_pairs={{0,1},{1,0},{2,3},{3,2},{4,5},{5,4},{6,7},{7,6},{8,16},{9,17},{10,... | collective-permute-start | bytes 49160 | tf_op jit(solution)/shard_map/ppermute | solution.py:377
  12.5 4.5 %collective-permute-start.5 = (f32[32,128]{1,0:T(8,128)S(1)}, f32[32,128]{1,0:T(8,128)S(1)}, u32[]{:S(2)}, u32[]{:S(2)}) collective-permute-start(f32[32,128]{1,0:T(8,128)S(1)} %get-tuple-element.29), channel_id=1, source_target_pairs={{0,8},{1,9},{2,10},{3,11},{4,12},{5,13},{6,14},{7,15},{8,0},{9,1},... | collective-permute-start | bytes 49160 | tf_op jit(solution)/shard_map/ppermute | solution.py:377
  18.0 1.4 %collective-permute-start.6 = (f32[4,72,128]{2,1,0:T(8,128)S(1)}, f32[4,72,128]{2,1,0:T(8,128)S(1)}, u32[]{:S(2)}, u32[]{:S(2)}) collective-permute-start(f32[4,72,128]{2,1,0:T(8,128)S(1)} %get-tuple-element.38), channel_id=1, source_target_pairs={{0,1},{1,0},{2,3},{3,2},{4,5},{5,4},{6,7},{7,6},{8,9},{9,8},{10,11... | collective-permute-start | bytes 442376 | tf_op jit(solution)/shard_map/ppermute | solution.py:368
  19.5 5.1 %collective-permute-start.7 = (s16[80,128]{1,0:T(8,128)(2,1)S(1)}, s16[80,128]{1,0:T(8,128)(2,1)S(1)}, u32[]{:S(2)}, u32[]{:S(2)}) collective-permute-start(s16[80,128]{1,0:T(8,128)(2,1)S(1)} %get-tuple-element.40), channel_id=1, source_target_pairs={{0,7},{1,6},{2,5},{3,4},{4,3},{5,2},{6,1},{7,0},{8,15},{9,14},{10,... | collective-permute-start | bytes 61448 | tf_op jit(solution)/shard_map/ppermute | solution.py:368
  21.4 4.2 %collective-permute-start.8 = (s16[80,128]{1,0:T(8,128)(2,1)S(1)}, s16[80,128]{1,0:T(8,128)(2,1)S(1)}, u32[]{:S(2)}, u32[]{:S(2)}) collective-permute-start(s16[80,128]{1,0:T(8,128)(2,1)S(1)} %get-tuple-element.41), channel_id=1, source_target_pairs={{0,5},{1,4},{2,7},{3,6},{4,1},{5,0},{6,3},{7,2},{8,13},{9,12},{10,... | collective-permute-start | bytes 61448 | tf_op jit(solution)/shard_map/ppermute | solution.py:368
  21.4 4.2 %collective-permute-start.9 = (s16[80,128]{1,0:T(8,128)(2,1)S(1)}, s16[80,128]{1,0:T(8,128)(2,1)S(1)}, u32[]{:S(2)}, u32[]{:S(2)}) collective-permute-start(s16[80,128]{1,0:T(8,128)(2,1)S(1)} %get-tuple-element.42), channel_id=1, source_target_pairs={{0,3},{1,2},{2,1},{3,0},{4,7},{5,6},{6,5},{7,4},{8,11},{9,10},{10,... | collective-permute-start | bytes 61448 | tf_op jit(solution)/shard_map/ppermute | solution.py:368
